TPU v7x, 32 devices: a whole 2x2x4 slice. The times are simulated.
32 devices in a mesh: clip: 8 (over z, y), win: 4 (over x, core).
Axes of the slice: x: 2, y: 2, z: 4, core: 2. Of those that a mesh axis runs over, the one named last changes fastest.
Arguments:
- tokens: bfloat16 [8, 10, 2, 8, 16, 1024], P('clip', None, None, 'win'), may hold values from -6 to 6
- condition: float32 [8, 1024], P('clip'), may hold values from -6 to 6
- frame_count: int32 [8], P('clip'), may hold values from 2 to 9, as said below
- triple_weight: bfloat16 [1024, 3072], P('clip'), may hold values from -0.1875 to 0.1875
- triple_bias: bfloat16 [2048], P('clip'), may hold values from -3 to 3
- project_weight: bfloat16 [1024, 1024], P('clip'), may hold values from -0.75 to 0.75
- project_bias: bfloat16 [1024], P('clip'), may hold values from -3 to 3
- up_weight: bfloat16 [1024, 4096], P('clip'), may hold values from -0.1875 to 0.1875
- up_bias: bfloat16 [4096], P('clip'), may hold values from -3 to 3
- down_weight: bfloat16 [4096, 1024], P('clip'), may hold values from -0.09375 to 0.09375
- down_bias: bfloat16 [1024], P('clip'), may hold values from -3 to 3
- modulate_weight: bfloat16 [1024, 6144], P('clip'), may hold values from -0.1875 to 0.1875
- modulate_bias: bfloat16 [6144], P('clip'), may hold values from -3 to 3
- position_table: float32 [16, 2025], replicated, may hold values from -3 to 3
- cotangent: bfloat16 [8, 10, 2, 8, 16, 1024], P('clip', None, None, 'win'), may hold values from -6 to 6
Outputs:
- output: bfloat16 [8, 10, 2, 8, 16, 1024], P('clip', None, None, 'win')
- input_grad: bfloat16 [8, 10, 2, 8, 16, 1024], P('clip', None, None, 'win')
- condition_grad: float32 [8, 1024], P('clip')
- triple_weight_grad: float32 [1024, 3072], P('clip')
- triple_bias_grad: float32 [2048], P('clip')
- project_weight_grad: float32 [1024, 1024], P('clip')
- project_bias_grad: float32 [1024], P('clip')
- up_weight_grad: float32 [1024, 4096], P('clip')
- up_bias_grad: float32 [4096], P('clip')
- down_weight_grad: float32 [4096, 1024], P('clip')
- down_bias_grad: float32 [1024], P('clip')
- modulate_weight_grad: float32 [1024, 6144], P('clip')
- modulate_bias_grad: float32 [6144], P('clip')
- position_table_grad: float32 [16, 2025], replicated
Inputs may be any that keep to these rules, and one draw needn't show every extreme that they name: Frames of clip c from frame_count[c] on are padding; a clip with at most 5 given frames has only padding in its later windows.
All inputs are finite; a program needn't handle non-finite values.
Results may differ from a plain program's by a relative error of at most 0.018.
The roundings to bfloat16 on the way count: a program that leaves them out, or rounds other values in their place, can miss the bound.
Values may be sent and summed in bfloat16 or wider, within the bound.
No kernel may reach another device: no remote copies, remote signals or barrier semaphores. Data moves between devices by JAX's collectives and lax.ppermute only.
A program may use at most 320 MiB of HBM per device.

v0:
```python
import jax
import jax.numpy as jnp
from jax import lax
from jax.sharding import PartitionSpec as P

WIN_T = 5
WIN_S = 8


eps_norm = 1e-06
neg_fill = -30000.0


def layer_norm(values):
    center = values - jnp.mean(values, axis=-1, keepdims=True)
    inverse = lax.rsqrt(jnp.mean(center * center, axis=-1, keepdims=True) + eps_norm)
    return (center * inverse, inverse)


def norm_back(grad_norm, normed, inverse):
    mean_grad = jnp.mean(grad_norm, axis=-1, keepdims=True)
    mean_cross = jnp.mean(grad_norm * normed, axis=-1, keepdims=True)
    return inverse * (grad_norm - mean_grad - normed * mean_cross)


def offset_index():
    window_size = WIN_T * WIN_S * WIN_S
    place = jnp.arange(window_size)
    frame = place // (WIN_S * WIN_S)
    row = place // WIN_S % WIN_S
    column = place % WIN_S
    span = 2 * WIN_S - 1
    first = (
        (frame[:, None] - frame[None, :] + WIN_T - 1) * span
        + row[:, None]
        - row[None, :]
        + WIN_S
        - 1
    )
    return first * span + column[:, None] - column[None, :] + WIN_S - 1


def build_bias(table):
    return jnp.take(table, offset_index(), axis=1)


def window_rows(grid, groups):
    clips_here, frames, halves, rows, side, width = grid.shape
    periods = frames // WIN_T
    cells = grid.reshape(clips_here, periods, WIN_T, halves, rows, halves, WIN_S, width)
    cells = cells.transpose(0, 1, 3, 5, 2, 4, 6, 7)
    return cells.reshape(groups, -1, WIN_T, rows, WIN_S, width)


def window_back(pieces, shape):
    clips_here, frames, halves, rows, side, width = shape
    periods = frames // WIN_T
    cells = pieces.reshape(clips_here, periods, halves, halves, WIN_T, rows, WIN_S, width)
    return cells.transpose(0, 1, 4, 2, 5, 3, 6, 7).reshape(shape)


def body(
    tokens,
    condition,
    frame_count,
    triple_weight,
    triple_bias,
    project_weight,
    project_bias,
    up_weight,
    up_bias,
    down_weight,
    down_bias,
    modulate_weight,
    modulate_bias,
    position_table,
    cotangent,
):
    width = tokens.shape[-1]
    heads = position_table.shape[0]
    head_dim = width // heads
    groups = lax.axis_size("win")
    clips_here = tokens.shape[0]
    halves = tokens.shape[2]
    per_time = tokens.shape[1] // WIN_T
    per_clip = per_time * halves * halves
    per_dev = clips_here * per_clip // groups
    window_size = WIN_T * WIN_S * WIN_S
    scale = head_dim ** (-0.5)
    floats = jnp.float32
    halfs = jnp.bfloat16
    sigma = jax.nn.sigmoid(condition)
    cond_in = (condition * sigma).astype(halfs)
    (
        triple_full,
        project_full,
        up_full,
        down_full,
        triple_bias_full,
        project_bias_full,
        up_bias_full,
        down_bias_full,
        modulate_full,
        modulate_bias_full,
    ) = (
        lax.all_gather(triple_weight, "clip", axis=0, tiled=True),
        lax.all_gather(project_weight, "clip", axis=0, tiled=True),
        lax.all_gather(up_weight, "clip", axis=0, tiled=True),
        lax.all_gather(down_weight, "clip", axis=0, tiled=True),
        lax.all_gather(triple_bias, "clip", axis=0, tiled=True),
        lax.all_gather(project_bias, "clip", axis=0, tiled=True),
        lax.all_gather(up_bias, "clip", axis=0, tiled=True),
        lax.all_gather(down_bias, "clip", axis=0, tiled=True),
        lax.all_gather(modulate_weight, "clip", axis=0, tiled=True),
        lax.all_gather(modulate_bias, "clip", axis=0, tiled=True),
    )
    modulation = jnp.dot(
        cond_in, modulate_full, preferred_element_type=floats
    ) + modulate_bias_full.astype(floats)
    send_tokens = window_rows(tokens, groups)
    send_grads = window_rows(cotangent, groups)
    got_tokens, got_grads = (
        lax.all_to_all(send_tokens, "win", split_axis=0, concat_axis=3, tiled=True),
        lax.all_to_all(send_grads, "win", split_axis=0, concat_axis=3, tiled=True),
    )
    values = got_tokens.reshape(per_dev, window_size, width).astype(floats)
    grad_out = got_grads.reshape(per_dev, window_size, width).astype(floats)
    window_id = lax.axis_index("win") * per_dev + jnp.arange(per_dev)
    clip_of = window_id // per_clip
    time_of = window_id // (halves * halves) % per_time
    pick = clip_of[:, None] == jnp.arange(clips_here)[None, :]
    count_here = jnp.sum(jnp.where(pick, frame_count[None, :], 0), axis=1)
    frame_of = time_of[:, None] * WIN_T + (jnp.arange(window_size) // (WIN_S * WIN_S))[None, :]
    keep = (frame_of < count_here[:, None]).astype(floats)
    mod_here = jnp.sum(jnp.where(pick[:, :, None], modulation[None], 0.0), axis=1).reshape(
        per_dev, 6, 1, width
    )
    shift_one, scale_one, gate_one = (mod_here[:, 0], mod_here[:, 1], mod_here[:, 2])
    shift_two, scale_two, gate_two = (mod_here[:, 3], mod_here[:, 4], mod_here[:, 5])
    keep_cols = keep[..., None]
    valid = keep[:, None, None, :] > 0
    bias, bias_back = jax.vjp(build_bias, position_table)
    normed_one, inverse_one = layer_norm(values)
    norm_in = (normed_one * (1.0 + scale_one) + shift_one).astype(halfs)
    bias_all = jnp.concatenate(
        [triple_bias_full[:width], jnp.zeros((width,), halfs), triple_bias_full[width:]]
    ).astype(floats)
    triple = (
        jnp.dot(norm_in.reshape(-1, width), triple_full, preferred_element_type=floats) + bias_all
    )
    triple = triple.astype(halfs).reshape(per_dev, window_size, 3, heads, head_dim)
    query, key, value = (triple[:, :, 0], triple[:, :, 1], triple[:, :, 2])

    def scores_of():
        raw = (
            jnp.einsum("wqhd,wkhd->whqk", query, key, preferred_element_type=floats) * scale
            + bias[None]
        )
        return jnp.where(valid, raw, neg_fill)

    score = scores_of()
    peak = jnp.max(score, axis=-1, keepdims=True)
    exponent = jnp.exp(score - peak)
    total = jnp.sum(exponent, axis=-1, keepdims=True)
    log_total = peak + jnp.log(total)
    prob = (exponent / total).astype(halfs)
    mixed = (
        jnp.einsum("whqk,wkhd->wqhd", prob, value, preferred_element_type=floats)
        .astype(halfs)
        .reshape(-1, width)
    )
    attention = (
        jnp.dot(mixed, project_full, preferred_element_type=floats)
        + project_bias_full.astype(floats)
    ).reshape(per_dev, window_size, width)
    middle = values + keep_cols * gate_one * attention
    normed_two, inverse_two = layer_norm(middle)
    norm_mid = (normed_two * (1.0 + scale_two) + shift_two).astype(halfs).reshape(-1, width)
    hidden = jnp.dot(norm_mid, up_full, preferred_element_type=floats) + up_bias_full.astype(floats)
    gelu_out, gelu_back = jax.vjp(lambda item: jax.nn.gelu(item, approximate=True), hidden)
    activated = gelu_out.astype(halfs)
    feedforward = (
        jnp.dot(activated, down_full, preferred_element_type=floats) + down_bias_full.astype(floats)
    ).reshape(per_dev, window_size, width)
    result = (middle + keep_cols * gate_two * feedforward).astype(halfs)
    output = lax.all_to_all(
        result.reshape(1, per_dev, WIN_T, WIN_S, WIN_S, width),
        "win",
        split_axis=3,
        concat_axis=0,
        tiled=True,
    )
    output = window_back(output, tokens.shape)
    gated_two = keep_cols * grad_out
    grad_ffn = (gated_two * gate_two).astype(halfs).reshape(-1, width)
    grad_gate_two = jnp.sum(gated_two * feedforward, axis=1)
    down_bias_grad = jnp.sum(grad_ffn.astype(floats), axis=0)
    down_weight_grad = jnp.einsum("nf,nd->fd", activated, grad_ffn, preferred_element_type=floats)
    grad_act = jnp.einsum("nd,fd->nf", grad_ffn, down_full, preferred_element_type=floats)
    grad_hidden = gelu_back(grad_act)[0].astype(halfs)
    up_bias_grad = jnp.sum(grad_hidden.astype(floats), axis=0)
    up_weight_grad = jnp.einsum("nd,nf->df", norm_mid, grad_hidden, preferred_element_type=floats)
    grad_norm_mid = jnp.einsum(
        "nf,df->nd", grad_hidden, up_full, preferred_element_type=floats
    ).reshape(per_dev, window_size, width)
    grad_shift_two = jnp.sum(grad_norm_mid, axis=1)
    grad_scale_two = jnp.sum(grad_norm_mid * normed_two, axis=1)
    grad_middle = grad_out + norm_back(grad_norm_mid * (1.0 + scale_two), normed_two, inverse_two)
    gated_one = keep_cols * grad_middle
    grad_attention = (gated_one * gate_one).astype(halfs).reshape(-1, width)
    grad_gate_one = jnp.sum(gated_one * attention, axis=1)
    project_bias_grad = jnp.sum(grad_attention.astype(floats), axis=0)
    project_weight_grad = jnp.einsum(
        "nd,ne->de", mixed, grad_attention, preferred_element_type=floats
    )
    grad_mixed = (
        jnp.einsum("ne,de->nd", grad_attention, project_full, preferred_element_type=floats)
        .astype(halfs)
        .reshape(per_dev, window_size, heads, head_dim)
    )
    prob_again = jnp.exp(scores_of() - log_total)
    grad_value = jnp.einsum(
        "whqk,wqhd->wkhd", prob_again.astype(halfs), grad_mixed, preferred_element_type=floats
    ).astype(halfs)
    grad_prob = jnp.einsum("wqhd,wkhd->whqk", grad_mixed, value, preferred_element_type=floats)
    grad_score = prob_again * (grad_prob - jnp.sum(grad_prob * prob_again, axis=-1, keepdims=True))
    grad_score = jnp.where(valid, grad_score, 0.0).astype(halfs)
    grad_bias = jnp.sum(grad_score.astype(floats), axis=0)
    grad_query = (
        jnp.einsum("whqk,wkhd->wqhd", grad_score, key, preferred_element_type=floats) * scale
    ).astype(halfs)
    grad_key = (
        jnp.einsum("whqk,wqhd->wkhd", grad_score, query, preferred_element_type=floats) * scale
    ).astype(halfs)
    grad_triple = jnp.stack([grad_query, grad_key, grad_value], axis=2).reshape(-1, 3 * width)
    triple_bias_grad = jnp.concatenate(
        [
            jnp.sum(grad_query.reshape(-1, width).astype(floats), axis=0),
            jnp.sum(grad_value.reshape(-1, width).astype(floats), axis=0),
        ]
    )
    triple_weight_grad = jnp.einsum(
        "nd,ne->de", norm_in.reshape(-1, width), grad_triple, preferred_element_type=floats
    )
    grad_norm_in = jnp.einsum(
        "ne,de->nd", grad_triple, triple_full, preferred_element_type=floats
    ).reshape(per_dev, window_size, width)
    grad_shift_one = jnp.sum(grad_norm_in, axis=1)
    grad_scale_one = jnp.sum(grad_norm_in * normed_one, axis=1)
    grad_input = grad_middle + norm_back(grad_norm_in * (1.0 + scale_one), normed_one, inverse_one)
    input_grad = lax.all_to_all(
        grad_input.astype(halfs).reshape(1, per_dev, WIN_T, WIN_S, WIN_S, width),
        "win",
        split_axis=3,
        concat_axis=0,
        tiled=True,
    )
    input_grad = window_back(input_grad, tokens.shape)
    grad_mod_here = jnp.concatenate(
        [
            grad_shift_one,
            grad_scale_one,
            grad_gate_one,
            grad_shift_two,
            grad_scale_two,
            grad_gate_two,
        ],
        axis=-1,
    )
    grad_mod_part = jnp.sum(jnp.where(pick.T[:, :, None], grad_mod_here[None], 0.0), axis=1)
    grad_modulation = lax.psum(grad_mod_part, "win").astype(halfs)
    silu_slope = sigma * (1.0 + condition * (1.0 - sigma))
    modulate_weight_full = jnp.einsum(
        "cd,ce->de", cond_in, grad_modulation, preferred_element_type=floats
    )
    modulate_bias_full_grad = jnp.sum(grad_modulation.astype(floats), axis=0)
    cond_back = jnp.einsum(
        "ce,de->cd", grad_modulation, modulate_full, preferred_element_type=floats
    )
    (
        triple_weight_grad,
        project_weight_grad,
        up_weight_grad,
        down_weight_grad,
        triple_bias_grad,
        project_bias_grad,
        up_bias_grad,
        down_bias_grad,
        modulate_weight_grad,
        modulate_bias_grad,
    ) = (
        lax.psum_scatter(
            triple_weight_grad.astype(jnp.bfloat16), "clip", scatter_dimension=0, tiled=True
        ).astype(jnp.float32),
        lax.psum_scatter(
            project_weight_grad.astype(jnp.bfloat16), "clip", scatter_dimension=0, tiled=True
        ).astype(jnp.float32),
        lax.psum_scatter(
            up_weight_grad.astype(jnp.bfloat16), "clip", scatter_dimension=0, tiled=True
        ).astype(jnp.float32),
        lax.psum_scatter(
            down_weight_grad.astype(jnp.bfloat16), "clip", scatter_dimension=0, tiled=True
        ).astype(jnp.float32),
        lax.psum_scatter(
            triple_bias_grad.astype(jnp.bfloat16), "clip", scatter_dimension=0, tiled=True
        ).astype(jnp.float32),
        lax.psum_scatter(
            project_bias_grad.astype(jnp.bfloat16), "clip", scatter_dimension=0, tiled=True
        ).astype(jnp.float32),
        lax.psum_scatter(
            up_bias_grad.astype(jnp.bfloat16), "clip", scatter_dimension=0, tiled=True
        ).astype(jnp.float32),
        lax.psum_scatter(
            down_bias_grad.astype(jnp.bfloat16), "clip", scatter_dimension=0, tiled=True
        ).astype(jnp.float32),
        lax.psum_scatter(
            modulate_weight_full.astype(jnp.bfloat16), "clip", scatter_dimension=0, tiled=True
        ).astype(jnp.float32),
        lax.psum_scatter(
            modulate_bias_full_grad.astype(jnp.bfloat16), "clip", scatter_dimension=0, tiled=True
        ).astype(jnp.float32),
    )
    condition_grad = cond_back * silu_slope
    (
        triple_weight_grad,
        project_weight_grad,
        up_weight_grad,
        down_weight_grad,
        triple_bias_grad,
        project_bias_grad,
        up_bias_grad,
        down_bias_grad,
    ) = (
        lax.psum(triple_weight_grad.astype(jnp.bfloat16), "win").astype(jnp.float32),
        lax.psum(project_weight_grad.astype(jnp.bfloat16), "win").astype(jnp.float32),
        lax.psum(up_weight_grad.astype(jnp.bfloat16), "win").astype(jnp.float32),
        lax.psum(down_weight_grad.astype(jnp.bfloat16), "win").astype(jnp.float32),
        lax.psum(triple_bias_grad.astype(jnp.bfloat16), "win").astype(jnp.float32),
        lax.psum(project_bias_grad.astype(jnp.bfloat16), "win").astype(jnp.float32),
        lax.psum(up_bias_grad.astype(jnp.bfloat16), "win").astype(jnp.float32),
        lax.psum(down_bias_grad.astype(jnp.bfloat16), "win").astype(jnp.float32),
    )
    table_grad = lax.psum(bias_back(grad_bias)[0], ("clip", "win"))
    return (
        output,
        input_grad,
        condition_grad,
        triple_weight_grad,
        triple_bias_grad,
        project_weight_grad,
        project_bias_grad,
        up_weight_grad,
        up_bias_grad,
        down_weight_grad,
        down_bias_grad,
        modulate_weight_grad,
        modulate_bias_grad,
        table_grad,
    )


def solution(mesh):
    placed = (
        P("clip", None, None, "win", None, None),
        P("clip", None),
        P("clip"),
        P("clip", None),
        P("clip"),
        P("clip", None),
        P("clip"),
        P("clip", None),
        P("clip"),
        P("clip", None),
        P("clip"),
        P("clip", None),
        P("clip"),
        P(),
        P("clip", None, None, "win", None, None),
    )
    return jax.shard_map(
        body,
        mesh=mesh,
        in_specs=placed,
        out_specs=(
            P("clip", None, None, "win", None, None),
            P("clip", None, None, "win", None, None),
            P("clip", None),
            P("clip", None),
            P("clip"),
            P("clip", None),
            P("clip"),
            P("clip", None),
            P("clip"),
            P("clip", None),
            P("clip"),
            P("clip", None),
            P("clip"),
            P(),
        ),
        check_vma=False,
    )
```

profile of v0, /device:TPU:1, one launch (start us, length us, event | category | flops | bytes accessed | tf_op | source)
XLA Modules:
  0.0 1842.3 jit_solution(929622427698485688)
XLA Ops:
  16.3 18.1 all-gather.1
  36.9 24.6 %all-gather = bf16[8,1,768]{2,1,0:T(2,128)(2,1)S(1)} all-gather(bf16[1,1,768]{2,1,0:T(2,128)(2,1)S(1)} %reshape.1191), channel_id=1, replica_groups=mesh['clip'=8,'win'=4] {'clip'}, dimensions={0}, use_global_device_ids=true | all-gather | bytes 13824 | tf_op jit(solution)/shard_map/all_gather | solution.py:115
  61.9 336.5 %gather_fusion = f32[102400,16]{1,0:T(8,128)} fusion(f32[16,2025]{0,1:T(8,128)S(1)} %copy.163, s32[102400]{0:T(1024)S(1)} %broadcast_clamp_fusion), kind=kCustom, calls=%fused_computation | custom fusion | bytes 13516800 | tf_op jit(solution)/shard_map/jvp(jit(_take))/gather | solution.py:44
  398.4 34.4 %copy.164 = f32[320,320,16]{0,1,2:T(8,128)} copy(f32[320,320,16]{2,1,0:T(8,128)} %bitcast.289) | data formatting | bytes 13107200 | tf_op jit(solution)/shard_map/jvp(jit(_take))/gather | solution.py:44
  432.8 13.0 all-gather.2
  446.9 22.3 %all-gather.3 = bf16[8,1,512]{2,1,0:T(2,128)(2,1)S(1)} all-gather(bf16[1,1,512]{2,1,0:T(2,128)(2,1)S(1)} %reshape.1197), channel_id=1, replica_groups=mesh['clip'=8,'win'=4] {'clip'}, dimensions={0}, use_global_device_ids=true | all-gather | bytes 9216 | tf_op jit(solution)/shard_map/all_gather | solution.py:112
  469.3 14.0 all-gather.4
  491.1 24.0 %all-to-all-start.2 = ((bf16[4,2,5,2,8,1024]{5,4,3,2,1,0:T(8,128)(2,1)}), bf16[4,2,5,2,8,1024]{5,4,3,2,1,0:T(8,128)(2,1)S(1)}, u32[]{:S(2)}, u32[]{:S(2)}) async-start(bf16[4,2,5,2,8,1024]{5,4,3,2,1,0:T(8,128)(2,1)} %bitcast.302), calls=%async_computation.2 | async-start | bytes 2621440 | tf_op jit(solution)/shard_map/all_to_all | solution.py:124
  519.7 12.0 all-to-all-done.2
  620.7 12.1 fusion.88
  632.8 18.4 fusion.82
  699.5 32.4 %convert_reduce_fusion = (f32[16,320,320]{1,2,0:T(8,128)}, bf16[2,16,320,320]{2,3,1,0:T(8,128)(2,1)}) fusion(f32[2,16,320,320]{2,3,1,0:T(8,128)} %fusion.47, f32[2,16,320,320]{2,3,1,0:T(8,128)} %get-tuple-element.146, f32[2,16,320]{2,1,0:T(8,128)S(1)} %log_add_fusion, pred[2,320]{1,0:T(4,128)(4,1)S(1)} %get-tuple-element.130), kind=kOutput, calls=%fused_computation.4 | output fusion | flops 27863360 | bytes 39363200 | tf_op jit(solution)/shard_map/sub | solution.py:226
  738.1 13.7 convolution_add_fusion
  783.2 14.0 multiply_reduce_fusion.2
  807.3 13.8 convolution_convert_fusion.1
  821.2 11.8 convolution_convert_fusion
  833.8 32.0 %copy.194 = f32[320,320,16]{2,1,0:T(8,128)} copy(f32[320,320,16]{0,1,2:T(8,128)} %bitcast.291) | data formatting | bytes 13107200 | tf_op jit(solution)/shard_map/reduce_sum | solution.py:228
  865.8 543.3 %scatter_custom_fusion = f32[16,2025]{0,1:T(8,128)} fusion(s32[102400]{0:T(1024)} %copy-done.20, f32[102400,16]{1,0:T(8,128)} %bitcast.290, f32[]{:T(128)} %constant.182.clone.1), kind=kCustom, calls=%fused_computation.106 | custom fusion | flops 1638400 | bytes 130112 | tf_op jit(solution)/shard_map/transpose(jvp(jit(_take)))/scatter-add | solution.py:44
  1409.2 12.8 psum.70
  1459.3 27.5 %all-reduce.5 = (bf16[2048]{0:T(1024)(128)(2,1)S(1)}, bf16[1024]{0:T(1024)(128)(2,1)S(1)}, bf16[4096]{0:T(1024)(128)(2,1)S(1)}, bf16[1024]{0:T(1024)(128)(2,1)S(1)}, bf16[6144]{0:T(1024)(128)(2,1)S(1)}) all-reduce(bf16[2048]{0:T(1024)(128)(2,1)S(1)} %pad_maximum_fusion.1, ...), channel_id=3, replica_groups=mesh['clip'=8,'win'=4] {'clip'}, use_global_device_ids=true, to_apply=%region_23.24.clone | all-reduce | flops 14336 | bytes 57344
  1487.1 12.6 all-reduce.6
  1511.1 37.8 %all-reduce.11.cloned.1.call-done = f32[16,2025]{0,1:T(8,128)} async-done(((f32[16,2025]{0,1:T(8,128)}), f32[16,2025]{0,1:T(8,128)}) %all-reduce.11.cloned.1.call-update) | async-done | bytes 129616 | tf_op jit(solution)/shard_map/psum | solution.py:343
  1555.4 65.1 %all-reduce.13.cloned.1.call-done = (bf16[128,3072]{1,0:T(8,128)(2,1)}, bf16[128,1024]{1,0:T(8,128)(2,1)}, bf16[128,4096]{1,0:T(8,128)(2,1)}, bf16[512,1024]{1,0:T(8,128)(2,1)}) async-done(((bf16[128,3072]{1,0:T(8,128)(2,1)}, bf16[128,1024]{1,0:T(8,128)(2,1)}, bf16[128,4096]{1,0:T(8,128)(2,1)}, bf16[512,1024]{1,0:T(8,128)(2,1)}), (bf16[128,3072]{1,0:T(8,128)(2,1)}, bf16[128,1024]{1,0:T(8,128)(2,1)}, ...) | async-done | bytes 3145744 | tf_op jit(solution)/shard_map/psum | solution.py:334
  1627.0 204.8 %reduce-scatter.14.cloned.1.call-done = bf16[128,6144]{1,0:T(8,128)(2,1)} async-done(((bf16[1024,6144]{1,0:T(8,128)(2,1)}), bf16[128,6144]{1,0:T(8,128)(2,1)}) %reduce-scatter.14.cloned.1.call-update) | async-done | bytes 1572880 | tf_op jit(solution)/shard_map/reduce_scatter | solution.py:316
  (292 shorter events, 273.0 us)
Async XLA Ops:
  7.2 526.4 %all-gather.11.cloned.1.call-start = ((), (), s32[]{:S(2)}) async-start(), calls=%async_computation.9 | async-start | bytes 14155776 | tf_op jit(solution)/shard_map/all_gather | solution.py:114
  7.9 533.1 %all-gather.13.cloned.1.call-start = ((), (), s32[]{:S(2)}) async-start(), calls=%async_computation.10 | async-start | bytes 7077888 | tf_op jit(solution)/shard_map/all_gather | solution.py:106
  8.7 601.0 %all-gather.15.cloned.1.call-start = ((), (), s32[]{:S(2)}) async-start(), calls=%async_computation.11 | async-start | bytes 2359296 | tf_op jit(solution)/shard_map/all_gather | solution.py:107
  9.4 611.3 %all-gather.17.cloned.1.call-start = ((), (), s32[]{:S(2)}) async-start(), calls=%async_computation.12 | async-start | bytes 9437184 | tf_op jit(solution)/shard_map/all_gather | solution.py:108
  11.2 50.3 %copy-start.29 = (f32[16,2025]{1,0:T(8,128)S(1)}, f32[16,2025]{1,0:T(8,128)}, u32[]{:S(2)}) copy-start(f32[16,2025]{1,0:T(8,128)} %param.28) | copy-start | bytes 388804
  11.2 479.9 %all-to-all-start = ((bf16[4,2,5,2,8,1024]{5,4,3,2,1,0:T(8,128)(2,1)}), bf16[4,2,5,2,8,1024]{5,4,3,2,1,0:T(8,128)(2,1)S(1)}, u32[]{:S(2)}, u32[]{:S(2)}) async-start(bf16[4,2,5,2,8,1024]{5,4,3,2,1,0:T(8,128)(2,1)} %bitcast.2), calls=%async_computation | async-start | bytes 2621440 | tf_op jit(solution)/shard_map/all_to_all | solution.py:123
  15.6 617.2 %all-gather.19.cloned.1.call-start = ((), (), s32[]{:S(2)}) async-start(), calls=%async_computation.13 | async-start | bytes 9437184 | tf_op jit(solution)/shard_map/all_gather | solution.py:109
  36.4 577.8 %copy-start.26 = (f32[2,5,4,2,8]{4,3,2,1,0:T(2,128)}, f32[2,5,4,2,8]{4,3,2,1,0:T(2,128)S(1)}, u32[]{:S(2)}) copy-start(f32[2,5,4,2,8]{4,3,2,1,0:T(2,128)S(1)} %compare_convert_fusion) | copy-start | bytes 7684
  36.9 503.0 %copy-start.47 = (pred[2]{0:T(512)(128)(4,1)}, pred[2]{0:T(512)(128)(4,1)S(1)}, u32[]{:S(2)}) copy-start(pred[2]{0:T(512)(128)(4,1)S(1)} %fusion.80) | copy-start | bytes 10
  398.4 47.4 %copy-start.23 = (bf16[1,10,2,2,16,1024]{5,4,3,2,1,0:T(8,128)(2,1)S(1)}, bf16[1,10,2,2,16,1024]{5,4,3,2,1,0:T(8,128)(2,1)}, u32[]{:S(2)}) copy-start(bf16[1,10,2,2,16,1024]{5,4,3,2,1,0:T(8,128)(2,1)} %param.29) | copy-start | bytes 3932164
  432.8 36.5 %copy-start.52 = (bf16[128]{0:T(256)(128)(2,1)S(1)}, bf16[128]{0:T(256)(128)(2,1)}, u32[]{:S(2)}) copy-start(bf16[128]{0:T(256)(128)(2,1)} %param.25) | copy-start | bytes 772
  491.1 49.0 %copy-start = (bf16[4,2,5,2,8,1024]{5,4,3,2,1,0:T(8,128)(2,1)}, bf16[4,2,5,2,8,1024]{5,4,3,2,1,0:T(8,128)(2,1)S(1)}, u32[]{:S(2)}) copy-start(bf16[4,2,5,2,8,1024]{5,4,3,2,1,0:T(8,128)(2,1)S(1)} %all-to-all-done) | copy-start | bytes 3932164
  491.1 40.6 %all-to-all-start.2 = ((bf16[4,2,5,2,8,1024]{5,4,3,2,1,0:T(8,128)(2,1)}), bf16[4,2,5,2,8,1024]{5,4,3,2,1,0:T(8,128)(2,1)S(1)}, u32[]{:S(2)}, u32[]{:S(2)}) async-start(bf16[4,2,5,2,8,1024]{5,4,3,2,1,0:T(8,128)(2,1)} %bitcast.302), calls=%async_computation.2 | async-start | bytes 2621440 | tf_op jit(solution)/shard_map/all_to_all | solution.py:124
  515.2 907.0 %reduce-scatter.8.cloned.1.call-start = ((), (), s32[]{:S(2)}) async-start(), calls=%async_computation.15 | async-start | bytes 2359296 | tf_op jit(solution)/shard_map/reduce_scatter | solution.py:295
  540.1 76.4 %copy-start.30 = (f32[2,1024]{1,0:T(2,128)}, f32[2,1024]{1,0:T(2,128)S(1)}, u32[]{:S(2)}) copy-start(f32[2,1024]{1,0:T(2,128)S(1)} %get-tuple-element.137) | copy-start | bytes 24580
  666.3 755.9 %reduce-scatter.6.cloned.1.call-start = ((), (), s32[]{:S(2)}) async-start(), calls=%async_computation.14 | async-start | bytes 7077888 | tf_op jit(solution)/shard_map/reduce_scatter | solution.py:292
  807.3 614.9 %reduce-scatter.12.cloned.1.call-start = ((), (), s32[]{:S(2)}) async-start(), calls=%async_computation.17 | async-start | bytes 9437184 | tf_op jit(solution)/shard_map/reduce_scatter | solution.py:301
  821.1 601.1 %reduce-scatter.10.cloned.1.call-start = ((), (), s32[]{:S(2)}) async-start(), calls=%async_computation.16 | async-start | bytes 9437184 | tf_op jit(solution)/shard_map/reduce_scatter | solution.py:298
  833.0 715.9 %all-reduce.11.cloned.1.call-start = ((), (), s32[]{:S(2)}) async-start(), calls=%async_computation.19 | async-start | bytes 2080768 | tf_op jit(solution)/shard_map/psum | solution.py:343
  833.8 575.3 %copy-start.48 = (pred[2]{0:T(512)(128)(4,1)S(1)}, pred[2]{0:T(512)(128)(4,1)}, u32[]{:S(2)}) copy-start(pred[2]{0:T(512)(128)(4,1)} %copy-done.47) | copy-start | bytes 10
  1422.0 198.4 %all-reduce.13.cloned.1.call-start = ((), (), s32[]{:S(2)}) async-start(), calls=%async_computation.20 | async-start | bytes 6291456 | tf_op jit(solution)/shard_map/psum | solution.py:334
  1422.8 409.1 %reduce-scatter.14.cloned.1.call-start = ((), (), s32[]{:S(2)}) async-start(), calls=%async_computation.18 | async-start | bytes 14155776 | tf_op jit(solution)/shard_map/reduce_scatter | solution.py:316
  1433.2 21.2 %all-to-all-start.3 = ((bf16[1,2,5,8,8,1024]{5,4,2,1,0,3:T(8,128)(2,1)}), bf16[1,2,5,8,8,1024]{5,4,2,1,0,3:T(8,128)(2,1)}, u32[]{:S(2)}, u32[]{:S(2)}) async-start(bf16[1,2,5,8,8,1024]{5,4,2,1,0,3:T(8,128)(2,1)} %copy.181), calls=%async_computation.3 | async-start | bytes 2621440 | tf_op jit(solution)/shard_map/all_to_all | solution.py:251
  1454.3 99.6 %all-to-all-start.1 = ((bf16[1,2,5,8,8,1024]{5,4,2,1,0,3:T(8,128)(2,1)}), bf16[1,2,5,8,8,1024]{5,4,2,1,0,3:T(8,128)(2,1)S(1)}, u32[]{:S(2)}, u32[]{:S(2)}) async-start(bf16[1,2,5,8,8,1024]{5,4,2,1,0,3:T(8,128)(2,1)} %copy.167), calls=%async_computation.1 | async-start | bytes 2621440 | tf_op jit(solution)/shard_map/all_to_all | solution.py:186
  (49 other events, 539.8 us)
Sparse Core Ops, SparseCore 0:
  10.2 178.3 all-gather.10
  190.8 97.0 all-gather.12
  290.0 46.8 all-gather.14
  338.9 124.1 all-gather.16
  465.1 123.1 all-gather.18
  666.4 63.4 reduce-scatter.7
  807.4 114.7 reduce-scatter.5
  925.9 148.9 reduce-scatter.11
  1079.0 147.9 reduce-scatter.9
  1422.1 126.7 all-reduce.10
  1551.7 68.6 all-reduce.12
  1624.3 207.5 reduce-scatter.13
where the time goes:
time: 1850 us; the launch traced here: 1840 us
  other arithmetic  638 us (34%)
  local copies, waits for them, and re-layouts  489 us (26%)
  waiting for transfers between devices  332 us (18%)
  matrix products  182 us (10%)
  blocking collectives  145 us (8%)
  starting transfers between devices  38.3 us (2%)
  between operations  18.6 us (1%)
    scatter-add x1, other arithmetic, build_bias(): return jnp.take(table, offset_index(), axis=1)  543 us
    gather x2, local copies, waits for them, and re-layouts, build_bias(): return jnp.take(table, offset_index(), axis=1)  371 us
    reduce_scatter x1, waiting for transfers between devices, body(): lax.psum_scatter(modulate_weight_full.astype(jnp.bfloat16), 'clip', scatt...  205 us
    psum x1, waiting for transfers between devices, body(): lax.psum(triple_weight_grad.astype(jnp.bfloat16), 'win').astype(jnp.float32)  65.1 us
    psum x1, waiting for transfers between devices, body(): table_grad = lax.psum(bias_back(grad_bias)[0], ('clip', 'win'))  37.8 us
  transfers between devices with their start and end apart: 16, of which 5 were waited for; matrix products, arithmetic and copies ran while one was open for 69% of the time, Pallas kernels for 0%

commit v1 on v0

v1 whole, which is shorter than its diff:
```python
import math
import jax
import jax.numpy as jnp
import numpy as np
from jax import lax
from jax.experimental import pallas as pl
from jax.experimental.pallas import tpu as pltpu
from jax.sharding import PartitionSpec as P

WIN_T = 5
WIN_S = 8
WINDOW = WIN_T * WIN_S * WIN_S
CELL = WIN_S * WIN_S
SPAN = 2 * WIN_S - 1
TSPAN = 2 * WIN_T - 1
HEAD = 64
CORES = 2
EPS = 1e-06
NEG = -30000.0
GELU_C = math.sqrt(2.0 / math.pi)
GELU_A = 0.044715
F32 = jnp.float32
BF16 = jnp.bfloat16
VMEM_LIMIT = 56 * 1024 * 1024

NN = (((1,), (0,)), ((), ()))
NT = (((1,), (1,)), ((), ()))
TN = (((0,), (0,)), ((), ()))


def mm(a, b, dims=NN):
    return lax.dot_general(a, b, dims, preferred_element_type=F32)


def any_spec():
    return pl.BlockSpec(memory_space=pl.ANY)


def params(grid_rank):
    return pltpu.CompilerParams(
        dimension_semantics=("arbitrary",) * grid_rank, vmem_limit_bytes=VMEM_LIMIT
    )


def ring_order(n):
    ny = 1 << (int(math.log2(n)) // 2)
    nz = n // ny
    if ny < 2 or nz % 2:
        return list(range(n))
    walk = []
    for z in range(nz):
        ys = list(range(1, ny))
        walk += [z * ny + y for y in (ys if z % 2 == 0 else ys[::-1])]
    return walk + [z * ny for z in reversed(range(nz))]


class Ring:
    def __init__(self, n):
        self.n = n
        order = ring_order(n)
        place = [order.index(r) for r in range(n)]
        self.order = jnp.asarray(np.array(order, np.int32))
        self.place = jnp.asarray(np.array(place, np.int32))
        self.rank = lax.axis_index("clip")
        self.pos = self.place[self.rank]
        self.up = [(order[i], order[(i + 1) % n]) for i in range(n)]
        self.down = [(b, a) for a, b in self.up]
        self.core = lax.axis_index("win") % CORES
        wins = lax.axis_size("win")
        self.swap = [(w, w ^ 1) for w in range(wins)]
        self.across = [
            [(w, w ^ k) for w in range(wins)] for k in (2 << i for i in range(8)) if k < wins
        ]
        self.pairs = [[(w, w ^ k) for w in range(wins)] for k in (1 << i for i in range(8)) if k < wins]
        self.clip_pairs = [
            (k, [(r, r ^ k) for r in range(n)]) for k in (1 << i for i in range(8)) if k < n
        ]

    def at(self, offset):
        return self.order[(self.pos + offset) % self.n]

    def steps(self, flip):
        far, near = self.n // 2, (self.n - 1) // 2
        return (near, far) if flip else (far, near)

    def index(self):
        ranks = [self.at(p) for p in range(self.n)]
        return jnp.stack(ranks + [self.core]).astype(jnp.int32)

    def gather(self, piece, flip):
        far, near = self.steps(flip)
        ahead, back = [], []
        a = b = piece
        for s in range(max(far, near)):
            if s < far:
                a = lax.ppermute(a, "clip", self.up)
                ahead.append(a)
            if s < near:
                b = lax.ppermute(b, "clip", self.down)
                back.append(b)
        own = back + ahead[::-1]
        return own, [lax.ppermute(o, "win", self.swap) for o in own]

    def scatter(self, keep, send, flip):
        far, near = self.steps(flip)
        got = lax.ppermute(send, "win", self.swap)

        def part(offset):
            r = self.at(offset)
            one = lambda arr: lax.dynamic_index_in_dim(arr, r, 0, keepdims=False).astype(F32)
            return one(keep) + one(got)

        a, b = part(far).astype(BF16), part(-near).astype(BF16)
        for s in range(max(far, near)):
            if s < far:
                a = lax.ppermute(a, "clip", self.up)
                if s < far - 1:
                    a = (a.astype(F32) + part(far - 1 - s)).astype(BF16)
            if s < near:
                b = lax.ppermute(b, "clip", self.down)
                if s < near - 1:
                    b = (b.astype(F32) + part(1 + s - near)).astype(BF16)
        total = (part(0) + a.astype(F32) + b.astype(F32)).astype(BF16)
        for perm in self.across:
            other = lax.ppermute(total, "win", perm)
            total = (total.astype(F32) + other.astype(F32)).astype(BF16)
        other = lax.ppermute(total, "win", self.swap)
        first = jnp.where(self.core == 0, total, other)
        second = jnp.where(self.core == 0, other, total)
        return first, second

    def gather_small(self, block):
        for k, perm in self.clip_pairs:
            other = lax.ppermute(block, "clip", perm)
            high = (self.rank & k) > 0
            block = jnp.where(
                high, jnp.concatenate([other, block]), jnp.concatenate([block, other])
            )
        return block

    def scatter_small(self, block):
        for k, perm in reversed(self.clip_pairs):
            high = (self.rank & k) > 0
            low_part, high_part = block[:k], block[k:]
            other = lax.ppermute(jnp.where(high, low_part, high_part), "clip", perm)
            block = jnp.where(high, high_part, low_part) + other
        return block[0]

    def sum_win(self, block):
        for perm in self.pairs:
            block = block + lax.ppermute(block, "win", perm)
        return block

    def sum_all(self, block):
        block = self.sum_win(block)
        for _, perm in self.clip_pairs:
            block = block + lax.ppermute(block, "clip", perm)
        return block


class Weight:
    def __init__(self, local, own, sib, col=0):
        self.local, self.own, self.sib, self.col = local, own, sib, col
        self.rows, self.cols = local.shape
        self.count = len(own)

    def operands(self):
        return [self.local, *self.own, *self.sib]

    def specs(self):
        return [any_spec()] * (1 + 2 * self.count)

    def shape(self):
        return (self.rows * (self.count + 1), self.cols)

    def n_sems(self):
        return 2 * self.count + 1

    def piece(self, idx, refs, dst, sems, i, base, start, width):
        half = self.rows // 2
        cols = pl.ds(start, width)
        into = pl.ds(start, width)
        if i == 0:
            rows = pl.ds(pl.multiple_of(base, self.rows), self.rows)
            return [
                pltpu.make_async_copy(refs[0].at[:, cols], dst.at[rows, into], sems.at[0])
            ]
        from_cols = pl.ds(self.col + start, width)
        core = idx[self.count + 1]
        copies = []
        for which, place in ((0, core), (1, 1 - core)):
            slot = which * self.count + i
            rows = pl.ds(pl.multiple_of(base + place * half, half), half)
            copies.append(
                pltpu.make_async_copy(
                    refs[slot].at[:, from_cols], dst.at[rows, into], sems.at[slot]
                )
            )
        return copies

    def whole(self, idx, refs, dst, sems, start=0, width=None):
        copies = []
        for i in range(self.count + 1):
            copies += self.piece(
                idx, refs, dst, sems, i, idx[i] * self.rows, start, width or self.cols
            )
        return copies


def kernel_call(body, idx, grid, in_specs, out_specs, out_shape, scratch, operands, flops, nbytes):
    return pl.pallas_call(
        body,
        grid_spec=pltpu.PrefetchScalarGridSpec(
            num_scalar_prefetch=1,
            grid=grid,
            in_specs=in_specs,
            out_specs=out_specs,
            scratch_shapes=scratch,
        ),
        out_shape=out_shape,
        compiler_params=params(len(grid)),
        cost_estimate=pl.CostEstimate(
            flops=int(flops), bytes_accessed=int(nbytes), transcendentals=0
        ),
    )(idx, *operands)


def norm_rows(v):
    center = v - jnp.mean(v, axis=-1, keepdims=True)
    inverse = lax.rsqrt(jnp.mean(center * center, axis=-1, keepdims=True) + EPS)
    return center * inverse, inverse


def norm_back(grad, normed, inverse):
    mean_grad = jnp.mean(grad, axis=-1, keepdims=True)
    mean_cross = jnp.mean(grad * normed, axis=-1, keepdims=True)
    return inverse * (grad - mean_grad - normed * mean_cross)


CHUNK = 64


def qkv_project(idx, x, mod, weight, bias):
    tokens, width = x.shape
    cols = weight.cols
    block = 512
    steps = cols // block
    rows = WINDOW
    nw = tokens // rows
    nref = weight.n_sems()

    def body(idx, x_ref, mod_ref, bias_ref, *rest):
        w_refs, rest = rest[:nref], rest[nref:]
        norm_ref, out_ref, w_buf, sems = rest
        j, w = pl.program_id(0), pl.program_id(1)

        @pl.when((j == 0) & (w == 0))
        def _():
            for s in range(steps):
                for c in weight.whole(idx, w_refs, w_buf, sems.at[s], s * block, block):
                    c.start()

            def chunk(i, _):
                r = pl.ds(pl.multiple_of(i * CHUNK, CHUNK), CHUNK)
                normed, _inv = norm_rows(x_ref[r, :].astype(F32))
                norm_ref[r, :] = (normed * (1.0 + mod_ref[1:2, :]) + mod_ref[0:1, :]).astype(BF16)
                return 0

            lax.fori_loop(0, tokens // CHUNK, chunk, 0)

        for s in range(steps):

            @pl.when((j == s) & (w == 0))
            def _():
                for c in weight.whole(idx, w_refs, w_buf, sems.at[s], s * block, block):
                    c.wait()

        a = norm_ref[pl.ds(pl.multiple_of(w * rows, rows), rows), :]
        b = w_buf[:, pl.ds(pl.multiple_of(j * block, block), block)]
        out_ref[...] = (mm(a, b) + bias_ref[...]).astype(BF16)

    return kernel_call(
        body,
        idx,
        (steps, nw),
        [
            pl.BlockSpec((tokens, width), lambda j, w, idx: (0, 0)),
            pl.BlockSpec((6, width), lambda j, w, idx: (0, 0)),
            pl.BlockSpec((1, block), lambda j, w, idx: (0, j)),
            *weight.specs(),
        ],
        [
            pl.BlockSpec((tokens, width), lambda j, w, idx: (0, 0)),
            pl.BlockSpec((rows, block), lambda j, w, idx: (w, j)),
        ],
        [
            jax.ShapeDtypeStruct((tokens, width), BF16),
            jax.ShapeDtypeStruct((tokens, cols), BF16),
        ],
        [pltpu.VMEM((width, cols), BF16), pltpu.SemaphoreType.DMA((steps, nref))],
        [x, mod, bias, *weight.operands()],
        2 * tokens * width * cols,
        2 * (tokens * (2 * width + cols) + width * cols),
    )


def bias_rows(table):
    return jnp.concatenate(
        [table[:, (WIN_T - 1 - f) * CELL : (WIN_T - 1 - f) * CELL + WINDOW] for f in range(WIN_T)],
        axis=0,
    )


def attention_specs(pairs):
    q = pl.BlockSpec((WINDOW, 2 * HEAD), lambda h, w, nv: (w, h))
    k = pl.BlockSpec((WINDOW, 2 * HEAD), lambda h, w, nv: (w, pairs + h))
    v = pl.BlockSpec((WINDOW, 2 * HEAD), lambda h, w, nv: (w, 2 * pairs + h))
    t = pl.BlockSpec((2, CELL, TSPAN * CELL), lambda h, w, nv: (h, 0, 0))
    return q, k, v, t


def attend(valid, triple, table):
    tokens = triple.shape[0]
    width = triple.shape[1] // 3
    nw = tokens // WINDOW
    pairs = width // (2 * HEAD)

    def body(nv, q_ref, k_ref, v_ref, t_ref, o_ref, l_ref):
        w = pl.program_id(1)
        keep = lax.broadcasted_iota(jnp.int32, (WINDOW, 1), 0) < nv[w] * CELL
        outs = []
        for a in range(2):
            cols = slice(a * HEAD, (a + 1) * HEAD)
            q = q_ref[:, cols] * jnp.asarray(HEAD**-0.5, BF16)
            s = mm(k_ref[:, cols], q, NT)
            s = jnp.where(keep, s + bias_rows(t_ref[a]), NEG)
            peak = jnp.max(s, axis=0, keepdims=True)
            e = jnp.exp(s - peak)
            total = jnp.sum(e, axis=0, keepdims=True)
            p = (e * (1.0 / total)).astype(BF16)
            l_ref[0, 0, a : a + 1, :] = peak + jnp.log(total)
            outs.append(mm(v_ref[:, cols], p, TN))
        o_ref[...] = jnp.concatenate(outs, axis=0).T.astype(BF16)

    q, k, v, t = attention_specs(pairs)
    return kernel_call(
        body,
        valid,
        (pairs, nw),
        [q, k, v, t],
        [
            pl.BlockSpec((WINDOW, 2 * HEAD), lambda h, w, nv: (w, h)),
            pl.BlockSpec((1, 1, 2, WINDOW), lambda h, w, nv: (w, h, 0, 0)),
        ],
        [
            jax.ShapeDtypeStruct((tokens, width), BF16),
            jax.ShapeDtypeStruct((nw, pairs, 2, WINDOW), F32),
        ],
        [],
        [triple, triple, triple, table],
        4 * tokens * WINDOW * width * 4,
        2 * tokens * 4 * width,
    )


def attend_back(valid, triple, table, grad, logs):
    tokens = triple.shape[0]
    width = triple.shape[1] // 3
    nw = tokens // WINDOW
    pairs = width // (2 * HEAD)

    def body(nv, q_ref, k_ref, v_ref, t_ref, g_ref, l_ref, dq_ref, dk_ref, dv_ref, dt_ref):
        w = pl.program_id(1)
        keep = lax.broadcasted_iota(jnp.int32, (WINDOW, 1), 0) < nv[w] * CELL
        dqs, dks, dvs = [], [], []

        @pl.when(w == 0)
        def _():
            dt_ref[...] = jnp.zeros_like(dt_ref)

        for a in range(2):
            cols = slice(a * HEAD, (a + 1) * HEAD)
            q = q_ref[:, cols] * jnp.asarray(HEAD**-0.5, BF16)
            k, g = k_ref[:, cols], g_ref[:, cols]
            s = mm(k, q, NT)
            s = jnp.where(keep, s + bias_rows(t_ref[a]), NEG)
            p = jnp.exp(s - l_ref[0, 0, a : a + 1, :])
            gp = mm(v_ref[:, cols], g, NT)
            delta = jnp.sum(gp * p, axis=0, keepdims=True)
            ds = jnp.where(keep, p * (gp - delta), 0.0).astype(BF16)
            dvs.append(mm(p.astype(BF16), g))
            dks.append(mm(ds, q))
            dqs.append(mm(k, ds, TN))
            wide = ds.astype(F32)
            for f in range(WIN_T):
                at = (WIN_T - 1 - f) * CELL
                dt_ref[a, :, at : at + WINDOW] += wide[f * CELL : (f + 1) * CELL, :]
        scale = HEAD**-0.5
        dq_ref[...] = (jnp.concatenate(dqs, axis=0) * scale).T.astype(BF16)
        dk_ref[...] = jnp.concatenate(dks, axis=1).astype(BF16)
        dv_ref[...] = jnp.concatenate(dvs, axis=1).astype(BF16)

    q, k, v, t = attention_specs(pairs)
    one = pl.BlockSpec((WINDOW, 2 * HEAD), lambda h, w, nv: (w, h))
    return kernel_call(
        body,
        valid,
        (pairs, nw),
        [q, k, v, t, one, pl.BlockSpec((1, 1, 2, WINDOW), lambda h, w, nv: (w, h, 0, 0))],
        [one, one, one, t],
        [jax.ShapeDtypeStruct((tokens, width), BF16)] * 3
        + [jax.ShapeDtypeStruct((2 * pairs, CELL, TSPAN * CELL), F32)],
        [],
        [triple, triple, triple, table, grad, logs],
        10 * tokens * WINDOW * width * 4,
        2 * tokens * 8 * width,
    )


def attention_out(idx, mixed, x, mod, keep, weight, bias):
    tokens, width = x.shape
    rows = WINDOW
    nref = weight.n_sems()

    def body(idx, mixed_ref, x_ref, mod_ref, keep_ref, bias_ref, *rest):
        w_refs, rest = rest[:nref], rest[nref:]
        att_ref, mid_ref, norm_ref, w_buf, acc, sems = rest

        @pl.when(pl.program_id(0) == 0)
        def _():
            copies = weight.whole(idx, w_refs, w_buf, sems)
            for c in copies:
                c.start()
            for c in copies:
                c.wait()

        acc[...] = mm(mixed_ref[...], w_buf[...])

        def chunk(i, _):
            r = pl.ds(pl.multiple_of(i * CHUNK, CHUNK), CHUNK)
            att = acc[r, :] + bias_ref[...]
            mid = x_ref[r, :].astype(F32) + keep_ref[r, :] * mod_ref[2:3, :] * att
            normed, _inv = norm_rows(mid)
            att_ref[r, :] = att.astype(BF16)
            mid_ref[r, :] = mid
            norm_ref[r, :] = (normed * (1.0 + mod_ref[4:5, :]) + mod_ref[3:4, :]).astype(BF16)
            return 0

        lax.fori_loop(0, rows // CHUNK, chunk, 0)

    block = pl.BlockSpec((rows, width), lambda w, idx: (w, 0))
    return kernel_call(
        body,
        idx,
        (tokens // rows,),
        [
            block,
            block,
            pl.BlockSpec((6, width), lambda w, idx: (0, 0)),
            pl.BlockSpec((rows, 1), lambda w, idx: (w, 0)),
            pl.BlockSpec((1, width), lambda w, idx: (0, 0)),
            *weight.specs(),
        ],
        [block, block, block],
        [
            jax.ShapeDtypeStruct((tokens, width), BF16),
            jax.ShapeDtypeStruct((tokens, width), F32),
            jax.ShapeDtypeStruct((tokens, width), BF16),
        ],
        [
            pltpu.VMEM((width, width), BF16),
            pltpu.VMEM((rows, width), F32),
            pltpu.SemaphoreType.DMA((nref,)),
        ],
        [mixed, x, mod, keep, bias, *weight.operands()],
        2 * tokens * width * width,
        tokens * width * 12 + 2 * width * width,
    )


def gelu_up(idx, norm_mid, weight, bias):
    tokens, width = norm_mid.shape
    cols = weight.cols
    block = 512
    steps = cols // block
    rows = WINDOW
    nw = tokens // rows
    nref = weight.n_sems()

    def body(idx, x_ref, bias_ref, *rest):
        w_refs, rest = rest[:nref], rest[nref:]
        act_ref, slope_ref, w_buf, sems = rest
        j, w = pl.program_id(0), pl.program_id(1)

        @pl.when((j == 0) & (w == 0))
        def _():
            for s in range(steps):
                for c in weight.whole(idx, w_refs, w_buf, sems.at[s], s * block, block):
                    c.start()

        for s in range(steps):

            @pl.when((j == s) & (w == 0))
            def _():
                for c in weight.whole(idx, w_refs, w_buf, sems.at[s], s * block, block):
                    c.wait()

        a = x_ref[pl.ds(pl.multiple_of(w * rows, rows), rows), :]
        b = w_buf[:, pl.ds(pl.multiple_of(j * block, block), block)]
        h = mm(a, b) + bias_ref[...]
        square = h * h
        inner = GELU_C * h * (1.0 + GELU_A * square)
        th = jnp.tanh(inner)
        left = 0.5 * (1.0 + th)
        act_ref[...] = (h * left).astype(BF16)
        slope = left + 0.5 * h * (1.0 - th * th) * (GELU_C * (1.0 + 3.0 * GELU_A * square))
        slope_ref[...] = slope.astype(BF16)

    return kernel_call(
        body,
        idx,
        (steps, nw),
        [
            pl.BlockSpec((tokens, width), lambda j, w, idx: (0, 0)),
            pl.BlockSpec((1, block), lambda j, w, idx: (0, j)),
            *weight.specs(),
        ],
        [pl.BlockSpec((rows, block), lambda j, w, idx: (w, j))] * 2,
        [jax.ShapeDtypeStruct((tokens, cols), BF16)] * 2,
        [pltpu.VMEM((width, cols), BF16), pltpu.SemaphoreType.DMA((steps, nref))],
        [norm_mid, bias, *weight.operands()],
        2 * tokens * width * cols,
        2 * (tokens * (width + 2 * cols) + width * cols),
    )


def ffn_down(idx, activated, middle, cot, keep, gate, weight, bias):
    tokens, inner = activated.shape
    width = weight.cols
    block = 256
    steps = width // block
    rows = WINDOW
    nw = tokens // rows
    nref = weight.n_sems()

    def body(idx, act_ref, mid_ref, cot_ref, keep_ref, gate_ref, bias_ref, *rest):
        w_refs, rest = rest[:nref], rest[nref:]
        out_ref, gg_ref, w_buf, sems = rest
        j, w = pl.program_id(0), pl.program_id(1)

        @pl.when((j == 0) & (w == 0))
        def _():
            for s in range(steps):
                for c in weight.whole(idx, w_refs, w_buf, sems.at[s], s * block, block):
                    c.start()

        for s in range(steps):

            @pl.when((j == s) & (w == 0))
            def _():
                for c in weight.whole(idx, w_refs, w_buf, sems.at[s], s * block, block):
                    c.wait()

        a = act_ref[pl.ds(pl.multiple_of(w * rows, rows), rows), :]
        b = w_buf[:, pl.ds(pl.multiple_of(j * block, block), block)]
        ff = (mm(a, b) + bias_ref[...]) * keep_ref[...]
        out_ref[...] = (mid_ref[...] + ff * gate_ref[...]).astype(BF16)
        part = jnp.sum(ff * cot_ref[...].astype(F32), axis=0, keepdims=True)

        @pl.when(w == 0)
        def _():
            gg_ref[...] = part

        @pl.when(w > 0)
        def _():
            gg_ref[...] += part

    cell = pl.BlockSpec((rows, block), lambda j, w, idx: (w, j))
    line = pl.BlockSpec((1, block), lambda j, w, idx: (0, j))
    return kernel_call(
        body,
        idx,
        (steps, nw),
        [
            pl.BlockSpec((tokens, inner), lambda j, w, idx: (0, 0)),
            cell,
            cell,
            pl.BlockSpec((rows, 1), lambda j, w, idx: (w, 0)),
            line,
            line,
            *weight.specs(),
        ],
        [cell, line],
        [jax.ShapeDtypeStruct((tokens, width), BF16), jax.ShapeDtypeStruct((1, width), F32)],
        [pltpu.VMEM((inner, width), BF16), pltpu.SemaphoreType.DMA((steps, nref))],
        [activated, middle, cot, keep, gate, bias, *weight.operands()],
        2 * tokens * inner * width,
        2 * (tokens * (inner + 4 * width) + width * inner),
    )


def outer_product(idx, left, right, block, sums=False):
    _, half, tokens = left.shape
    cols = right.shape[1]

    def body(idx, mine_ref, other_ref, right_ref, keep_ref, send_ref, *sum_ref):
        b = right_ref[...]
        send_ref[...] = mm(other_ref[...], b).astype(BF16)
        keep_ref[...] = mm(mine_ref[...], b).astype(BF16)
        if sums:
            sum_ref[0][...] = jnp.sum(b.astype(F32), axis=0, keepdims=True)

    n = idx.shape[0] - 1
    out = pl.BlockSpec((half, block), lambda j, idx: (0, j))
    shape = jax.ShapeDtypeStruct((half, cols), BF16)
    extra = [pl.BlockSpec((1, block), lambda j, idx: (0, j))] if sums else []
    extra_shape = [jax.ShapeDtypeStruct((1, cols), F32)] if sums else []
    return kernel_call(
        body,
        idx,
        (cols // block,),
        [
            pl.BlockSpec((None, half, tokens), lambda j, idx: (idx[n], 0, 0)),
            pl.BlockSpec((None, half, tokens), lambda j, idx: (1 - idx[n], 0, 0)),
            pl.BlockSpec((tokens, block), lambda j, idx: (0, j)),
        ],
        [out, out, *extra],
        [shape, shape, *extra_shape],
        [],
        [left, left, right],
        4 * tokens * half * cols,
        2 * (2 * half * tokens + tokens * cols + 2 * half * cols),
    )


def hidden_back(idx, grad_ffn, slope, norm_t, weight):
    tokens, width = grad_ffn.shape
    inner = slope.shape[1]
    block = weight.rows
    steps = weight.count + 1
    half = norm_t.shape[1]
    nref = weight.n_sems()

    def body(idx, g_ref, slope_ref, mine_ref, other_ref, *rest):
        w_refs, rest = rest[:nref], rest[nref:]
        gh_ref, keep_ref, send_ref, sum_ref, w_buf, sems = rest
        j = pl.program_id(0)

        def copies(s):
            return weight.piece(idx, w_refs, w_buf, sems, s, s * block, 0, width)

        @pl.when(j == 0)
        def _():
            for s in range(steps):
                for c in copies(s):
                    c.start()

        for s in range(steps):

            @pl.when(j == s)
            def _():
                for c in copies(s):
                    c.wait()

        b = w_buf[pl.ds(pl.multiple_of(j * block, block), block), :]
        gh = (mm(g_ref[...], b, NT) * slope_ref[...].astype(F32)).astype(BF16)
        gh_ref[...] = gh
        sum_ref[...] = jnp.sum(gh.astype(F32), axis=0, keepdims=True)
        send_ref[...] = mm(other_ref[...], gh).astype(BF16)
        keep_ref[...] = mm(mine_ref[...], gh).astype(BF16)

    n = weight.count + 1
    out = pl.BlockSpec((half, block), lambda j, idx: (0, idx[j]))
    return kernel_call(
        body,
        idx,
        (steps,),
        [
            pl.BlockSpec((tokens, width), lambda j, idx: (0, 0)),
            pl.BlockSpec((tokens, block), lambda j, idx: (0, idx[j])),
            pl.BlockSpec((None, half, tokens), lambda j, idx: (idx[n], 0, 0)),
            pl.BlockSpec((None, half, tokens), lambda j, idx: (1 - idx[n], 0, 0)),
            *weight.specs(),
        ],
        [
            pl.BlockSpec((tokens, block), lambda j, idx: (0, idx[j])),
            out,
            out,
            pl.BlockSpec((1, block), lambda j, idx: (0, idx[j])),
        ],
        [
            jax.ShapeDtypeStruct((tokens, inner), BF16),
            jax.ShapeDtypeStruct((half, inner), BF16),
            jax.ShapeDtypeStruct((half, inner), BF16),
            jax.ShapeDtypeStruct((1, inner), F32),
        ],
        [pltpu.VMEM((inner, width), BF16), pltpu.SemaphoreType.DMA((nref,))],
        [grad_ffn, slope, norm_t, norm_t, *weight.operands()],
        8 * tokens * width * inner,
        2 * (tokens * (width + 2 * inner) + 2 * width * inner),
    )


def middle_back(idx, grad_hidden, middle, cot, attention, keep, mod, up, project):
    tokens, inner = grad_hidden.shape
    width = middle.shape[1]
    rows = WINDOW
    n_up, n_pr = up.n_sems(), project.n_sems()

    def body(idx, gh_ref, mid_ref, cot_ref, att_ref, keep_ref, mod_ref, *rest):
        up_refs, rest = rest[:n_up], rest[n_up:]
        pr_refs, rest = rest[:n_pr], rest[n_pr:]
        gm_ref, ga_ref, gx_ref, sum_ref, up_buf, pr_buf, acc, up_sems, pr_sems = rest

        @pl.when(pl.program_id(0) == 0)
        def _():
            first = up.whole(idx, up_refs, up_buf, up_sems)
            second = project.whole(idx, pr_refs, pr_buf, pr_sems)
            for c in first + second:
                c.start()
            sum_ref[...] = jnp.zeros_like(sum_ref)
            for c in first + second:
                c.wait()

        acc[...] = mm(gh_ref[...], up_buf[...], NT)

        def chunk(i, sums):
            r = pl.ds(pl.multiple_of(i * CHUNK, CHUNK), CHUNK)
            grad = acc[r, :]
            normed, inverse = norm_rows(mid_ref[r, :])
            whole = cot_ref[r, :].astype(F32) + norm_back(
                grad * (1.0 + mod_ref[4:5, :]), normed, inverse
            )
            gm_ref[r, :] = whole
            gated = keep_ref[r, :] * whole
            ga = (gated * mod_ref[2:3, :]).astype(BF16)
            ga_ref[r, :] = ga
            terms = (grad, grad * normed, gated * att_ref[r, :].astype(F32), ga.astype(F32))
            return tuple(
                s + jnp.sum(t.reshape(CHUNK // 8, 8, width), axis=0)
                for s, t in zip(sums, terms)
            )

        zero = jnp.zeros((8, width), F32)
        sums = lax.fori_loop(0, rows // CHUNK, chunk, (zero,) * 4)
        for i, s in enumerate(sums):
            sum_ref[i : i + 1, :] += jnp.sum(s, axis=0, keepdims=True)
        gx_ref[...] = mm(ga_ref[...], pr_buf[...], NT).astype(BF16)

    block = pl.BlockSpec((rows, width), lambda w, idx: (w, 0))
    return kernel_call(
        body,
        idx,
        (tokens // rows,),
        [
            pl.BlockSpec((rows, inner), lambda w, idx: (w, 0)),
            block,
            block,
            block,
            pl.BlockSpec((rows, 1), lambda w, idx: (w, 0)),
            pl.BlockSpec((6, width), lambda w, idx: (0, 0)),
            *up.specs(),
            *project.specs(),
        ],
        [block, block, block, pl.BlockSpec((4, width), lambda w, idx: (0, 0))],
        [
            jax.ShapeDtypeStruct((tokens, width), F32),
            jax.ShapeDtypeStruct((tokens, width), BF16),
            jax.ShapeDtypeStruct((tokens, width), BF16),
            jax.ShapeDtypeStruct((4, width), F32),
        ],
        [
            pltpu.VMEM((width, inner), BF16),
            pltpu.VMEM((width, width), BF16),
            pltpu.VMEM((rows, width), F32),
            pltpu.SemaphoreType.DMA((n_up,)),
            pltpu.SemaphoreType.DMA((n_pr,)),
        ],
        [grad_hidden, middle, cot, attention, keep, mod, *up.operands(), *project.operands()],
        2 * tokens * width * (inner + width),
        2 * (tokens * (inner + 8 * width) + width * (inner + width)),
    )


def input_back(idx, grads, x, grad_middle, mod, weight):
    tokens, width = x.shape
    rows = WINDOW
    nref = weight.n_sems()

    def body(idx, dq_ref, dk_ref, dv_ref, x_ref, gm_ref, mod_ref, *rest):
        w_refs, rest = rest[:nref], rest[nref:]
        out_ref, sum_ref, w_buf, acc, sems = rest

        @pl.when(pl.program_id(0) == 0)
        def _():
            copies = weight.whole(idx, w_refs, w_buf, sems)
            for c in copies:
                c.start()
            sum_ref[...] = jnp.zeros_like(sum_ref)
            for c in copies:
                c.wait()

        acc[...] = (
            mm(dq_ref[...], w_buf[:, 0:width], NT)
            + mm(dk_ref[...], w_buf[:, width : 2 * width], NT)
            + mm(dv_ref[...], w_buf[:, 2 * width : 3 * width], NT)
        )

        def chunk(i, sums):
            r = pl.ds(pl.multiple_of(i * CHUNK, CHUNK), CHUNK)
            grad = acc[r, :]
            normed, inverse = norm_rows(x_ref[r, :].astype(F32))
            back = norm_back(grad * (1.0 + mod_ref[1:2, :]), normed, inverse)
            out_ref[r, :] = (gm_ref[r, :] + back).astype(BF16)
            return tuple(
                s + jnp.sum(t.reshape(CHUNK // 8, 8, width), axis=0)
                for s, t in zip(sums, (grad, grad * normed))
            )

        zero = jnp.zeros((8, width), F32)
        sums = lax.fori_loop(0, rows // CHUNK, chunk, (zero,) * 2)
        for i, s in enumerate(sums):
            sum_ref[i : i + 1, :] += jnp.sum(s, axis=0, keepdims=True)

    block = pl.BlockSpec((rows, width), lambda w, idx: (w, 0))
    return kernel_call(
        body,
        idx,
        (tokens // rows,),
        [
            *([block] * 5),
            pl.BlockSpec((6, width), lambda w, idx: (0, 0)),
            *weight.specs(),
        ],
        [block, pl.BlockSpec((2, width), lambda w, idx: (0, 0))],
        [jax.ShapeDtypeStruct((tokens, width), BF16), jax.ShapeDtypeStruct((2, width), F32)],
        [
            pltpu.VMEM((width, 3 * width), BF16),
            pltpu.VMEM((rows, width), F32),
            pltpu.SemaphoreType.DMA((nref,)),
        ],
        [*grads, x, grad_middle, mod, *weight.operands()],
        6 * tokens * width * width,
        2 * (tokens * 9 * width + 3 * width * width),
    )


def triple_outer(idx, left, grads, block):
    _, half, tokens = left.shape
    width = grads[0].shape[1]
    per = width // block

    def body(idx, mine_ref, other_ref, q_ref, k_ref, v_ref, keep_ref, send_ref, sum_ref):
        for part, ref in enumerate((q_ref, k_ref, v_ref)):

            @pl.when(pl.program_id(0) // per == part)
            def _():
                b = ref[...]
                send_ref[...] = mm(other_ref[...], b).astype(BF16)
                keep_ref[...] = mm(mine_ref[...], b).astype(BF16)
                sum_ref[...] = jnp.sum(b.astype(F32), axis=0, keepdims=True)

    n = idx.shape[0] - 1
    out = pl.BlockSpec((half, block), lambda j, idx: (0, j))
    shape = jax.ShapeDtypeStruct((half, 3 * width), BF16)

    def part_spec(part):
        return pl.BlockSpec(
            (tokens, block), lambda j, idx: (0, jnp.clip(j - part * per, 0, per - 1))
        )

    return kernel_call(
        body,
        idx,
        (3 * per,),
        [
            pl.BlockSpec((None, half, tokens), lambda j, idx: (idx[n], 0, 0)),
            pl.BlockSpec((None, half, tokens), lambda j, idx: (1 - idx[n], 0, 0)),
            part_spec(0),
            part_spec(1),
            part_spec(2),
        ],
        [out, out, pl.BlockSpec((1, block), lambda j, idx: (0, j))],
        [shape, shape, jax.ShapeDtypeStruct((1, 3 * width), F32)],
        [],
        [left, left, *grads],
        12 * tokens * half * width,
        2 * (2 * half * tokens + 3 * tokens * width + 6 * half * width),
    )


def spread_table(table):
    heads = table.shape[0]
    grid = table.reshape(heads, TSPAN, SPAN, SPAN)
    cols = jnp.stack([grid[..., WIN_S - 1 - x : SPAN - x] for x in range(WIN_S)], axis=1)
    cols = cols.reshape(heads, WIN_S, TSPAN, SPAN * WIN_S)
    rows = jnp.stack(
        [cols[..., (WIN_S - 1 - y) * WIN_S : (SPAN - y) * WIN_S] for y in range(WIN_S)], axis=1
    )
    return rows.reshape(heads, CELL, TSPAN * CELL)


def window_rows(grid, groups):
    clips_here, frames, halves, rows, side, width = grid.shape
    periods = frames // WIN_T
    cells = grid.reshape(clips_here, periods, WIN_T, halves, rows, halves, WIN_S, width)
    cells = cells.transpose(0, 1, 3, 5, 2, 4, 6, 7)
    return cells.reshape(groups, -1, WIN_T, rows, WIN_S, width)


def window_back(pieces, shape):
    clips_here, frames, halves, rows, side, width = shape
    periods = frames // WIN_T
    cells = pieces.reshape(clips_here, periods, halves, halves, WIN_T, rows, WIN_S, width)
    return cells.transpose(0, 1, 4, 2, 5, 3, 6, 7).reshape(shape)


def to_windows(grid, groups):
    got = lax.all_to_all(
        window_rows(grid, groups), "win", split_axis=0, concat_axis=3, tiled=True
    )
    return got.reshape(-1, grid.shape[-1])


def from_windows(rows, per_dev, shape):
    out = lax.all_to_all(
        rows.reshape(1, per_dev, WIN_T, WIN_S, WIN_S, shape[-1]),
        "win",
        split_axis=3,
        concat_axis=0,
        tiled=True,
    )
    return window_back(out, shape)


def body(
    tokens,
    condition,
    frame_count,
    triple_weight,
    triple_bias,
    project_weight,
    project_bias,
    up_weight,
    up_bias,
    down_weight,
    down_bias,
    modulate_weight,
    modulate_bias,
    position_table,
    cotangent,
):
    width = tokens.shape[-1]
    n = lax.axis_size("clip")
    groups = lax.axis_size("win")
    halves = tokens.shape[2]
    per_time = tokens.shape[1] // WIN_T
    per_dev = per_time * halves * halves // groups
    count = per_dev * WINDOW
    ring = Ring(n)
    core = ring.core
    rows = width // n

    def half_of(shard):
        size = shard.shape[0] // CORES
        return lax.dynamic_slice_in_dim(shard, core * size, size, 0)

    x = to_windows(tokens, groups)
    sigma = jax.nn.sigmoid(condition)
    cond_in = (condition * sigma).astype(BF16)
    vectors = [cond_in[0], triple_bias, project_bias, up_bias, down_bias, modulate_bias]
    sizes = np.cumsum([0] + [v.shape[0] for v in vectors])
    small = ring.gather_small(jnp.concatenate(vectors)[None])
    cond_all, triple_b, project_b, up_b, down_b, modulate_b = (
        small[:, sizes[i] : sizes[i + 1]] for i in range(len(vectors))
    )
    flat = lambda v: v.reshape(1, -1).astype(F32)
    triple_b, project_b, up_b, down_b = map(flat, (triple_b, project_b, up_b, down_b))
    bias_all = jnp.concatenate(
        [triple_b[:, :width], jnp.zeros((1, width), F32), triple_b[:, width:]], axis=1
    )
    cond_rows = lax.dynamic_slice_in_dim(cond_all, ring.rank * rows, rows, 1)
    mod = ring.scatter_small(mm(cond_rows, modulate_weight)) + modulate_b.reshape(-1).astype(F32)
    mod = mod.reshape(6, width)

    first = jnp.concatenate([half_of(triple_weight), half_of(project_weight)], axis=1)
    own_a, sib_a = ring.gather(first, False)
    own_b, sib_b = ring.gather(half_of(up_weight), True)
    own_c, sib_c = ring.gather(half_of(down_weight), False)
    idx = ring.index()
    triple_w = Weight(triple_weight, own_a, sib_a)
    project_w = Weight(project_weight, own_a, sib_a, 3 * width)
    up_w = Weight(up_weight, own_b, sib_b)
    down_w = Weight(down_weight, own_c, sib_c)

    window_id = lax.axis_index("win") * per_dev + jnp.arange(per_dev)
    start = window_id // (halves * halves) * WIN_T
    valid = jnp.clip(frame_count[0] - start, 0, WIN_T).astype(jnp.int32)
    keep = (jnp.arange(WINDOW)[None] // CELL < valid[:, None]).astype(F32).reshape(count, 1)
    table, table_back = jax.vjp(spread_table, position_table)
    cot = to_windows(cotangent, groups)
    gate_two = mod[5:6]
    grad_ffn = (keep * cot.astype(F32) * gate_two).astype(BF16)
    down_bias_grad = jnp.sum(grad_ffn.astype(F32), axis=0)

    def turned(v):
        v = v.reshape(count, n, CORES, rows // CORES).transpose(2, 1, 3, 0)
        return v.reshape(CORES, width // CORES, count)

    norm_in, triple = qkv_project(idx, x, mod, triple_w, bias_all)
    mixed, logs = attend(valid, triple, table)
    attention, middle, norm_mid = attention_out(
        idx, mixed, x, mod, keep, project_w, project_b
    )
    activated, slope = gelu_up(idx, norm_mid, up_w, up_b)
    result, grad_gate_two = ffn_down(
        idx, activated, middle, cot, keep, gate_two, down_w, down_b
    )
    output = from_windows(result, per_dev, tokens.shape)

    turned_ffn = grad_ffn.T.reshape(CORES, width // CORES, count)
    inner = activated.shape[1]
    down_keep, down_send = outer_product(idx, turned_ffn, activated, 512)
    split_cols = lambda g: g.reshape(width // CORES, n, inner // n).transpose(1, 0, 2)
    down_parts = ring.scatter(split_cols(down_keep), split_cols(down_send), False)
    down_weight_grad = jnp.concatenate([p.T for p in down_parts], axis=1).astype(F32)

    grad_hidden, up_keep, up_send, up_bias_grad = hidden_back(
        idx, grad_ffn, slope, turned(norm_mid), down_w
    )
    split_rows = lambda g: g.reshape(n, rows // CORES, -1)
    up_parts = ring.scatter(split_rows(up_keep), split_rows(up_send), True)
    up_weight_grad = jnp.concatenate(up_parts, axis=0).astype(F32)

    grad_middle, grad_attention, grad_mixed, mid_sums = middle_back(
        idx, grad_hidden, middle, cot, attention, keep, mod, up_w, project_w
    )
    grad_shift_two, grad_scale_two, grad_gate_one, project_bias_grad = mid_sums
    project_keep, project_send = outer_product(idx, turned(mixed), grad_attention, 512)
    *grads, grad_table = attend_back(valid, triple, table, grad_mixed, logs)
    triple_keep, triple_send, triple_sums = triple_outer(idx, turned(norm_in), grads, 512)
    last_parts = ring.scatter(
        split_rows(jnp.concatenate([triple_keep, project_keep], axis=1)),
        split_rows(jnp.concatenate([triple_send, project_send], axis=1)),
        False,
    )
    last = jnp.concatenate(last_parts, axis=0).astype(F32)
    triple_weight_grad, project_weight_grad = last[:, : 3 * width], last[:, 3 * width :]
    grad_rows, in_sums = input_back(idx, grads, x, grad_middle, mod, triple_w)
    input_grad = from_windows(grad_rows, per_dev, tokens.shape)

    table_grad = table_back(grad_table)[0]
    triple_bias_grad = jnp.concatenate([triple_sums[0, :width], triple_sums[0, 2 * width :]])
    pieces = [
        table_grad.reshape(-1),
        triple_bias_grad,
        project_bias_grad,
        up_bias_grad[0],
        down_bias_grad,
    ]
    ends = np.cumsum([0] + [p.shape[0] for p in pieces])
    pad = -int(ends[-1]) % 1024
    packed = jnp.concatenate(pieces + [jnp.zeros((pad,), F32)]).reshape(-1, 128)
    packed = ring.sum_all(packed).reshape(-1)
    table_grad, *bias_grads = (packed[ends[i] : ends[i + 1]] for i in range(len(pieces)))
    table_grad = table_grad.reshape(position_table.shape)
    bias_grads = [
        lax.dynamic_slice_in_dim(g, ring.rank * (g.shape[0] // n), g.shape[0] // n)
        for g in bias_grads
    ]
    grad_mod = jnp.concatenate(
        [
            in_sums[0],
            in_sums[1],
            grad_gate_one,
            grad_shift_two,
            grad_scale_two,
            grad_gate_two[0],
        ]
    )
    grad_mod = ring.sum_win(grad_mod[None]).astype(BF16)
    grad_mod = ring.gather_small(grad_mod)
    modulate_weight_grad = mm(cond_rows, grad_mod, TN)
    modulate_bias_grad = lax.dynamic_slice_in_dim(
        jnp.sum(grad_mod.astype(F32), axis=0), ring.rank * (6 * rows), 6 * rows
    )
    back = ring.gather_small(mm(grad_mod, modulate_weight, NT)[None])
    back = lax.dynamic_index_in_dim(back, ring.rank, 1, keepdims=False).reshape(1, width)
    condition_grad = back * (sigma * (1.0 + condition * (1.0 - sigma)))
    triple_bias_grad, project_bias_grad, up_bias_grad, down_bias_grad = bias_grads
    return (
        output,
        input_grad,
        condition_grad,
        triple_weight_grad,
        triple_bias_grad,
        project_weight_grad,
        project_bias_grad,
        up_weight_grad,
        up_bias_grad,
        down_weight_grad,
        down_bias_grad,
        modulate_weight_grad,
        modulate_bias_grad,
        table_grad,
    )


def solution(mesh):
    grid = P("clip", None, None, "win", None, None)
    matrix, vector = P("clip", None), P("clip")
    placed = (
        grid,
        matrix,
        vector,
        matrix,
        vector,
        matrix,
        vector,
        matrix,
        vector,
        matrix,
        vector,
        matrix,
        vector,
        P(),
        grid,
    )
    return jax.shard_map(
        body,
        mesh=mesh,
        in_specs=placed,
        out_specs=(grid, grid, *placed[1:2], *placed[3:14]),
        check_vma=False,
    )
```

time: 1850 us -> 695 us (0.38)
  other arithmetic: 638 us -> 53.2 us
  local copies, waits for them, and re-layouts: 489 us -> 146 us
  waiting for transfers between devices: 332 us -> 135 us
  Pallas kernels: 0 us -> 187 us
  matrix products: 182 us -> 3.77 us
  blocking collectives: 145 us -> 0 us
  starting transfers between devices: 38.3 us -> 128 us
    scatter-add x1 -> x0, other arithmetic: 543 us -> none  [build_bias(): return jnp.take(table, offset_index(), axis=1)]
    gather x2 -> x0, local copies, waits for them, and re-layouts: 371 us -> none  [build_bias(): return jnp.take(table, offset_index(), axis=1)]
    reduce_scatter x5 -> x0, waiting for transfers between devices: 205 us -> none  [the longest x1 205 us: body(): lax.psum_scatter(modulate_weight_full.astype(jnp.bfloat16), 'clip', scatt...]
    pallas_call x0 -> x12, Pallas kernels: none -> 187 us  [kernel_call(): pl.pallas_call(body, grid_spec=pltpu.PrefetchScalarGridSpec(num_scalar_pr...]
    dot_general x20 -> x3, matrix products: 182 us -> 3.77 us  [mm(): return lax.dot_general(a, b, dims, preferred_element_type=F32)]
    ppermute x0 -> x91, waiting for transfers between devices: none -> 125 us  [the longest x11 84.2 us: scatter(): a = lax.ppermute(a, 'clip', self.up)]
    ppermute x0 -> x91, starting transfers between devices: none -> 108 us  [the longest x21 33.1 us: gather(): return (own, [lax.ppermute(o, 'win', self.swap) for o in own])]
    psum x2 -> x0, waiting for transfers between devices: 103 us -> none  [the longest x1 65.1 us: body(): lax.psum(triple_weight_grad.astype(jnp.bfloat16), 'win').astype(jnp.float32)]
  transfers between devices with their start and end apart: 16 -> 95, of which waited for: 5 -> 25; matrix products, arithmetic and copies ran while one was open for 69% -> 28% of each run, Pallas kernels for 0% -> 14%
where the time goes in v1:
time: 695 us; the launch traced here: 683 us
  Pallas kernels  187 us (27%)
  local copies, waits for them, and re-layouts  146 us (21%)
  waiting for transfers between devices  135 us (19%)
  starting transfers between devices  128 us (18%)
  other arithmetic  53.2 us (8%)
  between operations  29.2 us (4%)
    pallas_call x12, Pallas kernels, kernel_call(): pl.pallas_call(body, grid_spec=pltpu.PrefetchScalarGridSpec(num_scalar_pr...  187 us
    ppermute x11, waiting for transfers between devices, scatter(): a = lax.ppermute(a, 'clip', self.up)  84.2 us
    ppermute x21, starting transfers between devices, gather(): return (own, [lax.ppermute(o, 'win', self.swap) for o in own])  33.1 us
    slice x9, local copies, waits for them, and re-layouts, spread_table(): grid[..., WIN_S - 1 - x:SPAN - x]  22.3 us
    ppermute x11, waiting for transfers between devices, gather(): a = lax.ppermute(a, 'clip', self.up)  19 us
    another operation x10, local copies, waits for them, and re-layouts, spread_table(): jnp.stack([grid[..., WIN_S - 1 - x:SPAN - x] for x in range(WIN_S)], axis=1)  17.9 us
    ppermute x9, starting transfers between devices, gather_small(): other = lax.ppermute(block, 'clip', perm)  14.3 us
  transfers between devices with their start and end apart: 95, of which 25 were waited for; matrix products, arithmetic and copies ran while one was open for 28% of the time, Pallas kernels for 14%

profile of v1, /device:TPU:1, one launch (start us, length us, event | category | flops | bytes accessed | tf_op | source)
XLA Modules:
  0.0 682.9 jit_solution(1189351629264904836)
XLA Ops:
  91.4 7.6 %collective-permute-start.19 = (bf16[64,4096]{1,0:T(8,128)(2,1)S(1)}, bf16[64,4096]{1,0:T(8,128)(2,1)S(1)}, u32[]{:S(2)}, u32[]{:S(2)}) collective-permute-start(bf16[64,4096]{1,0:T(8,128)(2,1)S(1)} %collective-permute-done.9.rest_7_.rest_22_), channel_id=1, source_target_pairs={{0,1},{1,0},{2,3},{3,2},{4,5},{5,4},{6,7},{7,6},{8,9},{9,8},{10,11... | collective-permute-start | bytes 1572872 | tf_op jit(solution)/shard_map/ppermute | solution.py:102
  131.1 7.3 %copy.232 = f32[16,8,8,9,64]{4,3,2,1,0:T(8,128)} copy(f32[16,8,8,9,64]{4,2,3,0,1:T(8,128)} %fusion.29) | data formatting | bytes 4718592 | tf_op jit(solution)/shard_map/jvp()/stack | solution.py:897
  161.7 7.6 %collective-permute-done.11.rest_5_.rest_20_ = bf16[64,4096]{1,0:T(8,128)(2,1)} collective-permute-done((bf16[64,4096]{1,0:T(8,128)(2,1)}, bf16[64,4096]{1,0:T(8,128)(2,1)}, u32[]{:S(2)}, u32[]{:S(2)}) %collective-permute-start.11) | collective-permute-done | bytes 524320 | tf_op jit(solution)/shard_map/ppermute | solution.py:96
  186.6 8.7 %collective-permute-done.12.rest_4_.rest_19_ = bf16[64,4096]{1,0:T(8,128)(2,1)} collective-permute-done((bf16[64,4096]{1,0:T(8,128)(2,1)}, bf16[64,4096]{1,0:T(8,128)(2,1)}, u32[]{:S(2)}, u32[]{:S(2)}) %collective-permute-start.12) | collective-permute-done | bytes 524320 | tf_op jit(solution)/shard_map/ppermute | solution.py:96
  212.4 13.9 %shard_map.272 = (bf16[640,1024]{1,0:T(8,128)(2,1)}, bf16[640,3072]{1,0:T(8,128)(2,1)}) custom-call(s32[9]{0:T(128)} %stack.61.idx, bf16[640,1024]{1,0:T(8,128)(2,1)} %bitcast.319, f32[6,1024]{1,0:T(8,128)} %add.582.mod_ref, f32[1,3072]{1,0:T(1,128)} %pad_maximum_fusion.3.bias_ref, bf16[128,3072]{1,0:T(8,128)(2,1)} %rest_0_.13, ...), custom_call_target="tpu_custom_call" | custom-call | flops 4026531840 | bytes 12845056 | tf_op jit(solution)/shard_map/pallas_call | solution.py:211
  226.3 18.5 %shard_map.273 = (bf16[640,1024]{1,0:T(8,128)(2,1)}, f32[2,8,2,320]{3,2,1,0:T(2,128)}) custom-call(s32[2]{0:T(128)} %copy-done.34, bf16[640,3072]{1,0:T(8,128)(2,1)} %get-tuple-element.46.q_ref.k_ref.v_ref, bf16[640,3072]{1,0:T(8,128)(2,1)} %get-tuple-element.46.q_ref.k_ref.v_ref, bf16[640,3072]{1,0:T(8,128)(2,1)} %get-tuple-element.46.q_ref.k_ref.v_ref, ...), custom_call_target="tpu_custom_call" | custom-call | flops 3355443200 | bytes 5242880 | tf_op jit(solution)/shard_map/pallas_call | solution.py:211
  246.7 10.3 %shard_map.274 = (bf16[640,1024]{1,0:T(8,128)(2,1)}, f32[640,1024]{1,0:T(8,128)}, bf16[640,1024]{1,0:T(8,128)(2,1)}) custom-call(s32[9]{0:T(128)} %stack.61.idx, bf16[640,1024]{1,0:T(8,128)(2,1)} %get-tuple-element.47.mixed_ref, bf16[640,1024]{1,0:T(8,128)(2,1)} %bitcast.320, f32[6,1024]{1,0:T(8,128)} %add.582.mod_ref, f32[640,1]{1,0:T(8,128)} %reshape.494.keep_ref, ...), custom_call_target="tpu_custom_call" | custom-call | flops 1342177280 | bytes 9961472 | tf_op jit(solution)/shard_map/pallas_call | solution.py:211
  261.5 21.8 %shard_map.275 = (bf16[640,4096]{1,0:T(8,128)(2,1)}, bf16[640,4096]{1,0:T(8,128)(2,1)}) custom-call(s32[9]{0:T(128)} %stack.61.idx, bf16[640,1024]{1,0:T(8,128)(2,1)} %get-tuple-element.48.x_ref, f32[1,4096]{1,0:T(1,128)} %bitcast.372, bf16[128,4096]{1,0:T(8,128)(2,1)} %rest_0_.12, bf16[64,4096]{1,0:T(8,128)(2,1)} %collective-permute-done.20.rest_1_, ...), custom_call_target="tpu_custom_call" | custom-call | flops 5368709120 | bytes 20185088 | tf_op jit(solution)/shard_map/pallas_call | solution.py:211
  283.4 19.7 %shard_map.277 = (bf16[640,4096]{1,0:T(8,128)(2,1)}, bf16[512,4096]{1,0:T(8,128)(2,1)}, bf16[512,4096]{1,0:T(8,128)(2,1)}, f32[1,4096]{1,0:T(1,128)}) custom-call(s32[9]{0:T(128)} %stack.61.idx, bf16[640,1024]{1,0:T(8,128)(2,1)} %multiply_convert_fusion.1.g_ref, bf16[640,4096]{1,0:T(8,128)(2,1)} %get-tuple-element.52.slope_ref, ...), custom_call_target="tpu_custom_call" | custom-call | flops 21474836480 | bytes 28573696 | tf_op jit(solution)/shard_map/pallas_call | solution.py:211
  303.0 20.8 %shard_map.278 = (f32[640,1024]{1,0:T(8,128)}, bf16[640,1024]{1,0:T(8,128)(2,1)}, bf16[640,1024]{1,0:T(8,128)(2,1)}, f32[4,1024]{1,0:T(4,128)}) custom-call(s32[9]{0:T(128)} %stack.61.idx, bf16[640,4096]{1,0:T(8,128)(2,1)} %get-tuple-element.53.gh_ref, f32[640,1024]{1,0:T(8,128)} %get-tuple-element.50.mid_ref, bf16[640,1024]{1,0:T(8,128)(2,1)} %bitcast.317, ...), custom_call_target="tpu_custom_call" | custom-call | flops 6710886400 | bytes 26214400 | tf_op jit(solution)/shard_map/pallas_call | solution.py:211
  323.9 24.1 %shard_map.279 = (bf16[640,1024]{1,0:T(8,128)(2,1)}, bf16[640,1024]{1,0:T(8,128)(2,1)}, bf16[640,1024]{1,0:T(8,128)(2,1)}, f32[16,64,576]{2,1,0:T(8,128)}) custom-call(s32[2]{0:T(128)} %copy-done.34, bf16[640,3072]{1,0:T(8,128)(2,1)} %get-tuple-element.46.q_ref.k_ref.v_ref, bf16[640,3072]{1,0:T(8,128)(2,1)} %get-tuple-element.46.q_ref.k_ref.v_ref, ...), custom_call_target="tpu_custom_call" | custom-call | flops 8388608000 | bytes 10485760 | tf_op jit(solution)/shard_map/pallas_call | solution.py:211
  348.0 15.0 %shard_map.280 = (bf16[640,1024]{1,0:T(8,128)(2,1)}, f32[2,1024]{1,0:T(2,128)}) custom-call(s32[9]{0:T(128)} %stack.61.idx, bf16[640,1024]{1,0:T(8,128)(2,1)} %get-tuple-element.57.dq_ref.q_ref, bf16[640,1024]{1,0:T(8,128)(2,1)} %get-tuple-element.58.dk_ref.k_ref, bf16[640,1024]{1,0:T(8,128)(2,1)} %get-tuple-element.59.dv_ref.v_ref, ...), custom_call_target="tpu_custom_call" | custom-call | flops 4026531840 | bytes 18087936 | tf_op jit(solution)/shard_map/pallas_call | solution.py:211
  363.8 15.2 %shard_map.276 = (bf16[640,1024]{1,0:T(8,128)(2,1)}, f32[1,1024]{1,0:T(1,128)}) custom-call(s32[9]{0:T(128)} %stack.61.idx, bf16[640,4096]{1,0:T(8,128)(2,1)} %get-tuple-element.49.act_ref.right_ref, f32[640,1024]{1,0:T(8,128)} %get-tuple-element.50.mid_ref, bf16[640,1024]{1,0:T(8,128)(2,1)} %bitcast.318, f32[640,1]{1,0:T(8,128)} %reshape.494.keep_ref, ...), custom_call_target="tpu_custom_call" | custom-call | flops 5368709120 | bytes 18874368 | tf_op jit(solution)/shard_map/pallas_call | solution.py:211
  379.8 12.0 %shard_map.283 = (bf16[512,4096]{1,0:T(8,128)(2,1)}, bf16[512,4096]{1,0:T(8,128)(2,1)}) custom-call(s32[9]{0:T(128)} %stack.61.idx, bf16[2,512,640]{2,1,0:T(8,128)(2,1)} %bitcast.353, bf16[2,512,640]{2,1,0:T(8,128)(2,1)} %bitcast.354, bf16[640,4096]{1,0:T(8,128)(2,1)} %get-tuple-element.49.act_ref.right_ref), custom_call_target="tpu_custom_call" | custom-call | flops 5368709120 | bytes 14942208 | tf_op jit(solution)/shard_map/pallas_call | solution.py:211
  401.7 10.8 %shard_map.281 = (bf16[512,3072]{1,0:T(8,128)(2,1)}, bf16[512,3072]{1,0:T(8,128)(2,1)}, f32[1,3072]{1,0:T(1,128)}) custom-call(s32[9]{0:T(128)} %stack.61.idx, bf16[2,512,640]{2,1,0:T(8,128)(2,1)} %bitcast.357, bf16[2,512,640]{2,1,0:T(8,128)(2,1)} %bitcast.358, bf16[640,1024]{1,0:T(8,128)(2,1)} %get-tuple-element.57.dq_ref.q_ref, ...), custom_call_target="tpu_custom_call" | custom-call | flops 4026531840 | bytes 11534336 | tf_op jit(solution)/shard_map/pallas_call | solution.py:211
  520.2 9.5 %all-to-all-done.2 = bf16[1,2,5,8,8,1024]{5,4,2,1,0,3:T(8,128)(2,1)} async-done(((bf16[1,2,5,8,8,1024]{5,4,2,1,0,3:T(8,128)(2,1)}), bf16[1,2,5,8,8,1024]{5,4,2,1,0,3:T(8,128)(2,1)}, u32[]{:S(2)}, u32[]{:S(2)}) %all-to-all-start.2) | async-done | bytes 1310752 | tf_op jit(solution)/shard_map/all_to_all | solution.py:926
  549.9 8.4 %collective-permute-done.57 = bf16[64,4096]{1,0:T(8,128)(2,1)S(1)} collective-permute-done((bf16[64,4096]{1,0:T(8,128)(2,1)S(1)}, bf16[64,4096]{1,0:T(8,128)(2,1)S(1)}, u32[]{:S(2)}, u32[]{:S(2)}) %collective-permute-start.57) | collective-permute-done | bytes 524320 | tf_op jit(solution)/shard_map/ppermute | solution.py:116
  562.3 18.5 %collective-permute-done.83 = bf16[512,512]{0,1:T(8,128)(2,1)S(1)} collective-permute-done((bf16[512,512]{0,1:T(8,128)(2,1)S(1)}, bf16[512,512]{0,1:T(8,128)(2,1)S(1)}, u32[]{:S(2)}, u32[]{:S(2)}) %collective-permute-start.83) | collective-permute-done | bytes 524320 | tf_op jit(solution)/shard_map/ppermute | solution.py:116
  606.4 8.1 %collective-permute-done.59 = bf16[64,4096]{1,0:T(8,128)(2,1)S(1)} collective-permute-done((bf16[64,4096]{1,0:T(8,128)(2,1)S(1)}, bf16[64,4096]{1,0:T(8,128)(2,1)S(1)}, u32[]{:S(2)}, u32[]{:S(2)}) %collective-permute-start.59) | collective-permute-done | bytes 524320 | tf_op jit(solution)/shard_map/ppermute | solution.py:116
  618.0 7.7 %collective-permute-done.73 = bf16[64,4096]{1,0:T(8,128)(2,1)S(1)} collective-permute-done((bf16[64,4096]{1,0:T(8,128)(2,1)S(1)}, bf16[64,4096]{1,0:T(8,128)(2,1)S(1)}, u32[]{:S(2)}, u32[]{:S(2)}) %collective-permute-start.73) | collective-permute-done | bytes 524320 | tf_op jit(solution)/shard_map/ppermute | solution.py:116
  628.9 8.0 %collective-permute-done.85 = bf16[512,512]{0,1:T(8,128)(2,1)S(1)} collective-permute-done((bf16[512,512]{0,1:T(8,128)(2,1)S(1)}, bf16[512,512]{0,1:T(8,128)(2,1)S(1)}, u32[]{:S(2)}, u32[]{:S(2)}) %collective-permute-start.85) | collective-permute-done | bytes 524320 | tf_op jit(solution)/shard_map/ppermute | solution.py:116
  640.3 7.8 %collective-permute-done.60 = bf16[64,4096]{1,0:T(8,128)(2,1)S(1)} collective-permute-done((bf16[64,4096]{1,0:T(8,128)(2,1)S(1)}, bf16[64,4096]{1,0:T(8,128)(2,1)S(1)}, u32[]{:S(2)}, u32[]{:S(2)}) %collective-permute-start.60) | collective-permute-done | bytes 524320 | tf_op jit(solution)/shard_map/ppermute | solution.py:116
  650.2 9.2 %collective-permute-done.74 = bf16[64,4096]{1,0:T(8,128)(2,1)S(1)} collective-permute-done((bf16[64,4096]{1,0:T(8,128)(2,1)S(1)}, bf16[64,4096]{1,0:T(8,128)(2,1)S(1)}, u32[]{:S(2)}, u32[]{:S(2)}) %collective-permute-start.74) | collective-permute-done | bytes 524320 | tf_op jit(solution)/shard_map/ppermute | solution.py:116
  666.8 7.1 %collective-permute-done.79 = bf16[64,4096]{1,0:T(8,128)(2,1)S(1)} collective-permute-done((bf16[64,4096]{1,0:T(8,128)(2,1)S(1)}, bf16[64,4096]{1,0:T(8,128)(2,1)S(1)}, u32[]{:S(2)}, u32[]{:S(2)}) %collective-permute-start.79) | collective-permute-done | bytes 524320 | tf_op jit(solution)/shard_map/ppermute | solution.py:125
  (434 shorter events, 356.2 us)
Async XLA Ops:
  3.7 75.2 %collective-permute-start.9 = (bf16[64,4096]{1,0:T(8,128)(2,1)}, bf16[64,4096]{1,0:T(8,128)(2,1)S(1)}, u32[]{:S(2)}, u32[]{:S(2)}) collective-permute-start(bf16[64,4096]{1,0:T(8,128)(2,1)} %pad_maximum_fusion.2), channel_id=1, source_target_pairs={{4,12},{12,20},{20,28},{28,24},{24,16},{16,8},{8,0},{0,4},{5,13},{... | collective-permute-start | bytes 1572872 | tf_op jit(solution)/shard_map/ppermute | solution.py:96
  5.8 74.4 %collective-permute-start.6 = (bf16[64,4096]{1,0:T(8,128)(2,1)}, bf16[64,4096]{1,0:T(8,128)(2,1)}, u32[]{:S(2)}, u32[]{:S(2)}) collective-permute-start(bf16[64,4096]{1,0:T(8,128)(2,1)} %pad_maximum_fusion.2), channel_id=1, source_target_pairs={{12,4},{20,12},{28,20},{24,28},{16,24},{8,16},{0,8},{4,0},{13,5},{... | collective-permute-start | bytes 1572872 | tf_op jit(solution)/shard_map/ppermute | solution.py:99
  7.7 75.5 %collective-permute-start.20 = (bf16[64,4096]{1,0:T(8,128)(2,1)}, bf16[64,4096]{1,0:T(8,128)(2,1)}, u32[]{:S(2)}, u32[]{:S(2)}) collective-permute-start(bf16[64,4096]{1,0:T(8,128)(2,1)} %constant_dynamic-slice_fusion.1), channel_id=1, source_target_pairs={{12,4},{20,12},{28,20},{24,28},{16,24},{8,16},{0,8},{4,0},{13,5},{... | collective-permute-start | bytes 1572872 | tf_op jit(solution)/shard_map/ppermute | solution.py:99
  9.1 75.5 %collective-permute-start.24 = (bf16[64,4096]{1,0:T(8,128)(2,1)}, bf16[64,4096]{1,0:T(8,128)(2,1)}, u32[]{:S(2)}, u32[]{:S(2)}) collective-permute-start(bf16[64,4096]{1,0:T(8,128)(2,1)} %constant_dynamic-slice_fusion.1), channel_id=1, source_target_pairs={{4,12},{12,20},{20,28},{28,24},{24,16},{16,8},{8,0},{0,4},{5,13},{... | collective-permute-start | bytes 1572872 | tf_op jit(solution)/shard_map/ppermute | solution.py:96
  11.3 49.2 %collective-permute-start = (bf16[1,2816]{1,0:T(2,128)(2,1)}, bf16[1,2816]{1,0:T(2,128)(2,1)}, u32[]{:S(2)}, u32[]{:S(2)}) collective-permute-start(bf16[1,2816]{1,0:T(2,128)(2,1)} %broadcast_in_dim.17), channel_id=1, source_target_pairs={{0,4},{4,0},{8,12},{12,8},{16,20},{20,16},{24,28},{28,24},{1,5},{5... | collective-permute-start | bytes 16904 | tf_op jit(solution)/shard_map/ppermute | solution.py:134
  13.9 144.1 %all-to-all-start = ((bf16[4,2,5,2,8,1024]{5,4,3,2,1,0:T(8,128)(2,1)}), bf16[4,2,5,2,8,1024]{5,4,3,2,1,0:T(8,128)(2,1)}, u32[]{:S(2)}, u32[]{:S(2)}) async-start(bf16[4,2,5,2,8,1024]{5,4,3,2,1,0:T(8,128)(2,1)} %bitcast.5), calls=%async_computation | async-start | bytes 2621440 | tf_op jit(solution)/shard_map/all_to_all | solution.py:919
  102.7 51.7 %collective-permute-start.27 = (bf16[64,4096]{1,0:T(8,128)(2,1)}, bf16[64,4096]{1,0:T(8,128)(2,1)S(1)}, u32[]{:S(2)}, u32[]{:S(2)}) collective-permute-start(bf16[64,4096]{1,0:T(8,128)(2,1)} %collective-permute-done.20.rest_1_), channel_id=1, source_target_pairs={{0,1},{1,0},{2,3},{3,2},{4,5},{5,4},{6,7},{7,6},{8,9},{9,8},{10,11... | collective-permute-start | bytes 1572872 | tf_op jit(solution)/shard_map/ppermute | solution.py:102
  108.3 46.5 %collective-permute-start.33 = (bf16[64,4096]{1,0:T(8,128)(2,1)}, bf16[64,4096]{1,0:T(8,128)(2,1)}, u32[]{:S(2)}, u32[]{:S(2)}) collective-permute-start(bf16[64,4096]{1,0:T(8,128)(2,1)} %collective-permute-done.24.rest_7_), channel_id=1, source_target_pairs={{0,1},{1,0},{2,3},{3,2},{4,5},{5,4},{6,7},{7,6},{8,9},{9,8},{10,11... | collective-permute-start | bytes 1572872 | tf_op jit(solution)/shard_map/ppermute | solution.py:102
  109.3 46.3 %collective-permute-start.35 = (bf16[256,1024]{1,0:T(8,128)(2,1)}, bf16[256,1024]{1,0:T(8,128)(2,1)}, u32[]{:S(2)}, u32[]{:S(2)}) collective-permute-start(bf16[256,1024]{1,0:T(8,128)(2,1)} %collective-permute-done.34.rest_1_), channel_id=1, source_target_pairs={{12,4},{20,12},{28,20},{24,28},{16,24},{8,16},{0,8},{4,0},{13,5},{... | collective-permute-start | bytes 1572872 | tf_op jit(solution)/shard_map/ppermute | solution.py:99
  113.3 43.5 %collective-permute-start.41 = (bf16[256,1024]{1,0:T(8,128)(2,1)}, bf16[256,1024]{1,0:T(8,128)(2,1)}, u32[]{:S(2)}, u32[]{:S(2)}) collective-permute-start(bf16[256,1024]{1,0:T(8,128)(2,1)} %collective-permute-done.34.rest_1_), channel_id=1, source_target_pairs={{0,1},{1,0},{2,3},{3,2},{4,5},{5,4},{6,7},{7,6},{8,9},{9,8},{10,11... | collective-permute-start | bytes 1572872 | tf_op jit(solution)/shard_map/ppermute | solution.py:102
  118.9 36.1 %collective-permute-start.38 = (bf16[256,1024]{1,0:T(8,128)(2,1)}, bf16[256,1024]{1,0:T(8,128)(2,1)}, u32[]{:S(2)}, u32[]{:S(2)}) collective-permute-start(bf16[256,1024]{1,0:T(8,128)(2,1)} %collective-permute-done.37.rest_7_), channel_id=1, source_target_pairs={{4,12},{12,20},{20,28},{28,24},{24,16},{16,8},{8,0},{0,4},{5,13},{... | collective-permute-start | bytes 1572872 | tf_op jit(solution)/shard_map/ppermute | solution.py:96
  158.0 43.2 %all-to-all-start.1 = ((bf16[4,2,5,2,8,1024]{5,4,3,2,1,0:T(8,128)(2,1)}), bf16[4,2,5,2,8,1024]{5,4,3,2,1,0:T(8,128)(2,1)S(1)}, u32[]{:S(2)}, u32[]{:S(2)}) async-start(bf16[4,2,5,2,8,1024]{5,4,3,2,1,0:T(8,128)(2,1)} %bitcast.323), calls=%async_computation.1 | async-start | bytes 2621440 | tf_op jit(solution)/shard_map/all_to_all | solution.py:919
  209.4 35.4 %collective-permute-start.36 = (bf16[256,1024]{1,0:T(8,128)(2,1)}, bf16[256,1024]{1,0:T(8,128)(2,1)}, u32[]{:S(2)}, u32[]{:S(2)}) collective-permute-start(bf16[256,1024]{1,0:T(8,128)(2,1)} %collective-permute-done.35.rest_2_), channel_id=1, source_target_pairs={{12,4},{20,12},{28,20},{24,28},{16,24},{8,16},{0,8},{4,0},{13,5},{... | collective-permute-start | bytes 1572872 | tf_op jit(solution)/shard_map/ppermute | solution.py:99
  244.8 38.5 %collective-permute-start.42 = (bf16[256,1024]{1,0:T(8,128)(2,1)}, bf16[256,1024]{1,0:T(8,128)(2,1)}, u32[]{:S(2)}, u32[]{:S(2)}) collective-permute-start(bf16[256,1024]{1,0:T(8,128)(2,1)} %collective-permute-done.35.rest_2_), channel_id=1, source_target_pairs={{0,1},{1,0},{2,3},{3,2},{4,5},{5,4},{6,7},{7,6},{8,9},{9,8},{10,11... | collective-permute-start | bytes 1572872 | tf_op jit(solution)/shard_map/ppermute | solution.py:102
  244.9 38.4 %collective-permute-start.46 = (bf16[256,1024]{1,0:T(8,128)(2,1)}, bf16[256,1024]{1,0:T(8,128)(2,1)}, u32[]{:S(2)}, u32[]{:S(2)}) collective-permute-start(bf16[256,1024]{1,0:T(8,128)(2,1)} %collective-permute-done.38.rest_6_), channel_id=1, source_target_pairs={{0,1},{1,0},{2,3},{3,2},{4,5},{5,4},{6,7},{7,6},{8,9},{9,8},{10,11... | collective-permute-start | bytes 1572872 | tf_op jit(solution)/shard_map/ppermute | solution.py:102
  245.4 38.0 %collective-permute-start.45 = (bf16[256,1024]{1,0:T(8,128)(2,1)}, bf16[256,1024]{1,0:T(8,128)(2,1)}, u32[]{:S(2)}, u32[]{:S(2)}) collective-permute-start(bf16[256,1024]{1,0:T(8,128)(2,1)} %collective-permute-done.39.rest_5_), channel_id=1, source_target_pairs={{0,1},{1,0},{2,3},{3,2},{4,5},{5,4},{6,7},{7,6},{8,9},{9,8},{10,11... | collective-permute-start | bytes 1572872 | tf_op jit(solution)/shard_map/ppermute | solution.py:102
  245.5 37.9 %collective-permute-start.43 = (bf16[256,1024]{1,0:T(8,128)(2,1)}, bf16[256,1024]{1,0:T(8,128)(2,1)}, u32[]{:S(2)}, u32[]{:S(2)}) collective-permute-start(bf16[256,1024]{1,0:T(8,128)(2,1)} %collective-permute-done.36.rest_3_), channel_id=1, source_target_pairs={{0,1},{1,0},{2,3},{3,2},{4,5},{5,4},{6,7},{7,6},{8,9},{9,8},{10,11... | collective-permute-start | bytes 1572872 | tf_op jit(solution)/shard_map/ppermute | solution.py:102
  245.9 37.5 %collective-permute-start.44 = (bf16[256,1024]{1,0:T(8,128)(2,1)}, bf16[256,1024]{1,0:T(8,128)(2,1)}, u32[]{:S(2)}, u32[]{:S(2)}) collective-permute-start(bf16[256,1024]{1,0:T(8,128)(2,1)} %collective-permute-done.40.rest_4_), channel_id=1, source_target_pairs={{0,1},{1,0},{2,3},{3,2},{4,5},{5,4},{6,7},{7,6},{8,9},{9,8},{10,11... | collective-permute-start | bytes 1572872 | tf_op jit(solution)/shard_map/ppermute | solution.py:102
  379.7 58.4 %collective-permute-start.48 = (f32[1,6144]{1,0:T(1,128)S(1)}, f32[1,6144]{1,0:T(1,128)S(1)}, u32[]{:S(2)}, u32[]{:S(2)}) collective-permute-start(f32[1,6144]{1,0:T(1,128)S(1)} %bitcast.363), channel_id=1, source_target_pairs={{0,1},{1,0},{2,3},{3,2},{4,5},{5,4},{6,7},{7,6},{8,9},{9,8},{10,11... | collective-permute-start | bytes 73736 | tf_op jit(solution)/shard_map/ppermute | solution.py:151
  398.3 134.3 %collective-permute-start.81 = (bf16[8,512,512]{1,2,0:T(8,128)(2,1)}, bf16[8,512,512]{1,2,0:T(8,128)(2,1)}, u32[]{:S(2)}, u32[]{:S(2)}) collective-permute-start(bf16[8,512,512]{1,2,0:T(8,128)(2,1)} %bitcast.337), channel_id=1, source_target_pairs={{0,1},{1,0},{2,3},{3,2},{4,5},{5,4},{6,7},{7,6},{8,9},{9,8},{10,11... | collective-permute-start | bytes 12582920 | tf_op jit(solution)/shard_map/ppermute | solution.py:106
  398.7 140.1 %collective-permute-start.71 = (bf16[8,64,4096]{2,1,0:T(8,128)(2,1)}, bf16[8,64,4096]{2,1,0:T(8,128)(2,1)}, u32[]{:S(2)}, u32[]{:S(2)}) collective-permute-start(bf16[8,64,4096]{2,1,0:T(8,128)(2,1)} %bitcast.380), channel_id=1, source_target_pairs={{0,1},{1,0},{2,3},{3,2},{4,5},{5,4},{6,7},{7,6},{8,9},{9,8},{10,11... | collective-permute-start | bytes 12582920 | tf_op jit(solution)/shard_map/ppermute | solution.py:106
  422.5 113.2 %collective-permute-start.56 = (bf16[8,64,4096]{2,1,0:T(8,128)(2,1)}, bf16[8,64,4096]{2,1,0:T(8,128)(2,1)}, u32[]{:S(2)}, u32[]{:S(2)}) collective-permute-start(bf16[8,64,4096]{2,1,0:T(8,128)(2,1)} %bitcast.67), channel_id=1, source_target_pairs={{0,1},{1,0},{2,3},{3,2},{4,5},{5,4},{6,7},{7,6},{8,9},{9,8},{10,11... | collective-permute-start | bytes 12582920 | tf_op jit(solution)/shard_map/ppermute | solution.py:106
  540.7 54.3 %collective-permute-start.72 = (bf16[64,4096]{1,0:T(8,128)(2,1)S(1)}, bf16[64,4096]{1,0:T(8,128)(2,1)S(1)}, u32[]{:S(2)}, u32[]{:S(2)}) collective-permute-start(bf16[64,4096]{1,0:T(8,128)(2,1)S(1)} %get-tuple-element.92), channel_id=1, source_target_pairs={{4,12},{12,20},{20,28},{28,24},{24,16},{16,8},{8,0},{0,4},{5,13},{... | collective-permute-start | bytes 1572872 | tf_op jit(solution)/shard_map/ppermute | solution.py:116
  542.1 41.8 %collective-permute-start.61 = (bf16[64,4096]{1,0:T(8,128)(2,1)S(1)}, bf16[64,4096]{1,0:T(8,128)(2,1)S(1)}, u32[]{:S(2)}, u32[]{:S(2)}) collective-permute-start(bf16[64,4096]{1,0:T(8,128)(2,1)S(1)} %get-tuple-element.107), channel_id=1, source_target_pairs={{12,4},{20,12},{28,20},{24,28},{16,24},{8,16},{0,8},{4,0},{13,5},{... | collective-permute-start | bytes 1572872 | tf_op jit(solution)/shard_map/ppermute | solution.py:120
  (112 other events, 1849.0 us)

commit v2 on v1

--- a/solution.py
+++ b/solution.py
@@ -14,6 +14,7 @@
 SPAN = 2 * WIN_S - 1
 TSPAN = 2 * WIN_T - 1
 HEAD = 64
+LANES = 128
 CORES = 2
 EPS = 1e-06
 NEG = -30000.0
@@ -21,7 +22,7 @@
 GELU_A = 0.044715
 F32 = jnp.float32
 BF16 = jnp.bfloat16
-VMEM_LIMIT = 56 * 1024 * 1024
+VMEM_SPARE = 58 * 1024 * 1024
 
 NN = (((1,), (0,)), ((), ()))
 NT = (((1,), (1,)), ((), ()))
@@ -36,10 +37,16 @@
     return pl.BlockSpec(memory_space=pl.ANY)
 
 
-def params(grid_rank):
-    return pltpu.CompilerParams(
-        dimension_semantics=("arbitrary",) * grid_rank, vmem_limit_bytes=VMEM_LIMIT
-    )
+def vmem_need(specs, shapes, scratch):
+    total = VMEM_SPARE
+    for spec, shape in zip(specs, shapes):
+        if spec.block_shape is not None:
+            block = [b for b in spec.block_shape if b is not None]
+            total += 2 * math.prod(block) * max(shape.dtype.itemsize, 2)
+    for ref in scratch:
+        if ref.memory_space == pltpu.VMEM:
+            total += math.prod(ref.shape) * np.dtype(ref.dtype).itemsize
+    return total
 
 
 def ring_order(n):
@@ -54,108 +61,139 @@
     return walk + [z * ny for z in reversed(range(nz))]
 
 
+def after(value, *deps):
+    return together(value, *deps)[0]
+
+
+def together(*values):
+    flat, tree = jax.tree.flatten(values)
+    return jax.tree.unflatten(tree, lax.optimization_barrier(flat))
+
+
+def stage(groups, *values):
+    states = [(g.a, g.b) for g in groups]
+    states, values = together(states, values)
+    for g, (a, b) in zip(groups, states):
+        g.settle(a, b)
+    return values
+
+
 class Ring:
     def __init__(self, n):
         self.n = n
         order = ring_order(n)
-        place = [order.index(r) for r in range(n)]
-        self.order = jnp.asarray(np.array(order, np.int32))
-        self.place = jnp.asarray(np.array(place, np.int32))
         self.rank = lax.axis_index("clip")
-        self.pos = self.place[self.rank]
+        self.core = lax.axis_index("win") % CORES
         self.up = [(order[i], order[(i + 1) % n]) for i in range(n)]
         self.down = [(b, a) for a, b in self.up]
-        self.core = lax.axis_index("win") % CORES
+        rows = [
+            [order[(order.index(r) + k) % n] for k in range(n)] + [c]
+            for r in range(n)
+            for c in range(CORES)
+        ]
+        self.index = lax.dynamic_slice_in_dim(
+            jnp.asarray(np.array(rows, np.int32)), self.rank * CORES + self.core, 1, 0
+        ).reshape(n + 1)
         wins = lax.axis_size("win")
         self.swap = [(w, w ^ 1) for w in range(wins)]
-        self.across = [
-            [(w, w ^ k) for w in range(wins)] for k in (2 << i for i in range(8)) if k < wins
-        ]
-        self.pairs = [[(w, w ^ k) for w in range(wins)] for k in (1 << i for i in range(8)) if k < wins]
-        self.clip_pairs = [
-            (k, [(r, r ^ k) for r in range(n)]) for k in (1 << i for i in range(8)) if k < n
-        ]
-
-    def at(self, offset):
-        return self.order[(self.pos + offset) % self.n]
+        powers = [1 << i for i in range(8)]
+        self.pairs = [[(w, w ^ k) for w in range(wins)] for k in powers if k < wins]
+        self.across = self.pairs[1:]
 
     def steps(self, flip):
         far, near = self.n // 2, (self.n - 1) // 2
         return (near, far) if flip else (far, near)
 
-    def index(self):
-        ranks = [self.at(p) for p in range(self.n)]
-        return jnp.stack(ranks + [self.core]).astype(jnp.int32)
-
-    def gather(self, piece, flip):
-        far, near = self.steps(flip)
-        ahead, back = [], []
-        a = b = piece
-        for s in range(max(far, near)):
-            if s < far:
-                a = lax.ppermute(a, "clip", self.up)
-                ahead.append(a)
-            if s < near:
-                b = lax.ppermute(b, "clip", self.down)
-                back.append(b)
-        own = back + ahead[::-1]
-        return own, [lax.ppermute(o, "win", self.swap) for o in own]
-
-    def scatter(self, keep, send, flip):
-        far, near = self.steps(flip)
-        got = lax.ppermute(send, "win", self.swap)
-
-        def part(offset):
-            r = self.at(offset)
-            one = lambda arr: lax.dynamic_index_in_dim(arr, r, 0, keepdims=False).astype(F32)
-            return one(keep) + one(got)
-
-        a, b = part(far).astype(BF16), part(-near).astype(BF16)
-        for s in range(max(far, near)):
-            if s < far:
-                a = lax.ppermute(a, "clip", self.up)
-                if s < far - 1:
-                    a = (a.astype(F32) + part(far - 1 - s)).astype(BF16)
-            if s < near:
-                b = lax.ppermute(b, "clip", self.down)
-                if s < near - 1:
-                    b = (b.astype(F32) + part(1 + s - near)).astype(BF16)
-        total = (part(0) + a.astype(F32) + b.astype(F32)).astype(BF16)
-        for perm in self.across:
+    def gather_small(self, row):
+        return lax.all_to_all(jnp.broadcast_to(row[None], (self.n, *row.shape)), "clip", 0, 0)
+
+    def scatter_small(self, block):
+        return jnp.sum(lax.all_to_all(block, "clip", 0, 0, tiled=True), axis=0)
+
+    def sum_win(self, row):
+        wins = lax.axis_size("win")
+        return jnp.sum(
+            lax.all_to_all(jnp.broadcast_to(row[None], (wins, *row.shape)), "win", 0, 0), axis=0
+        )
+
+    def sum_all(self, rows):
+        both = ("clip", "win")
+        devices = self.n * lax.axis_size("win")
+        part = jnp.sum(lax.all_to_all(rows.reshape(devices, -1, LANES), both, 0, 0, tiled=True), axis=0)
+        whole = lax.all_to_all(jnp.broadcast_to(part[None], (devices, *part.shape)), both, 0, 0)
+        return whole.reshape(-1, LANES)
+
+
+class Gather:
+    def __init__(self, ring, piece, flip):
+        self.ring, self.ahead, self.back = ring, [], []
+        self.far, self.near = ring.steps(flip)
+        self.a = self.b = piece
+        self.swapped = {}
+
+    def step(self):
+        ring = self.ring
+        s = max(len(self.ahead), len(self.back))
+        if s < self.far:
+            self.a = lax.ppermute(self.a, "clip", ring.up)
+            self.ahead.append(self.a)
+        if s < self.near:
+            self.b = lax.ppermute(self.b, "clip", ring.down)
+            self.back.append(self.b)
+
+    def settle(self, a, b):
+        self.a, self.b = a, b
+        if self.ahead:
+            self.ahead[-1] = a
+        if self.back:
+            self.back[-1] = b
+
+    def pieces(self):
+        own = self.back + self.ahead[::-1]
+        return own, [lax.ppermute(o, "win", self.ring.swap) for o in own]
+
+
+class Scatter:
+    def __init__(self, ring, keep, got, flip):
+        self.ring, self.keep, self.got = ring, keep, got
+        self.far, self.near = ring.steps(flip)
+        self.a, self.b = self.part(self.far).astype(BF16), self.part(-self.near).astype(BF16)
+        self.s = 0
+
+    def part(self, k):
+        k = k % self.ring.n
+        return self.keep[k].astype(F32) + self.got[k].astype(F32)
+
+    def step(self):
+        s, far, near = self.s, self.far, self.near
+        if s < far:
+            if s > 0:
+                self.a = (self.a.astype(F32) + self.part(far - s)).astype(BF16)
+            self.a = lax.ppermute(self.a, "clip", self.ring.up)
+        if s < near:
+            if s > 0:
+                self.b = (self.b.astype(F32) + self.part(s - near)).astype(BF16)
+            self.b = lax.ppermute(self.b, "clip", self.ring.down)
+        self.s += 1
+
+    def settle(self, a, b):
+        self.a, self.b = a, b
+
+    def start_finish(self):
+        ring = self.ring
+        total = (self.part(0) + self.a.astype(F32) + self.b.astype(F32)).astype(BF16)
+        for perm in ring.across:
             other = lax.ppermute(total, "win", perm)
             total = (total.astype(F32) + other.astype(F32)).astype(BF16)
-        other = lax.ppermute(total, "win", self.swap)
-        first = jnp.where(self.core == 0, total, other)
-        second = jnp.where(self.core == 0, other, total)
+        return total
+
+    def finish(self, total):
+        ring = self.ring
+        other = lax.ppermute(total, "win", ring.swap)
+        total, other = lax.optimization_barrier((total, other))
+        first = jnp.where(ring.core == 0, total, other)
+        second = jnp.where(ring.core == 0, other, total)
         return first, second
-
-    def gather_small(self, block):
-        for k, perm in self.clip_pairs:
-            other = lax.ppermute(block, "clip", perm)
-            high = (self.rank & k) > 0
-            block = jnp.where(
-                high, jnp.concatenate([other, block]), jnp.concatenate([block, other])
-            )
-        return block
-
-    def scatter_small(self, block):
-        for k, perm in reversed(self.clip_pairs):
-            high = (self.rank & k) > 0
-            low_part, high_part = block[:k], block[k:]
-            other = lax.ppermute(jnp.where(high, low_part, high_part), "clip", perm)
-            block = jnp.where(high, high_part, low_part) + other
-        return block[0]
-
-    def sum_win(self, block):
-        for perm in self.pairs:
-            block = block + lax.ppermute(block, "win", perm)
-        return block
-
-    def sum_all(self, block):
-        block = self.sum_win(block)
-        for _, perm in self.clip_pairs:
-            block = block + lax.ppermute(block, "clip", perm)
-        return block
 
 
 class Weight:
@@ -207,7 +245,9 @@
         return copies
 
 
-def kernel_call(body, idx, grid, in_specs, out_specs, out_shape, scratch, operands, flops, nbytes):
+def kernel_call(
+    body, idx, grid, in_specs, out_specs, out_shape, scratch, operands, flops, nbytes, aliases=None
+):
     return pl.pallas_call(
         body,
         grid_spec=pltpu.PrefetchScalarGridSpec(
@@ -218,7 +258,13 @@
             scratch_shapes=scratch,
         ),
         out_shape=out_shape,
-        compiler_params=params(len(grid)),
+        input_output_aliases=aliases or {},
+        compiler_params=pltpu.CompilerParams(
+            dimension_semantics=("arbitrary",) * len(grid),
+            vmem_limit_bytes=VMEM_SPARE + 0 * vmem_need(
+                [*in_specs, *out_specs], [*operands, *out_shape], scratch
+            ),
+        ),
         cost_estimate=pl.CostEstimate(
             flops=int(flops), bytes_accessed=int(nbytes), transcendentals=0
         ),
@@ -238,6 +284,25 @@
 
 
 CHUNK = 64
+
+
+def pack_rows(condition, vectors):
+    lined = lambda v: jnp.pad(v, (0, -v.size % LANES)).reshape(-1, LANES)
+    operands = [condition.reshape(-1, LANES), *(lined(v) for v in vectors)]
+    ends = np.cumsum([0] + [v.shape[0] for v in operands])
+
+    def body(*refs):
+        out_ref = refs[-1]
+        for i, ref in enumerate(refs[:-1]):
+            v = ref[...].astype(F32)
+            if i == 0:
+                v = v / (1.0 + jnp.exp(-v))
+            out_ref[ends[i] : ends[i + 1], :] = v.astype(BF16).astype(F32)
+
+    rows = pl.pallas_call(
+        body, out_shape=jax.ShapeDtypeStruct((int(ends[-1]), LANES), F32)
+    )(*operands)
+    return rows, ends
 
 
 def qkv_project(idx, x, mod, weight, bias):
@@ -245,7 +310,7 @@
     cols = weight.cols
     block = 512
     steps = cols // block
-    rows = WINDOW
+    rows = tokens
     nw = tokens // rows
     nref = weight.n_sems()
 
@@ -304,6 +369,21 @@
     )
 
 
+def fill_table(near, rows):
+    for y in range(WIN_S):
+        for f in range(TSPAN):
+            at = f * LANES + (WIN_S - 1 - y) * WIN_S
+            rows[y * WIN_S : (y + 1) * WIN_S, f * CELL : (f + 1) * CELL] = near[:, at : at + CELL]
+
+
+def fold_table(rows, near):
+    near[...] = jnp.zeros_like(near)
+    for y in range(WIN_S):
+        for f in range(TSPAN):
+            at = f * LANES + (WIN_S - 1 - y) * WIN_S
+            near[:, at : at + CELL] += rows[y * WIN_S : (y + 1) * WIN_S, f * CELL : (f + 1) * CELL]
+
+
 def bias_rows(table):
     return jnp.concatenate(
         [table[:, (WIN_T - 1 - f) * CELL : (WIN_T - 1 - f) * CELL + WINDOW] for f in range(WIN_T)],
@@ -311,29 +391,38 @@
     )
 
 
-def attention_specs(pairs):
-    q = pl.BlockSpec((WINDOW, 2 * HEAD), lambda h, w, nv: (w, h))
-    k = pl.BlockSpec((WINDOW, 2 * HEAD), lambda h, w, nv: (w, pairs + h))
-    v = pl.BlockSpec((WINDOW, 2 * HEAD), lambda h, w, nv: (w, 2 * pairs + h))
-    t = pl.BlockSpec((2, CELL, TSPAN * CELL), lambda h, w, nv: (h, 0, 0))
+def attention_specs(pairs, lo=0):
+    q = pl.BlockSpec((WINDOW, 2 * HEAD), lambda h, w, nv: (w, lo + h))
+    k = pl.BlockSpec((WINDOW, 2 * HEAD), lambda h, w, nv: (w, pairs + lo + h))
+    v = pl.BlockSpec((WINDOW, 2 * HEAD), lambda h, w, nv: (w, 2 * pairs + lo + h))
+    t = pl.BlockSpec((2, WIN_S, TSPAN * LANES), lambda h, w, nv: (lo + h, 0, 0))
     return q, k, v, t
 
 
-def attend(valid, triple, table):
+def attend(valid, triple, table, part, parts, before=None):
     tokens = triple.shape[0]
     width = triple.shape[1] // 3
     nw = tokens // WINDOW
     pairs = width // (2 * HEAD)
-
-    def body(nv, q_ref, k_ref, v_ref, t_ref, o_ref, l_ref):
+    here = pairs // parts
+    lo = part * here
+
+    def body(nv, q_ref, k_ref, v_ref, t_ref, *rest):
+        o_ref, l_ref, rows = rest[-3:]
         w = pl.program_id(1)
         keep = lax.broadcasted_iota(jnp.int32, (WINDOW, 1), 0) < nv[w] * CELL
+
+        @pl.when(w == 0)
+        def _():
+            for a in range(2):
+                fill_table(t_ref.at[a], rows.at[a])
+
         outs = []
         for a in range(2):
             cols = slice(a * HEAD, (a + 1) * HEAD)
             q = q_ref[:, cols] * jnp.asarray(HEAD**-0.5, BF16)
             s = mm(k_ref[:, cols], q, NT)
-            s = jnp.where(keep, s + bias_rows(t_ref[a]), NEG)
+            s = jnp.where(keep, s + bias_rows(rows[a]), NEG)
             peak = jnp.max(s, axis=0, keepdims=True)
             e = jnp.exp(s - peak)
             total = jnp.sum(e, axis=0, keepdims=True)
@@ -342,24 +431,25 @@
             outs.append(mm(v_ref[:, cols], p, TN))
         o_ref[...] = jnp.concatenate(outs, axis=0).T.astype(BF16)
 
-    q, k, v, t = attention_specs(pairs)
+    kept = list(before) if before else []
     return kernel_call(
         body,
         valid,
-        (pairs, nw),
-        [q, k, v, t],
-        [
-            pl.BlockSpec((WINDOW, 2 * HEAD), lambda h, w, nv: (w, h)),
-            pl.BlockSpec((1, 1, 2, WINDOW), lambda h, w, nv: (w, h, 0, 0)),
+        (here, nw),
+        [*attention_specs(pairs, lo), *[any_spec()] * len(kept)],
+        [
+            pl.BlockSpec((WINDOW, 2 * HEAD), lambda h, w, nv: (w, lo + h)),
+            pl.BlockSpec((1, 1, 2, WINDOW), lambda h, w, nv: (w, lo + h, 0, 0)),
         ],
         [
             jax.ShapeDtypeStruct((tokens, width), BF16),
             jax.ShapeDtypeStruct((nw, pairs, 2, WINDOW), F32),
         ],
-        [],
-        [triple, triple, triple, table],
-        4 * tokens * WINDOW * width * 4,
-        2 * tokens * 4 * width,
+        [pltpu.VMEM((2, CELL, TSPAN * CELL), F32)],
+        [triple, triple, triple, table, *kept],
+        4 * tokens * WINDOW * width * 4 // parts,
+        2 * tokens * 4 * width // parts,
+        {5 + i: i for i in range(len(kept))},
     )
 
 
@@ -369,21 +459,25 @@
     nw = tokens // WINDOW
     pairs = width // (2 * HEAD)
 
-    def body(nv, q_ref, k_ref, v_ref, t_ref, g_ref, l_ref, dq_ref, dk_ref, dv_ref, dt_ref):
+    def body(
+        nv, q_ref, k_ref, v_ref, t_ref, g_ref, l_ref, dq_ref, dk_ref, dv_ref, dt_ref, rows, drows
+    ):
         w = pl.program_id(1)
         keep = lax.broadcasted_iota(jnp.int32, (WINDOW, 1), 0) < nv[w] * CELL
         dqs, dks, dvs = [], [], []
 
         @pl.when(w == 0)
         def _():
-            dt_ref[...] = jnp.zeros_like(dt_ref)
+            for a in range(2):
+                fill_table(t_ref.at[a], rows.at[a])
+            drows[...] = jnp.zeros_like(drows)
 
         for a in range(2):
             cols = slice(a * HEAD, (a + 1) * HEAD)
             q = q_ref[:, cols] * jnp.asarray(HEAD**-0.5, BF16)
             k, g = k_ref[:, cols], g_ref[:, cols]
             s = mm(k, q, NT)
-            s = jnp.where(keep, s + bias_rows(t_ref[a]), NEG)
+            s = jnp.where(keep, s + bias_rows(rows[a]), NEG)
             p = jnp.exp(s - l_ref[0, 0, a : a + 1, :])
             gp = mm(v_ref[:, cols], g, NT)
             delta = jnp.sum(gp * p, axis=0, keepdims=True)
@@ -394,11 +488,16 @@
             wide = ds.astype(F32)
             for f in range(WIN_T):
                 at = (WIN_T - 1 - f) * CELL
-                dt_ref[a, :, at : at + WINDOW] += wide[f * CELL : (f + 1) * CELL, :]
+                drows[a, :, at : at + WINDOW] += wide[f * CELL : (f + 1) * CELL, :]
         scale = HEAD**-0.5
         dq_ref[...] = (jnp.concatenate(dqs, axis=0) * scale).T.astype(BF16)
         dk_ref[...] = jnp.concatenate(dks, axis=1).astype(BF16)
         dv_ref[...] = jnp.concatenate(dvs, axis=1).astype(BF16)
+
+        @pl.when(w == nw - 1)
+        def _():
+            for a in range(2):
+                fold_table(drows.at[a], dt_ref.at[a])
 
     q, k, v, t = attention_specs(pairs)
     one = pl.BlockSpec((WINDOW, 2 * HEAD), lambda h, w, nv: (w, h))
@@ -409,8 +508,8 @@
         [q, k, v, t, one, pl.BlockSpec((1, 1, 2, WINDOW), lambda h, w, nv: (w, h, 0, 0))],
         [one, one, one, t],
         [jax.ShapeDtypeStruct((tokens, width), BF16)] * 3
-        + [jax.ShapeDtypeStruct((2 * pairs, CELL, TSPAN * CELL), F32)],
-        [],
+        + [jax.ShapeDtypeStruct((2 * pairs, WIN_S, TSPAN * LANES), F32)],
+        [pltpu.VMEM((2, CELL, TSPAN * CELL), F32)] * 2,
         [triple, triple, triple, table, grad, logs],
         10 * tokens * WINDOW * width * 4,
         2 * tokens * 8 * width,
@@ -478,35 +577,37 @@
     )
 
 
-def gelu_up(idx, norm_mid, weight, bias):
+def gelu_up(idx, norm_mid, weight, bias, part, parts, before=None):
     tokens, width = norm_mid.shape
     cols = weight.cols
     block = 512
-    steps = cols // block
-    rows = WINDOW
+    steps = cols // block // parts
+    lo = part * steps
+    kept = list(before) if before else []
+    rows = tokens
     nw = tokens // rows
     nref = weight.n_sems()
 
     def body(idx, x_ref, bias_ref, *rest):
-        w_refs, rest = rest[:nref], rest[nref:]
-        act_ref, slope_ref, w_buf, sems = rest
+        w_refs = rest[:nref]
+        act_ref, slope_ref, w_buf, sems = rest[-4:]
         j, w = pl.program_id(0), pl.program_id(1)
 
         @pl.when((j == 0) & (w == 0))
         def _():
             for s in range(steps):
-                for c in weight.whole(idx, w_refs, w_buf, sems.at[s], s * block, block):
+                for c in weight.whole(idx, w_refs, w_buf, sems.at[s], (lo + s) * block, block):
                     c.start()
 
         for s in range(steps):
 
             @pl.when((j == s) & (w == 0))
             def _():
-                for c in weight.whole(idx, w_refs, w_buf, sems.at[s], s * block, block):
+                for c in weight.whole(idx, w_refs, w_buf, sems.at[s], (lo + s) * block, block):
                     c.wait()
 
         a = x_ref[pl.ds(pl.multiple_of(w * rows, rows), rows), :]
-        b = w_buf[:, pl.ds(pl.multiple_of(j * block, block), block)]
+        b = w_buf[:, pl.ds(pl.multiple_of((lo + j) * block, block), block)]
         h = mm(a, b) + bias_ref[...]
         square = h * h
         inner = GELU_C * h * (1.0 + GELU_A * square)
@@ -522,15 +623,17 @@
         (steps, nw),
         [
             pl.BlockSpec((tokens, width), lambda j, w, idx: (0, 0)),
-            pl.BlockSpec((1, block), lambda j, w, idx: (0, j)),
+            pl.BlockSpec((1, block), lambda j, w, idx: (0, lo + j)),
             *weight.specs(),
-        ],
-        [pl.BlockSpec((rows, block), lambda j, w, idx: (w, j))] * 2,
+            *[any_spec()] * len(kept),
+        ],
+        [pl.BlockSpec((rows, block), lambda j, w, idx: (w, lo + j))] * 2,
         [jax.ShapeDtypeStruct((tokens, cols), BF16)] * 2,
         [pltpu.VMEM((width, cols), BF16), pltpu.SemaphoreType.DMA((steps, nref))],
-        [norm_mid, bias, *weight.operands()],
-        2 * tokens * width * cols,
-        2 * (tokens * (width + 2 * cols) + width * cols),
+        [norm_mid, bias, *weight.operands(), *kept],
+        2 * tokens * width * cols // parts,
+        2 * (tokens * (width + 2 * cols) + width * cols) // parts,
+        {3 + nref + i: i for i in range(len(kept))},
     )
 
 
@@ -539,7 +642,7 @@
     width = weight.cols
     block = 256
     steps = width // block
-    rows = WINDOW
+    rows = tokens
     nw = tokens // rows
     nref = weight.n_sems()
 
@@ -599,37 +702,47 @@
     )
 
 
-def outer_product(idx, left, right, block, sums=False):
+def walk_rows(idx, refs, bufs, n):
+    for ref, buf in zip(refs, bufs):
+        size = buf.shape[0] // n
+        for k in range(n):
+            rows = pl.ds(pl.multiple_of(idx[k] * size, size), size)
+            buf[k * size : (k + 1) * size, :] = ref[rows, :]
+
+
+def half_specs(half, tokens, n):
+    return [
+        pl.BlockSpec((None, half, tokens), lambda j, idx: (idx[n], 0, 0)),
+        pl.BlockSpec((None, half, tokens), lambda j, idx: (1 - idx[n], 0, 0)),
+    ]
+
+
+def down_outer(idx, left, right):
     _, half, tokens = left.shape
-    cols = right.shape[1]
-
-    def body(idx, mine_ref, other_ref, right_ref, keep_ref, send_ref, *sum_ref):
+    n = idx.shape[0] - 1
+    block = right.shape[1] // n
+
+    def body(idx, mine_ref, other_ref, right_ref, keep_ref, send_ref):
         b = right_ref[...]
         send_ref[...] = mm(other_ref[...], b).astype(BF16)
         keep_ref[...] = mm(mine_ref[...], b).astype(BF16)
-        if sums:
-            sum_ref[0][...] = jnp.sum(b.astype(F32), axis=0, keepdims=True)
-
-    n = idx.shape[0] - 1
-    out = pl.BlockSpec((half, block), lambda j, idx: (0, j))
-    shape = jax.ShapeDtypeStruct((half, cols), BF16)
-    extra = [pl.BlockSpec((1, block), lambda j, idx: (0, j))] if sums else []
-    extra_shape = [jax.ShapeDtypeStruct((1, cols), F32)] if sums else []
+
+    out = pl.BlockSpec((None, half, block), lambda j, idx: (j, 0, 0))
+    shape = jax.ShapeDtypeStruct((n, half, block), BF16)
     return kernel_call(
         body,
         idx,
-        (cols // block,),
-        [
-            pl.BlockSpec((None, half, tokens), lambda j, idx: (idx[n], 0, 0)),
-            pl.BlockSpec((None, half, tokens), lambda j, idx: (1 - idx[n], 0, 0)),
-            pl.BlockSpec((tokens, block), lambda j, idx: (0, j)),
-        ],
-        [out, out, *extra],
-        [shape, shape, *extra_shape],
+        (n,),
+        [
+            *half_specs(half, tokens, n),
+            pl.BlockSpec((tokens, block), lambda j, idx: (0, idx[j])),
+        ],
+        [out, out],
+        [shape, shape],
         [],
         [left, left, right],
-        4 * tokens * half * cols,
-        2 * (2 * half * tokens + tokens * cols + 2 * half * cols),
+        4 * tokens * half * block * n,
+        2 * (2 * half * tokens + tokens * block * n + 2 * half * block * n),
     )
 
 
@@ -639,11 +752,12 @@
     block = weight.rows
     steps = weight.count + 1
     half = norm_t.shape[1]
+    n = weight.count + 1
     nref = weight.n_sems()
 
     def body(idx, g_ref, slope_ref, mine_ref, other_ref, *rest):
         w_refs, rest = rest[:nref], rest[nref:]
-        gh_ref, keep_ref, send_ref, sum_ref, w_buf, sems = rest
+        gh_ref, keep_ref, send_ref, sum_ref, w_buf, mine, other, sems = rest
         j = pl.program_id(0)
 
         def copies(s):
@@ -654,6 +768,7 @@
             for s in range(steps):
                 for c in copies(s):
                     c.start()
+            walk_rows(idx, (mine_ref, other_ref), (mine, other), n)
 
         for s in range(steps):
 
@@ -666,10 +781,9 @@
         gh = (mm(g_ref[...], b, NT) * slope_ref[...].astype(F32)).astype(BF16)
         gh_ref[...] = gh
         sum_ref[...] = jnp.sum(gh.astype(F32), axis=0, keepdims=True)
-        send_ref[...] = mm(other_ref[...], gh).astype(BF16)
-        keep_ref[...] = mm(mine_ref[...], gh).astype(BF16)
-
-    n = weight.count + 1
+        send_ref[...] = mm(other[...], gh).astype(BF16)
+        keep_ref[...] = mm(mine[...], gh).astype(BF16)
+
     out = pl.BlockSpec((half, block), lambda j, idx: (0, idx[j]))
     return kernel_call(
         body,
@@ -678,8 +792,7 @@
         [
             pl.BlockSpec((tokens, width), lambda j, idx: (0, 0)),
             pl.BlockSpec((tokens, block), lambda j, idx: (0, idx[j])),
-            pl.BlockSpec((None, half, tokens), lambda j, idx: (idx[n], 0, 0)),
-            pl.BlockSpec((None, half, tokens), lambda j, idx: (1 - idx[n], 0, 0)),
+            *half_specs(half, tokens, n),
             *weight.specs(),
         ],
         [
@@ -694,7 +807,12 @@
             jax.ShapeDtypeStruct((half, inner), BF16),
             jax.ShapeDtypeStruct((1, inner), F32),
         ],
-        [pltpu.VMEM((inner, width), BF16), pltpu.SemaphoreType.DMA((nref,))],
+        [
+            pltpu.VMEM((inner, width), BF16),
+            pltpu.VMEM((half, tokens), BF16),
+            pltpu.VMEM((half, tokens), BF16),
+            pltpu.SemaphoreType.DMA((nref,)),
+        ],
         [grad_ffn, slope, norm_t, norm_t, *weight.operands()],
         8 * tokens * width * inner,
         2 * (tokens * (width + 2 * inner) + 2 * width * inner),
@@ -845,59 +963,83 @@
     )
 
 
-def triple_outer(idx, left, grads, block):
-    _, half, tokens = left.shape
-    width = grads[0].shape[1]
+def last_outer(idx, norm_t, mixed_t, grads, grad_attention, block, other):
+    _, half, tokens = norm_t.shape
+    width = grad_attention.shape[1]
     per = width // block
-
-    def body(idx, mine_ref, other_ref, q_ref, k_ref, v_ref, keep_ref, send_ref, sum_ref):
-        for part, ref in enumerate((q_ref, k_ref, v_ref)):
-
-            @pl.when(pl.program_id(0) // per == part)
+    n = idx.shape[0] - 1
+
+    def body(idx, *refs):
+        ins, rest = refs[:6], refs[6:]
+        out_ref, mine = rest[0], rest[-1]
+        j = pl.program_id(0)
+
+        @pl.when(j == 0)
+        def _():
+            walk_rows(idx, ins[0:1], (mine,), n)
+
+        @pl.when(j == 3 * per)
+        def _():
+            walk_rows(idx, ins[1:2], (mine,), n)
+
+        for part, ref in enumerate(ins[2:]):
+
+            @pl.when(j // per == part)
             def _():
                 b = ref[...]
-                send_ref[...] = mm(other_ref[...], b).astype(BF16)
-                keep_ref[...] = mm(mine_ref[...], b).astype(BF16)
-                sum_ref[...] = jnp.sum(b.astype(F32), axis=0, keepdims=True)
-
-    n = idx.shape[0] - 1
-    out = pl.BlockSpec((half, block), lambda j, idx: (0, j))
-    shape = jax.ShapeDtypeStruct((half, 3 * width), BF16)
+                out_ref[...] = mm(mine[...], b).astype(BF16)
+                if other:
+                    rest[1][...] = jnp.sum(b.astype(F32), axis=0, keepdims=True)
 
     def part_spec(part):
         return pl.BlockSpec(
             (tokens, block), lambda j, idx: (0, jnp.clip(j - part * per, 0, per - 1))
         )
 
+    left = half_specs(half, tokens, n)[1 if other else 0]
+    out_specs = [pl.BlockSpec((half, block), lambda j, idx: (0, j))]
+    out_shape = [jax.ShapeDtypeStruct((half, 4 * width), BF16)]
+    if other:
+        out_specs.append(pl.BlockSpec((1, block), lambda j, idx: (0, j)))
+        out_shape.append(jax.ShapeDtypeStruct((1, 4 * width), F32))
     return kernel_call(
         body,
         idx,
-        (3 * per,),
-        [
-            pl.BlockSpec((None, half, tokens), lambda j, idx: (idx[n], 0, 0)),
-            pl.BlockSpec((None, half, tokens), lambda j, idx: (1 - idx[n], 0, 0)),
-            part_spec(0),
-            part_spec(1),
-            part_spec(2),
-        ],
-        [out, out, pl.BlockSpec((1, block), lambda j, idx: (0, j))],
-        [shape, shape, jax.ShapeDtypeStruct((1, 3 * width), F32)],
-        [],
-        [left, left, *grads],
-        12 * tokens * half * width,
-        2 * (2 * half * tokens + 3 * tokens * width + 6 * half * width),
-    )
+        (4 * per,),
+        [left, left, *(part_spec(p) for p in range(4))],
+        out_specs,
+        out_shape,
+        [pltpu.VMEM((half, tokens), BF16)],
+        [norm_t, mixed_t, *grads, grad_attention],
+        8 * tokens * half * width,
+        2 * (2 * half * tokens + 4 * tokens * width + 4 * half * width),
+    )
+
+
+def column_pick():
+    pick = np.zeros((SPAN, SPAN, WIN_S, LANES // WIN_S, WIN_S), np.float32)
+    for b in range(SPAN):
+        for key in range(WIN_S):
+            for query in range(WIN_S):
+                pick[b, query - key + WIN_S - 1, key, b, query] = 1.0
+    return jnp.asarray(pick.reshape(SPAN * SPAN, WIN_S * LANES))
 
 
 def spread_table(table):
     heads = table.shape[0]
-    grid = table.reshape(heads, TSPAN, SPAN, SPAN)
-    cols = jnp.stack([grid[..., WIN_S - 1 - x : SPAN - x] for x in range(WIN_S)], axis=1)
-    cols = cols.reshape(heads, WIN_S, TSPAN, SPAN * WIN_S)
-    rows = jnp.stack(
-        [cols[..., (WIN_S - 1 - y) * WIN_S : (SPAN - y) * WIN_S] for y in range(WIN_S)], axis=1
-    )
-    return rows.reshape(heads, CELL, TSPAN * CELL)
+    wide = jnp.dot(
+        table.reshape(heads * TSPAN, SPAN * SPAN), column_pick(), precision=lax.Precision.HIGHEST
+    )
+    wide = wide.reshape(heads, TSPAN, WIN_S, LANES).transpose(0, 2, 1, 3)
+    return wide.reshape(heads, WIN_S, TSPAN * LANES)
+
+
+def gather_table(grad):
+    heads = grad.shape[0]
+    wide = grad.reshape(heads, WIN_S, TSPAN, LANES).transpose(0, 2, 1, 3)
+    wide = wide.reshape(heads * TSPAN, WIN_S * LANES)
+    table = lax.dot_general(wide, column_pick(), NT, precision=lax.Precision.HIGHEST)
+    return table.reshape(heads, TSPAN * SPAN * SPAN)
 
 
 def window_rows(grid, groups):
@@ -965,128 +1107,197 @@
         size = shard.shape[0] // CORES
         return lax.dynamic_slice_in_dim(shard, core * size, size, 0)
 
-    x = to_windows(tokens, groups)
+    def turned(v):
+        v = v.reshape(count, n, CORES, rows // CORES).transpose(2, 1, 3, 0)
+        return v.reshape(CORES, width // CORES, count)
+
+    flat = lambda v: v.reshape(1, -1).astype(F32)
+    split_rows = lambda g: g.reshape(n, rows // CORES, -1)
+    swap = lambda g: lax.ppermute(g, "win", ring.swap)
+    idx = ring.index
+    steps = max(ring.steps(False))
+    spare = lambda group, used: [group.step() for _ in range(used, steps)]
+
+    first = jnp.concatenate([half_of(triple_weight), half_of(project_weight)], axis=1)
+    group_a = Gather(ring, first, False)
+    group_b = Gather(ring, half_of(up_weight), True)
+    group_c = Gather(ring, half_of(down_weight), False)
+
     sigma = jax.nn.sigmoid(condition)
-    cond_in = (condition * sigma).astype(BF16)
-    vectors = [cond_in[0], triple_bias, project_bias, up_bias, down_bias, modulate_bias]
-    sizes = np.cumsum([0] + [v.shape[0] for v in vectors])
-    small = ring.gather_small(jnp.concatenate(vectors)[None])
+    group_a.step()
+    tokens_here, condition_here = after((tokens, condition), first)
+    vectors = [triple_bias, project_bias, up_bias, down_bias, modulate_bias]
+    packed, ends = pack_rows(condition_here, vectors)
+    small = ring.gather_small(packed.astype(BF16))
+    x = to_windows(tokens_here, groups)
     cond_all, triple_b, project_b, up_b, down_b, modulate_b = (
-        small[:, sizes[i] : sizes[i + 1]] for i in range(len(vectors))
-    )
-    flat = lambda v: v.reshape(1, -1).astype(F32)
+        small[:, ends[i] : ends[i + 1]].reshape(n, -1)[:, : v.size]
+        for i, v in enumerate([condition, *vectors])
+    )
     triple_b, project_b, up_b, down_b = map(flat, (triple_b, project_b, up_b, down_b))
     bias_all = jnp.concatenate(
         [triple_b[:, :width], jnp.zeros((1, width), F32), triple_b[:, width:]], axis=1
     )
     cond_rows = lax.dynamic_slice_in_dim(cond_all, ring.rank * rows, rows, 1)
     mod = ring.scatter_small(mm(cond_rows, modulate_weight)) + modulate_b.reshape(-1).astype(F32)
+    table = spread_table(position_table)
     mod = mod.reshape(6, width)
-
-    first = jnp.concatenate([half_of(triple_weight), half_of(project_weight)], axis=1)
-    own_a, sib_a = ring.gather(first, False)
-    own_b, sib_b = ring.gather(half_of(up_weight), True)
-    own_c, sib_c = ring.gather(half_of(down_weight), False)
-    idx = ring.index()
-    triple_w = Weight(triple_weight, own_a, sib_a)
-    project_w = Weight(project_weight, own_a, sib_a, 3 * width)
-    up_w = Weight(up_weight, own_b, sib_b)
-    down_w = Weight(down_weight, own_c, sib_c)
+    stage([group_a])
+    group_a.step()
+    mod, table = stage([group_a], mod, table)
 
     window_id = lax.axis_index("win") * per_dev + jnp.arange(per_dev)
     start = window_id // (halves * halves) * WIN_T
     valid = jnp.clip(frame_count[0] - start, 0, WIN_T).astype(jnp.int32)
     keep = (jnp.arange(WINDOW)[None] // CELL < valid[:, None]).astype(F32).reshape(count, 1)
-    table, table_back = jax.vjp(spread_table, position_table)
+    group_a.step()
+    x, bias_all = stage([group_a], x, bias_all)
+    spare(group_a, 3)
+    stage([group_a])
+    triple_w = Weight(triple_weight, *group_a.pieces())
+    project_w = Weight(project_weight, triple_w.own, triple_w.sib, 3 * width)
+
+    (group_b.a, group_b.b), idx, valid = together(
+        after((group_b.a, group_b.b), (group_a.a, group_a.b)), idx, valid
+    )
+    group_b.step()
+    norm_in, triple, cotangent = stage(
+        [group_b], *qkv_project(idx, x, mod, triple_w, bias_all), cotangent
+    )
+    group_b.step()
     cot = to_windows(cotangent, groups)
+    norm_t = turned(norm_in)
+    half_mixed = attend(valid, triple, table, 0, 2)
+    *half_mixed, norm_t = stage([group_b], *half_mixed, norm_t)
+    group_b.step()
     gate_two = mod[5:6]
     grad_ffn = (keep * cot.astype(F32) * gate_two).astype(BF16)
+    mixed, logs = attend(valid, triple, table, 1, 2, half_mixed)
+    mixed, logs, grad_ffn = stage([group_b], mixed, logs, grad_ffn)
+    spare(group_b, 3)
+    ffn_t = grad_ffn.T.reshape(CORES, width // CORES, count)
+    mixed_t = turned(mixed)
+    attention, middle, norm_mid, ffn_t, mixed_t = stage(
+        [group_b],
+        *attention_out(idx, mixed, x, mod, keep, project_w, project_b),
+        ffn_t,
+        mixed_t,
+    )
+    up_w = Weight(up_weight, *group_b.pieces())
+
+    group_c.a, group_c.b = after((group_c.a, group_c.b), (group_b.a, group_b.b))
+    group_c.step()
+    half_act = stage([group_c], *gelu_up(idx, norm_mid, up_w, up_b, 0, 2))
+    group_c.step()
+    mid_t = turned(norm_mid)
+    activated, slope, mid_t = stage(
+        [group_c], *gelu_up(idx, norm_mid, up_w, up_b, 1, 2, half_act), mid_t
+    )
+    group_c.step()
+    down_keep, down_send = stage([group_c], *down_outer(idx, ffn_t, activated))
+    down_got = swap(down_send)
+    spare(group_c, 3)
+    (down_got,) = stage([group_c], down_got)
+    down_w = Weight(down_weight, *group_c.pieces())
+
+    sums_d = Scatter(ring, down_keep, down_got, False)
+    grad_ffn, idx = stage([sums_d], after((grad_ffn, idx), (group_c.a, group_c.b)))[0]
+    sums_d.step()
     down_bias_grad = jnp.sum(grad_ffn.astype(F32), axis=0)
-
-    def turned(v):
-        v = v.reshape(count, n, CORES, rows // CORES).transpose(2, 1, 3, 0)
-        return v.reshape(CORES, width // CORES, count)
-
-    norm_in, triple = qkv_project(idx, x, mod, triple_w, bias_all)
-    mixed, logs = attend(valid, triple, table)
-    attention, middle, norm_mid = attention_out(
-        idx, mixed, x, mod, keep, project_w, project_b
-    )
-    activated, slope = gelu_up(idx, norm_mid, up_w, up_b)
-    result, grad_gate_two = ffn_down(
-        idx, activated, middle, cot, keep, gate_two, down_w, down_b
-    )
-    output = from_windows(result, per_dev, tokens.shape)
-
-    turned_ffn = grad_ffn.T.reshape(CORES, width // CORES, count)
-    inner = activated.shape[1]
-    down_keep, down_send = outer_product(idx, turned_ffn, activated, 512)
-    split_cols = lambda g: g.reshape(width // CORES, n, inner // n).transpose(1, 0, 2)
-    down_parts = ring.scatter(split_cols(down_keep), split_cols(down_send), False)
-    down_weight_grad = jnp.concatenate([p.T for p in down_parts], axis=1).astype(F32)
-
-    grad_hidden, up_keep, up_send, up_bias_grad = hidden_back(
-        idx, grad_ffn, slope, turned(norm_mid), down_w
-    )
-    split_rows = lambda g: g.reshape(n, rows // CORES, -1)
-    up_parts = ring.scatter(split_rows(up_keep), split_rows(up_send), True)
-    up_weight_grad = jnp.concatenate(up_parts, axis=0).astype(F32)
-
-    grad_middle, grad_attention, grad_mixed, mid_sums = middle_back(
-        idx, grad_hidden, middle, cot, attention, keep, mod, up_w, project_w
+    (grad_hidden, up_keep, up_send, up_bias_grad), idx = stage(
+        [sums_d], hidden_back(idx, grad_ffn, slope, mid_t, down_w), idx
+    )
+    sums_u = Scatter(ring, split_rows(up_keep), swap(split_rows(up_send)), True)
+    sums_d.step()
+    (grad_middle, grad_attention, grad_mixed, mid_sums), idx, valid = stage(
+        [sums_d, sums_u],
+        middle_back(
+            idx, grad_hidden, middle, cot, attention, keep, mod, up_w, project_w
+        ),
+        idx,
+        valid,
     )
     grad_shift_two, grad_scale_two, grad_gate_one, project_bias_grad = mid_sums
-    project_keep, project_send = outer_product(idx, turned(mixed), grad_attention, 512)
-    *grads, grad_table = attend_back(valid, triple, table, grad_mixed, logs)
-    triple_keep, triple_send, triple_sums = triple_outer(idx, turned(norm_in), grads, 512)
-    last_parts = ring.scatter(
-        split_rows(jnp.concatenate([triple_keep, project_keep], axis=1)),
-        split_rows(jnp.concatenate([triple_send, project_send], axis=1)),
-        False,
-    )
-    last = jnp.concatenate(last_parts, axis=0).astype(F32)
-    triple_weight_grad, project_weight_grad = last[:, : 3 * width], last[:, 3 * width :]
-    grad_rows, in_sums = input_back(idx, grads, x, grad_middle, mod, triple_w)
+    sums_d.step()
+    sums_u.step()
+    (*grads, grad_table), idx = stage(
+        [sums_d, sums_u], attend_back(valid, triple, table, grad_mixed, logs), idx
+    )
+    spare(sums_d, 3)
+    sums_u.step()
+    last = (norm_t, mixed_t, grads, grad_attention, 1024)
+    (last_send, last_sums), idx = together(last_outer(idx, *last, True), idx)
+    last_got = swap(split_rows(last_send))
+    table_grad = gather_table(grad_table)
+    last_keep, last_got, idx, table_grad = stage(
+        [sums_d, sums_u], last_outer(idx, *last, False)[0], last_got, idx, table_grad
+    )
+    sums_l = Scatter(ring, split_rows(last_keep), last_got, False)
+    sums_u.step()
+    sums_l.step()
+    (grad_rows, in_sums), idx, down_sum = stage(
+        [sums_u, sums_l],
+        input_back(idx, grads, x, grad_middle, mod, triple_w),
+        idx,
+        sums_d.start_finish(),
+    )
+    spare(sums_u, 3)
+    sums_l.step()
     input_grad = from_windows(grad_rows, per_dev, tokens.shape)
-
-    table_grad = table_back(grad_table)[0]
-    triple_bias_grad = jnp.concatenate([triple_sums[0, :width], triple_sums[0, 2 * width :]])
+    input_grad, (result, grad_gate_two), down_parts = stage(
+        [sums_l, sums_u],
+        input_grad,
+        ffn_down(idx, activated, middle, cot, keep, gate_two, down_w, down_b),
+        sums_d.finish(down_sum),
+    )
+
+    rows_of = lambda v: v.reshape(-1, LANES)
+    grad_mod = jnp.concatenate(
+        [in_sums, grad_gate_one[None], mid_sums[0:2], grad_gate_two], axis=0
+    )
+    here = jnp.arange(n)[:, None, None] == ring.rank
+    spans = position_table.shape[1]
+    wide = -(-spans // LANES) * LANES
     pieces = [
-        table_grad.reshape(-1),
-        triple_bias_grad,
-        project_bias_grad,
-        up_bias_grad[0],
-        down_bias_grad,
+        rows_of(jnp.pad(table_grad, ((0, 0), (0, wide - spans)))),
+        rows_of(last_sums[0, :width]),
+        rows_of(last_sums[0, 2 * width : 3 * width]),
+        rows_of(project_bias_grad),
+        rows_of(up_bias_grad[0]),
+        rows_of(down_bias_grad),
+        jnp.where(here, rows_of(grad_mod)[None], 0.0).reshape(-1, LANES),
     ]
     ends = np.cumsum([0] + [p.shape[0] for p in pieces])
-    pad = -int(ends[-1]) % 1024
-    packed = jnp.concatenate(pieces + [jnp.zeros((pad,), F32)]).reshape(-1, 128)
-    packed = ring.sum_all(packed).reshape(-1)
-    table_grad, *bias_grads = (packed[ends[i] : ends[i + 1]] for i in range(len(pieces)))
-    table_grad = table_grad.reshape(position_table.shape)
+    pad = -int(ends[-1]) % (n * groups * 8)
+    packed = jnp.concatenate(pieces + [jnp.zeros((pad, LANES), F32)])
+    sums_l.step()
+    packed = ring.sum_all(packed)
+    output = from_windows(result, per_dev, tokens.shape)
+    up_sum, packed, output = stage([sums_l], sums_u.start_finish(), packed, output)
+    spare(sums_l, 3)
+    up_parts = sums_u.finish(up_sum)
+
+    down_weight_grad = jnp.concatenate([p.T for p in down_parts], axis=1).astype(F32)
+    up_weight_grad = jnp.concatenate(up_parts, axis=0).astype(F32)
+    table_grad, *bias_grads, grad_mod = (packed[ends[i] : ends[i + 1]] for i in range(len(pieces)))
+    table_grad = table_grad.reshape(-1, wide)[:, :spans]
+    bias_grads = [jnp.concatenate(bias_grads[:2]), *bias_grads[2:]]
     bias_grads = [
-        lax.dynamic_slice_in_dim(g, ring.rank * (g.shape[0] // n), g.shape[0] // n)
+        lax.dynamic_slice_in_dim(g.reshape(-1), ring.rank * (g.size // n), g.size // n)
         for g in bias_grads
     ]
-    grad_mod = jnp.concatenate(
-        [
-            in_sums[0],
-            in_sums[1],
-            grad_gate_one,
-            grad_shift_two,
-            grad_scale_two,
-            grad_gate_two[0],
-        ]
-    )
-    grad_mod = ring.sum_win(grad_mod[None]).astype(BF16)
-    grad_mod = ring.gather_small(grad_mod)
+    grad_mod = grad_mod.reshape(n, -1).astype(BF16)
     modulate_weight_grad = mm(cond_rows, grad_mod, TN)
     modulate_bias_grad = lax.dynamic_slice_in_dim(
         jnp.sum(grad_mod.astype(F32), axis=0), ring.rank * (6 * rows), 6 * rows
     )
-    back = ring.gather_small(mm(grad_mod, modulate_weight, NT)[None])
-    back = lax.dynamic_index_in_dim(back, ring.rank, 1, keepdims=False).reshape(1, width)
-    condition_grad = back * (sigma * (1.0 + condition * (1.0 - sigma)))
+    back = lax.all_to_all(mm(grad_mod, modulate_weight, NT), "clip", 0, 0, tiled=True)
+    condition_grad = back.reshape(1, width) * (sigma * (1.0 + condition * (1.0 - sigma)))
+    halves_l = sums_l.finish(sums_l.start_finish())
+    triple_weight_grad, project_weight_grad = (
+        jnp.concatenate([h[:, cols] for h in halves_l], axis=0).astype(F32)
+        for cols in (slice(0, 3 * width), slice(3 * width, 4 * width))
+    )
     triple_bias_grad, project_bias_grad, up_bias_grad, down_bias_grad = bias_grads
     return (
         output,

time: 695 us -> 523 us (0.75)
  local copies, waits for them, and re-layouts: 146 us -> 66.4 us
  waiting for transfers between devices: 135 us -> 84.8 us
  starting transfers between devices: 128 us -> 99.1 us
  between operations: 29.2 us -> 2.74 us
  Pallas kernels: 187 us -> 194 us
    ppermute x91 -> x72, waiting for transfers between devices: 125 us -> 46.9 us  [the longest x11 20.4 us: step(): self.a = lax.ppermute(self.a, 'clip', ring.up)]
    ppermute x91 -> x72, starting transfers between devices: 108 us -> 54.9 us  [the longest x11 11.9 us: step(): self.a = lax.ppermute(self.a, 'clip', ring.up)]
    another operation x14 -> x0, local copies, waits for them, and re-layouts: 35.8 us -> none  [the longest x10 17.9 us: spread_table(): jnp.stack([grid[..., WIN_S - 1 - x:SPAN - x] for x in range(WIN_S)], axis=1)]
    slice x13 -> x7, local copies, waits for them, and re-layouts: 24.4 us -> 0.85 us  [the longest x1 0.76 us: body(): gate_two = mod[5:6]]
    all_to_all x0 -> x5, starting transfers between devices: none -> 22.2 us  [the longest x1 6.38 us: gather_small(): lax.all_to_all(jnp.broadcast_to(row[None], (self.n, *row.shape)), 'clip',...]
    convert_element_type x21, other arithmetic: 24.1 us -> 44.6 us  [the longest x7 21.8 us: step(): self.b = (self.b.astype(F32) + self.part(s - near)).astype(BF16)]
    reshape x7 -> x8, local copies, waits for them, and re-layouts: 27.8 us -> 8.48 us  [the longest x1 4.37 us: body(): ffn_t = grad_ffn.T.reshape(CORES, width // CORES, count)]
    all_to_all x0 -> x5, waiting for transfers between devices: none -> 18.4 us  [the longest x1 11.2 us: sum_all(): lax.all_to_all(rows.reshape(devices, -1, LANES), both, 0, 0, tiled=True)]
  transfers between devices with their start and end apart: 95 -> 81, of which waited for: 25 -> 13; matrix products, arithmetic and copies ran while one was open for 28% -> 20% of each run, Pallas kernels for 14% -> 36%
where the time goes in v2:
time: 523 us; the launch traced here: 513 us
  Pallas kernels  194 us (37%)
  starting transfers between devices  99.1 us (19%)
  waiting for transfers between devices  84.8 us (16%)
  local copies, waits for them, and re-layouts  66.4 us (13%)
  other arithmetic  59.4 us (11%)
  matrix products  6.9 us (1%)
    pallas_call x14, Pallas kernels, kernel_call(): pl.pallas_call(body, grid_spec=pltpu.PrefetchScalarGridSpec(num_scalar_pr...  193 us
    convert_element_type x7, other arithmetic, step(): self.b = (self.b.astype(F32) + self.part(s - near)).astype(BF16)  21.8 us
    ppermute x11, waiting for transfers between devices, step(): self.a = lax.ppermute(self.a, 'clip', ring.up)  20.4 us
    ppermute x3, waiting for transfers between devices, start_finish(): other = lax.ppermute(total, 'win', perm)  16.4 us
    unnamed x113, local copies, waits for them, and re-layouts  13.8 us
    all_to_all x2, waiting for transfers between devices, to_windows(): lax.all_to_all(window_rows(grid, groups), 'win', split_axis=0, concat_axi...  12.1 us
    ppermute x11, starting transfers between devices, step(): self.a = lax.ppermute(self.a, 'clip', ring.up)  11.9 us
    all_to_all x1, waiting for transfers between devices, sum_all(): lax.all_to_all(rows.reshape(devices, -1, LANES), both, 0, 0, tiled=True)  11.2 us
  transfers between devices with their start and end apart: 81, of which 13 were waited for; matrix products, arithmetic and copies ran while one was open for 20% of the time, Pallas kernels for 36%

profile of v2, /device:TPU:1, one launch (start us, length us, event | category | flops | bytes accessed | tf_op | source)
XLA Modules:
  0.0 513.3 jit_solution(1690160477422997838)
XLA Ops:
  6.3 6.4 %all-to-all-start = ((bf16[8,22,128]{2,1,0:T(8,128)(2,1)}), bf16[8,22,128]{2,1,0:T(8,128)(2,1)S(1)}, u32[]{:S(2)}, u32[]{:S(2)}) async-start(bf16[8,22,128]{2,1,0:T(8,128)(2,1)} %broadcast_in_dim.49), calls=%async_computation | async-start | bytes 98304 | tf_op jit(solution)/shard_map/all_to_all | solution.py:108
  32.1 7.0 %all-to-all-start.2 = ((bf16[4,2,5,2,8,1024]{5,4,3,2,1,0:T(8,128)(2,1)}), bf16[4,2,5,2,8,1024]{5,4,3,2,1,0:T(8,128)(2,1)}, u32[]{:S(2)}, u32[]{:S(2)}) async-start(bf16[4,2,5,2,8,1024]{5,4,3,2,1,0:T(8,128)(2,1)} %bitcast.14), calls=%async_computation.2 | async-start | bytes 2621440 | tf_op jit(solution)/shard_map/all_to_all | solution.py:1061
  43.6 12.1 %all-to-all-done.2 = bf16[4,2,5,2,8,1024]{5,4,3,2,1,0:T(8,128)(2,1)} async-done(((bf16[4,2,5,2,8,1024]{5,4,3,2,1,0:T(8,128)(2,1)}), bf16[4,2,5,2,8,1024]{5,4,3,2,1,0:T(8,128)(2,1)}, u32[]{:S(2)}, u32[]{:S(2)}) %all-to-all-start.2) | async-done | bytes 1310752 | tf_op jit(solution)/shard_map/all_to_all | solution.py:1061
  63.2 7.9 %collective-permute-done.6.rest_4_.rest_19_ = bf16[64,4096]{1,0:T(8,128)(2,1)} collective-permute-done((bf16[64,4096]{1,0:T(8,128)(2,1)}, bf16[64,4096]{1,0:T(8,128)(2,1)}, u32[]{:S(2)}, u32[]{:S(2)}) %collective-permute-start.6) | collective-permute-done | bytes 524320 | tf_op jit(solution)/shard_map/ppermute | solution.py:138
  77.5 11.9 %shard_map.282 = (bf16[640,1024]{1,0:T(8,128)(2,1)}, bf16[640,3072]{1,0:T(8,128)(2,1)}) custom-call(s32[9]{0:T(128)} %fusion.54.idx, bf16[640,1024]{1,0:T(8,128)(2,1)} %bitcast.226, f32[6,1024]{1,0:T(8,128)} %add.233.mod_ref, f32[1,3072]{1,0:T(1,128)} %pad_maximum_fusion.2.bias_ref, bf16[128,3072]{1,0:T(8,128)(2,1)} %rest_0_.14, ...), custom_call_target="tpu_custom_call" | custom-call | flops 4026531840 | bytes 12845056 | tf_op jit(solution)/shard_map/pallas_call | solution.py:251
  101.1 11.0 %shard_map.283 = (bf16[640,1024]{1,0:T(8,128)(2,1)}, f32[2,8,2,320]{3,2,1,0:T(2,128)}) custom-call(s32[2]{0:T(128)} %subtract_clamp_fusion.nv, bf16[640,3072]{1,0:T(8,128)(2,1)} %get-tuple-element.201.q_ref.k_ref.v_ref, bf16[640,3072]{1,0:T(8,128)(2,1)} %get-tuple-element.201.q_ref.k_ref.v_ref, bf16[640,3072]{1,0:T(8,128)(2,1)} %get-tuple-element.201.q_ref.k_ref.v_ref, ...), custom_call_target="tpu_custom_call" | custom-call | flops 1677721600 | bytes 2621440 | tf_op jit(solution)/shard_map/pallas_call | solution.py:251
  114.6 10.9 %shard_map.284 = (bf16[640,1024]{1,0:T(8,128)(2,1)}, f32[2,8,2,320]{3,2,1,0:T(2,128)}) custom-call(s32[2]{0:T(128)} %subtract_clamp_fusion.nv, bf16[640,3072]{1,0:T(8,128)(2,1)} %get-tuple-element.201.q_ref.k_ref.v_ref, bf16[640,3072]{1,0:T(8,128)(2,1)} %get-tuple-element.201.q_ref.k_ref.v_ref, ...), custom_call_target="tpu_custom_call", output_to_operand_aliasing={{0}: (5, {}), {1}: (6, {})} | custom-call | flops 1677721600 | bytes 2621440 | tf_op jit(solution)/shard_map/pallas_call | solution.py:251
  143.3 10.1 %shard_map.285 = (bf16[640,1024]{1,0:T(8,128)(2,1)}, f32[640,1024]{1,0:T(8,128)}, bf16[640,1024]{1,0:T(8,128)(2,1)}) custom-call(s32[9]{0:T(128)} %fusion.54.idx, bf16[640,1024]{1,0:T(8,128)(2,1)} %get-tuple-element.215.mixed_ref, bf16[640,1024]{1,0:T(8,128)(2,1)} %bitcast.227, f32[6,1024]{1,0:T(8,128)} %add.233.mod_ref, f32[640,1]{1,0:T(8,128)} %reshape.497.keep_ref, ...), custom_call_target="tpu_custom_call" | custom-call | flops 1342177280 | bytes 9961472 | tf_op jit(solution)/shard_map/pallas_call | solution.py:251
  158.7 11.5 %shard_map.286 = (bf16[640,4096]{1,0:T(8,128)(2,1)}, bf16[640,4096]{1,0:T(8,128)(2,1)}) custom-call(s32[9]{0:T(128)} %fusion.54.idx, bf16[640,1024]{1,0:T(8,128)(2,1)} %get-tuple-element.224.x_ref, f32[1,4096]{1,0:T(1,128)} %bitcast.261, bf16[128,4096]{1,0:T(8,128)(2,1)} %rest_0_.13, bf16[64,4096]{1,0:T(8,128)(2,1)} %collective-permute-done.8.rest_1_, ...), custom_call_target="tpu_custom_call" | custom-call | flops 2684354560 | bytes 10092544 | tf_op jit(solution)/shard_map/pallas_call | solution.py:251
  175.7 11.5 %shard_map.287 = (bf16[640,4096]{1,0:T(8,128)(2,1)}, bf16[640,4096]{1,0:T(8,128)(2,1)}) custom-call(s32[9]{0:T(128)} %fusion.54.idx, bf16[640,1024]{1,0:T(8,128)(2,1)} %get-tuple-element.224.x_ref, f32[1,4096]{1,0:T(1,128)} %bitcast.262, bf16[128,4096]{1,0:T(8,128)(2,1)} %rest_0_.13, ...), custom_call_target="tpu_custom_call", output_to_operand_aliasing={{0}: (18, {}), {1}: (19, {})} | custom-call | flops 2684354560 | bytes 10092544 | tf_op jit(solution)/shard_map/pallas_call | solution.py:251
  191.4 11.9 %shard_map.288 = (bf16[8,512,512]{2,1,0:T(8,128)(2,1)}, bf16[8,512,512]{2,1,0:T(8,128)(2,1)}) custom-call(s32[9]{0:T(128)} %fusion.54.idx, bf16[2,512,640]{2,1,0:T(8,128)(2,1)} %copy.127.mine_ref.other_ref, bf16[2,512,640]{2,1,0:T(8,128)(2,1)} %copy.127.mine_ref.other_ref, bf16[640,4096]{1,0:T(8,128)(2,1)} %get-tuple-element.236.right_ref.act_ref), custom_call_target="tpu_custom_call" | custom-call | flops 5368709120 | bytes 14942208 | tf_op jit(solution)/shard_map/pallas_call | solution.py:251
  207.1 11.9 %collective-permute-done.34.rest_4_ = bf16[256,1024]{1,0:T(8,128)(2,1)S(1)} collective-permute-done((bf16[256,1024]{1,0:T(8,128)(2,1)}, bf16[256,1024]{1,0:T(8,128)(2,1)S(1)}, u32[]{:S(2)}, u32[]{:S(2)}) %collective-permute-start.34) | collective-permute-done | bytes 524320 | tf_op jit(solution)/shard_map/ppermute | solution.py:138
  225.8 19.7 %shard_map.289 = (bf16[640,4096]{1,0:T(8,128)(2,1)}, bf16[512,4096]{1,0:T(8,128)(2,1)}, bf16[512,4096]{1,0:T(8,128)(2,1)}, f32[1,4096]{1,0:T(1,128)}) custom-call(s32[9]{0:T(128)} %fusion.54.idx, bf16[640,1024]{1,0:T(8,128)(2,1)} %multiply_convert_fusion.g_ref, bf16[640,4096]{1,0:T(8,128)(2,1)} %get-tuple-element.252.slope_ref, ...), custom_call_target="tpu_custom_call" | custom-call | flops 21474836480 | bytes 28573696 | tf_op jit(solution)/shard_map/pallas_call | solution.py:251
  251.8 20.7 %shard_map.290 = (f32[640,1024]{1,0:T(8,128)}, bf16[640,1024]{1,0:T(8,128)(2,1)}, bf16[640,1024]{1,0:T(8,128)(2,1)}, f32[4,1024]{1,0:T(4,128)}) custom-call(s32[9]{0:T(128)} %fusion.54.idx, bf16[640,4096]{1,0:T(8,128)(2,1)} %get-tuple-element.263.gh_ref, f32[640,1024]{1,0:T(8,128)} %get-tuple-element.264.mid_ref, bf16[640,1024]{1,0:T(8,128)(2,1)} %bitcast.229, ...), custom_call_target="tpu_custom_call" | custom-call | flops 6710886400 | bytes 26214400 | tf_op jit(solution)/shard_map/pallas_call | solution.py:251
  282.1 27.3 %shard_map.291 = (bf16[640,1024]{1,0:T(8,128)(2,1)}, bf16[640,1024]{1,0:T(8,128)(2,1)}, bf16[640,1024]{1,0:T(8,128)(2,1)}, f32[16,8,1152]{2,1,0:T(8,128)}) custom-call(s32[2]{0:T(128)} %subtract_clamp_fusion.nv, bf16[640,3072]{1,0:T(8,128)(2,1)} %get-tuple-element.201.q_ref.k_ref.v_ref, bf16[640,3072]{1,0:T(8,128)(2,1)} %get-tuple-element.201.q_ref.k_ref.v_ref, ...), custom_call_target="tpu_custom_call" | custom-call | flops 8388608000 | bytes 10485760 | tf_op jit(solution)/shard_map/pallas_call | solution.py:251
  309.5 9.1 %shard_map.292 = (bf16[512,4096]{1,0:T(8,128)(2,1)}, f32[1,4096]{1,0:T(1,128)}) custom-call(s32[9]{0:T(128)} %fusion.54.idx, bf16[2,512,640]{2,1,0:T(8,128)(2,1)} %bitcast.235, bf16[2,512,640]{2,1,0:T(8,128)(2,1)} %bitcast.237, bf16[640,1024]{1,0:T(8,128)(2,1)} %get-tuple-element.289.refs_2_.dq_ref, bf16[640,1024]{1,0:T(8,128)(2,1)} %get-tuple-element.290.refs_3_.dk_ref, ...), custom_call_target="tpu_custom_call" | custom-call | flops 2684354560 | bytes 10747904 | tf_op jit(solution)/shard_map/pallas_call | solution.py:251
  329.9 8.8 %shard_map.293 = bf16[512,4096]{1,0:T(8,128)(2,1)} custom-call(s32[9]{0:T(128)} %fusion.54.idx, bf16[2,512,640]{2,1,0:T(8,128)(2,1)} %bitcast.236, bf16[2,512,640]{2,1,0:T(8,128)(2,1)} %bitcast.238, bf16[640,1024]{1,0:T(8,128)(2,1)} %get-tuple-element.289.refs_2_.dq_ref, bf16[640,1024]{1,0:T(8,128)(2,1)} %get-tuple-element.290.refs_3_.dk_ref, ...), custom_call_target="tpu_custom_call" | custom-call | flops 2684354560 | bytes 10747904 | tf_op jit(solution)/shard_map/pallas_call | solution.py:251
  338.8 9.6 %collective-permute-done.53 = bf16[64,4096]{1,0:T(8,128)(2,1)} collective-permute-done((bf16[64,4096]{1,0:T(8,128)(2,1)}, bf16[64,4096]{1,0:T(8,128)(2,1)}, u32[]{:S(2)}, u32[]{:S(2)}) %collective-permute-start.53) | collective-permute-done | bytes 524320 | tf_op jit(solution)/shard_map/ppermute | solution.py:172
  362.1 15.0 %shard_map.294 = (bf16[640,1024]{1,0:T(8,128)(2,1)}, f32[2,1024]{1,0:T(2,128)}) custom-call(s32[9]{0:T(128)} %fusion.54.idx, bf16[640,1024]{1,0:T(8,128)(2,1)} %get-tuple-element.289.refs_2_.dq_ref, bf16[640,1024]{1,0:T(8,128)(2,1)} %get-tuple-element.290.refs_3_.dk_ref, bf16[640,1024]{1,0:T(8,128)(2,1)} %get-tuple-element.291.refs_4_.dv_ref, ...), custom_call_target="tpu_custom_call" | custom-call | flops 4026531840 | bytes 18087936 | tf_op jit(solution)/shard_map/pallas_call | solution.py:251
  396.0 13.1 %shard_map.295 = (bf16[640,1024]{1,0:T(8,128)(2,1)}, f32[1,1024]{1,0:T(1,128)}) custom-call(s32[9]{0:T(128)} %fusion.54.idx, bf16[640,4096]{1,0:T(8,128)(2,1)} %get-tuple-element.236.right_ref.act_ref, f32[640,1024]{1,0:T(8,128)} %get-tuple-element.264.mid_ref, bf16[640,1024]{1,0:T(8,128)(2,1)} %bitcast.230, f32[640,1]{1,0:T(8,128)} %reshape.497.keep_ref, ...), custom_call_target="tpu_custom_call" | custom-call | flops 5368709120 | bytes 18874368 | tf_op jit(solution)/shard_map/pallas_call | solution.py:251
  418.8 11.2 %all-to-all-done.5 = f32[32,24,128]{2,1,0:T(8,128)S(1)} async-done(((f32[32,24,128]{2,1,0:T(8,128)}), f32[32,24,128]{2,1,0:T(8,128)S(1)}, u32[]{:S(2)}, u32[]{:S(2)}) %all-to-all-start.5) | async-done | bytes 393248 | tf_op jit(solution)/shard_map/all_to_all | solution.py:122
  444.3 7.5 %all-to-all-done.7 = bf16[1,2,5,8,8,1024]{5,4,2,1,0,3:T(8,128)(2,1)S(1)} async-done(((bf16[1,2,5,8,8,1024]{5,4,2,1,0,3:T(8,128)(2,1)}), bf16[1,2,5,8,8,1024]{5,4,2,1,0,3:T(8,128)(2,1)S(1)}, u32[]{:S(2)}, u32[]{:S(2)}) %all-to-all-start.7) | async-done | bytes 1310752 | tf_op jit(solution)/shard_map/all_to_all | solution.py:1068
  456.7 8.5 %collective-permute-done.67 = bf16[64,4096]{1,0:T(8,128)(2,1)} collective-permute-done((bf16[64,4096]{1,0:T(8,128)(2,1)S(1)}, bf16[64,4096]{1,0:T(8,128)(2,1)}, u32[]{:S(2)}, u32[]{:S(2)}) %collective-permute-start.67) | collective-permute-done | bytes 524320 | tf_op jit(solution)/shard_map/ppermute | solution.py:186
  491.5 7.9 %collective-permute-done.69 = bf16[64,4096]{1,0:T(8,128)(2,1)S(1)} collective-permute-done((bf16[64,4096]{1,0:T(8,128)(2,1)S(1)}, bf16[64,4096]{1,0:T(8,128)(2,1)S(1)}, u32[]{:S(2)}, u32[]{:S(2)}) %collective-permute-start.69) | collective-permute-done | bytes 524320 | tf_op jit(solution)/shard_map/ppermute | solution.py:186
  (379 shorter events, 228.1 us)
Async XLA Ops:
  32.1 23.5 %all-to-all-start.2 = ((bf16[4,2,5,2,8,1024]{5,4,3,2,1,0:T(8,128)(2,1)}), bf16[4,2,5,2,8,1024]{5,4,3,2,1,0:T(8,128)(2,1)}, u32[]{:S(2)}, u32[]{:S(2)}) async-start(bf16[4,2,5,2,8,1024]{5,4,3,2,1,0:T(8,128)(2,1)} %bitcast.14), calls=%async_computation.2 | async-start | bytes 2621440 | tf_op jit(solution)/shard_map/all_to_all | solution.py:1061
  90.6 34.9 %all-to-all-start.3 = ((bf16[4,2,5,2,8,1024]{5,4,3,2,1,0:T(8,128)(2,1)}), bf16[4,2,5,2,8,1024]{5,4,3,2,1,0:T(8,128)(2,1)S(1)}, u32[]{:S(2)}, u32[]{:S(2)}) async-start(bf16[4,2,5,2,8,1024]{5,4,3,2,1,0:T(8,128)(2,1)} %bitcast.240), calls=%async_computation.3 | async-start | bytes 2621440 | tf_op jit(solution)/shard_map/all_to_all | solution.py:1061
  129.5 24.0 %collective-permute-start.20 = (bf16[64,4096]{1,0:T(8,128)(2,1)}, bf16[64,4096]{1,0:T(8,128)(2,1)}, u32[]{:S(2)}, u32[]{:S(2)}) collective-permute-start(bf16[64,4096]{1,0:T(8,128)(2,1)} %collective-permute-done.19.rest_3_), channel_id=1, source_target_pairs={{12,4},{20,12},{28,20},{24,28},{16,24},{8,16},{0,8},{4,0},{13,5},{... | collective-permute-start | bytes 1572872 | tf_op jit(solution)/shard_map/ppermute | solution.py:141
  130.4 23.6 %collective-permute-start.23 = (bf16[64,4096]{1,0:T(8,128)(2,1)}, bf16[64,4096]{1,0:T(8,128)(2,1)}, u32[]{:S(2)}, u32[]{:S(2)}) collective-permute-start(bf16[64,4096]{1,0:T(8,128)(2,1)} %collective-permute-done.8.rest_1_), channel_id=1, source_target_pairs={{0,1},{1,0},{2,3},{3,2},{4,5},{5,4},{6,7},{7,6},{8,9},{9,8},{10,11... | collective-permute-start | bytes 1572872 | tf_op jit(solution)/shard_map/ppermute | solution.py:153
  246.5 26.0 %collective-permute-start.47 = (bf16[8,64,4096]{2,1,0:T(8,128)(2,1)}, bf16[8,64,4096]{2,1,0:T(8,128)(2,1)S(1)}, u32[]{:S(2)}, u32[]{:S(2)}) collective-permute-start(bf16[8,64,4096]{2,1,0:T(8,128)(2,1)} %bitcast.279), channel_id=1, source_target_pairs={{0,1},{1,0},{2,3},{3,2},{4,5},{5,4},{6,7},{7,6},{8,9},{9,8},{10,11... | collective-permute-start | bytes 12582920 | tf_op jit(solution)/shard_map/ppermute | solution.py:1116
  250.3 25.5 %collective-permute-start.45 = (bf16[512,512]{1,0:T(8,128)(2,1)}, bf16[512,512]{1,0:T(8,128)(2,1)}, u32[]{:S(2)}, u32[]{:S(2)}) collective-permute-start(bf16[512,512]{1,0:T(8,128)(2,1)} %get-tuple-element.427), channel_id=1, source_target_pairs={{4,12},{12,20},{20,28},{28,24},{24,16},{16,8},{8,0},{0,4},{5,13},{... | collective-permute-start | bytes 1572872 | tf_op jit(solution)/shard_map/ppermute | solution.py:172
  251.3 24.5 %collective-permute-start.46 = (bf16[512,512]{1,0:T(8,128)(2,1)}, bf16[512,512]{1,0:T(8,128)(2,1)}, u32[]{:S(2)}, u32[]{:S(2)}) collective-permute-start(bf16[512,512]{1,0:T(8,128)(2,1)} %get-tuple-element.426), channel_id=1, source_target_pairs={{12,4},{20,12},{28,20},{24,28},{16,24},{8,16},{0,8},{4,0},{13,5},{... | collective-permute-start | bytes 1572872 | tf_op jit(solution)/shard_map/ppermute | solution.py:176
  279.0 30.4 %collective-permute-start.48 = (bf16[512,512]{1,0:T(8,128)(2,1)}, bf16[512,512]{1,0:T(8,128)(2,1)S(1)}, u32[]{:S(2)}, u32[]{:S(2)}) collective-permute-start(bf16[512,512]{1,0:T(8,128)(2,1)} %get-tuple-element.423), channel_id=1, source_target_pairs={{4,12},{12,20},{20,28},{28,24},{24,16},{16,8},{8,0},{0,4},{5,13},{... | collective-permute-start | bytes 1572872 | tf_op jit(solution)/shard_map/ppermute | solution.py:172
  280.0 29.5 %collective-permute-start.49 = (bf16[512,512]{1,0:T(8,128)(2,1)}, bf16[512,512]{1,0:T(8,128)(2,1)S(1)}, u32[]{:S(2)}, u32[]{:S(2)}) collective-permute-start(bf16[512,512]{1,0:T(8,128)(2,1)} %get-tuple-element.422), channel_id=1, source_target_pairs={{12,4},{20,12},{28,20},{24,28},{16,24},{8,16},{0,8},{4,0},{13,5},{... | collective-permute-start | bytes 1572872 | tf_op jit(solution)/shard_map/ppermute | solution.py:176
  280.5 29.0 %collective-permute-start.50 = (bf16[64,4096]{1,0:T(8,128)(2,1)}, bf16[64,4096]{1,0:T(8,128)(2,1)S(1)}, u32[]{:S(2)}, u32[]{:S(2)}) collective-permute-start(bf16[64,4096]{1,0:T(8,128)(2,1)} %get-tuple-element.272), channel_id=1, source_target_pairs={{4,12},{12,20},{20,28},{28,24},{24,16},{16,8},{8,0},{0,4},{5,13},{... | collective-permute-start | bytes 1572872 | tf_op jit(solution)/shard_map/ppermute | solution.py:172
  281.4 28.1 %collective-permute-start.51 = (bf16[64,4096]{1,0:T(8,128)(2,1)}, bf16[64,4096]{1,0:T(8,128)(2,1)S(1)}, u32[]{:S(2)}, u32[]{:S(2)}) collective-permute-start(bf16[64,4096]{1,0:T(8,128)(2,1)} %get-tuple-element.273), channel_id=1, source_target_pairs={{12,4},{20,12},{28,20},{24,28},{16,24},{8,16},{0,8},{4,0},{13,5},{... | collective-permute-start | bytes 1572872 | tf_op jit(solution)/shard_map/ppermute | solution.py:176
  318.6 29.7 %collective-permute-start.55 = (bf16[8,64,4096]{2,1,0:T(8,128)(2,1)}, bf16[8,64,4096]{2,1,0:T(8,128)(2,1)}, u32[]{:S(2)}, u32[]{:S(2)}) collective-permute-start(bf16[8,64,4096]{2,1,0:T(8,128)(2,1)} %bitcast.278), channel_id=1, source_target_pairs={{0,1},{1,0},{2,3},{3,2},{4,5},{5,4},{6,7},{7,6},{8,9},{9,8},{10,11... | collective-permute-start | bytes 12582920 | tf_op jit(solution)/shard_map/ppermute | solution.py:1116
  351.7 28.9 %collective-permute-start.56 = (bf16[64,4096]{1,0:T(8,128)(2,1)}, bf16[64,4096]{1,0:T(8,128)(2,1)S(1)}, u32[]{:S(2)}, u32[]{:S(2)}) collective-permute-start(bf16[64,4096]{1,0:T(8,128)(2,1)} %get-tuple-element.419), channel_id=1, source_target_pairs={{4,12},{12,20},{20,28},{28,24},{24,16},{16,8},{8,0},{0,4},{5,13},{... | collective-permute-start | bytes 1572872 | tf_op jit(solution)/shard_map/ppermute | solution.py:172
  352.6 28.0 %collective-permute-start.57 = (bf16[64,4096]{1,0:T(8,128)(2,1)}, bf16[64,4096]{1,0:T(8,128)(2,1)}, u32[]{:S(2)}, u32[]{:S(2)}) collective-permute-start(bf16[64,4096]{1,0:T(8,128)(2,1)} %get-tuple-element.418), channel_id=1, source_target_pairs={{12,4},{20,12},{28,20},{24,28},{16,24},{8,16},{0,8},{4,0},{13,5},{... | collective-permute-start | bytes 1572872 | tf_op jit(solution)/shard_map/ppermute | solution.py:176
  355.9 24.8 %collective-permute-start.58 = (bf16[64,4096]{1,0:T(8,128)(2,1)}, bf16[64,4096]{1,0:T(8,128)(2,1)}, u32[]{:S(2)}, u32[]{:S(2)}) collective-permute-start(bf16[64,4096]{1,0:T(8,128)(2,1)} %get-tuple-element.417), channel_id=1, source_target_pairs={{4,12},{12,20},{20,28},{28,24},{24,16},{16,8},{8,0},{0,4},{5,13},{... | collective-permute-start | bytes 1572872 | tf_op jit(solution)/shard_map/ppermute | solution.py:172
  356.9 23.8 %collective-permute-start.59 = (bf16[64,4096]{1,0:T(8,128)(2,1)}, bf16[64,4096]{1,0:T(8,128)(2,1)}, u32[]{:S(2)}, u32[]{:S(2)}) collective-permute-start(bf16[64,4096]{1,0:T(8,128)(2,1)} %get-tuple-element.416), channel_id=1, source_target_pairs={{12,4},{20,12},{28,20},{24,28},{16,24},{8,16},{0,8},{4,0},{13,5},{... | collective-permute-start | bytes 1572872 | tf_op jit(solution)/shard_map/ppermute | solution.py:176
  384.2 27.5 %collective-permute-start.61 = (bf16[64,4096]{1,0:T(8,128)(2,1)}, bf16[64,4096]{1,0:T(8,128)(2,1)}, u32[]{:S(2)}, u32[]{:S(2)}) collective-permute-start(bf16[64,4096]{1,0:T(8,128)(2,1)} %get-tuple-element.415), channel_id=1, source_target_pairs={{4,12},{12,20},{20,28},{28,24},{24,16},{16,8},{8,0},{0,4},{5,13},{... | collective-permute-start | bytes 1572872 | tf_op jit(solution)/shard_map/ppermute | solution.py:172
  385.1 26.5 %collective-permute-start.62 = (bf16[64,4096]{1,0:T(8,128)(2,1)}, bf16[64,4096]{1,0:T(8,128)(2,1)}, u32[]{:S(2)}, u32[]{:S(2)}) collective-permute-start(bf16[64,4096]{1,0:T(8,128)(2,1)} %get-tuple-element.414), channel_id=1, source_target_pairs={{12,4},{20,12},{28,20},{24,28},{16,24},{8,16},{0,8},{4,0},{13,5},{... | collective-permute-start | bytes 1572872 | tf_op jit(solution)/shard_map/ppermute | solution.py:176
  386.8 23.4 %all-to-all-start.4 = ((bf16[1,2,5,8,8,1024]{5,4,2,1,0,3:T(8,128)(2,1)}), bf16[1,2,5,8,8,1024]{5,4,2,1,0,3:T(8,128)(2,1)S(1)}, u32[]{:S(2)}, u32[]{:S(2)}) async-start(bf16[1,2,5,8,8,1024]{5,4,2,1,0,3:T(8,128)(2,1)} %copy.130), calls=%async_computation.4 | async-start | bytes 2621440 | tf_op jit(solution)/shard_map/all_to_all | solution.py:1068
  437.1 28.1 %collective-permute-start.67 = (bf16[64,4096]{1,0:T(8,128)(2,1)S(1)}, bf16[64,4096]{1,0:T(8,128)(2,1)}, u32[]{:S(2)}, u32[]{:S(2)}) collective-permute-start(bf16[64,4096]{1,0:T(8,128)(2,1)S(1)} %fusion.7), channel_id=1, source_target_pairs={{0,2},{1,3},{2,0},{3,1},{4,6},{5,7},{6,4},{7,5},{8,10},{9,11},{10,... | collective-permute-start | bytes 1572872 | tf_op jit(solution)/shard_map/ppermute | solution.py:186
  441.8 26.1 %collective-permute-start.65 = (bf16[64,4096]{1,0:T(8,128)(2,1)}, bf16[64,4096]{1,0:T(8,128)(2,1)}, u32[]{:S(2)}, u32[]{:S(2)}) collective-permute-start(bf16[64,4096]{1,0:T(8,128)(2,1)} %get-tuple-element.413), channel_id=1, source_target_pairs={{4,12},{12,20},{20,28},{28,24},{24,16},{16,8},{8,0},{0,4},{5,13},{... | collective-permute-start | bytes 1572872 | tf_op jit(solution)/shard_map/ppermute | solution.py:172
  442.5 25.4 %collective-permute-start.66 = (bf16[64,4096]{1,0:T(8,128)(2,1)}, bf16[64,4096]{1,0:T(8,128)(2,1)}, u32[]{:S(2)}, u32[]{:S(2)}) collective-permute-start(bf16[64,4096]{1,0:T(8,128)(2,1)} %get-tuple-element.412), channel_id=1, source_target_pairs={{12,4},{20,12},{28,20},{24,28},{16,24},{8,16},{0,8},{4,0},{13,5},{... | collective-permute-start | bytes 1572872 | tf_op jit(solution)/shard_map/ppermute | solution.py:176
  478.9 28.2 %all-to-all-start.8 = ((f32[8,1,128]{2,1,0:T(1,128)}), f32[8,1,128]{2,1,0:T(1,128)S(1)}, u32[]{:S(2)}, u32[]{:S(2)}) async-start(f32[8,1,128]{2,1,0:T(1,128)} %bitcast.88), calls=%async_computation.8 | async-start | bytes 8192 | tf_op jit(solution)/shard_map/all_to_all | solution.py:1294
  482.2 25.5 %collective-permute-start.71 = (bf16[64,4096]{1,0:T(8,128)(2,1)S(1)}, bf16[64,4096]{1,0:T(8,128)(2,1)}, u32[]{:S(2)}, u32[]{:S(2)}) collective-permute-start(bf16[64,4096]{1,0:T(8,128)(2,1)S(1)} %add_convert_fusion.1), channel_id=1, source_target_pairs={{0,1},{1,0},{2,3},{3,2},{4,5},{5,4},{6,7},{7,6},{8,9},{9,8},{10,11... | collective-permute-start | bytes 1572872 | tf_op jit(solution)/shard_map/ppermute | solution.py:192
  (109 other events, 1229.0 us)

commit v3 on v2

--- a/solution.py
+++ b/solution.py
@@ -116,12 +116,15 @@
             lax.all_to_all(jnp.broadcast_to(row[None], (wins, *row.shape)), "win", 0, 0), axis=0
         )
 
-    def sum_all(self, rows):
-        both = ("clip", "win")
+    def sum_part(self, rows):
         devices = self.n * lax.axis_size("win")
-        part = jnp.sum(lax.all_to_all(rows.reshape(devices, -1, LANES), both, 0, 0, tiled=True), axis=0)
-        whole = lax.all_to_all(jnp.broadcast_to(part[None], (devices, *part.shape)), both, 0, 0)
-        return whole.reshape(-1, LANES)
+        rows = rows.reshape(devices, -1, LANES)
+        return jnp.sum(lax.all_to_all(rows, ("clip", "win"), 0, 0, tiled=True), axis=0)
+
+    def share_parts(self, part):
+        devices = self.n * lax.axis_size("win")
+        part = jnp.broadcast_to(part[None], (devices, *part.shape))
+        return lax.all_to_all(part, ("clip", "win"), 0, 0).reshape(-1, LANES)
 
 
 class Gather:
@@ -164,17 +167,20 @@
         k = k % self.ring.n
         return self.keep[k].astype(F32) + self.got[k].astype(F32)
 
-    def step(self):
+    def step(self, *values):
         s, far, near = self.s, self.far, self.near
+        if 0 < s < far:
+            self.a = (self.a.astype(F32) + self.part(far - s)).astype(BF16)
+        if 0 < s < near:
+            self.b = (self.b.astype(F32) + self.part(s - near)).astype(BF16)
+        if values:
+            (self.a, self.b), *values = together((self.a, self.b), *values)
         if s < far:
-            if s > 0:
-                self.a = (self.a.astype(F32) + self.part(far - s)).astype(BF16)
             self.a = lax.ppermute(self.a, "clip", self.ring.up)
         if s < near:
-            if s > 0:
-                self.b = (self.b.astype(F32) + self.part(s - near)).astype(BF16)
             self.b = lax.ppermute(self.b, "clip", self.ring.down)
         self.s += 1
+        return values
 
     def settle(self, a, b):
         self.a, self.b = a, b
@@ -188,12 +194,7 @@
         return total
 
     def finish(self, total):
-        ring = self.ring
-        other = lax.ppermute(total, "win", ring.swap)
-        total, other = lax.optimization_barrier((total, other))
-        first = jnp.where(ring.core == 0, total, other)
-        second = jnp.where(ring.core == 0, other, total)
-        return first, second
+        return total, lax.ppermute(total, "win", self.ring.swap)
 
 
 class Weight:
@@ -1016,6 +1017,61 @@
     )
 
 
+def join_halves(idx, own, other, widths, turn=False):
+    n = idx.shape[0] - 1
+    half, cols = own.shape
+    shapes = [(cols, CORES * half)] if turn else [(CORES * half, w) for w in widths]
+
+    def body(idx, own_ref, other_ref, *outs):
+        core = idx[n]
+        for ref, place in ((own_ref, core), (other_ref, 1 - core)):
+            at = pl.ds(pl.multiple_of(place * half, half), half)
+            if turn:
+                outs[0][:, at] = ref[...].astype(F32).T
+            else:
+                start = 0
+                for out, w in zip(outs, widths):
+                    out[at, :] = ref[:, start : start + w].astype(F32)
+                    start += w
+
+    whole = lambda shape: pl.BlockSpec(shape, lambda i, idx: (0, 0))
+    return kernel_call(
+        body,
+        idx,
+        (1,),
+        [whole(own.shape), whole(own.shape)],
+        [whole(shape) for shape in shapes],
+        [jax.ShapeDtypeStruct(shape, F32) for shape in shapes],
+        [],
+        [own, other],
+        3e10,
+        8 * half * cols,
+    )
+
+
+def turn_half(idx, piece, own, before=None):
+    n = idx.shape[0] - 1
+    half, cols = piece.shape
+    kept = [before] if before is not None else []
+
+    def body(idx, ref, *rest):
+        rest[-1][...] = ref[...].astype(F32).T
+
+    return kernel_call(
+        body,
+        idx,
+        (1,),
+        [pl.BlockSpec((half, cols), lambda i, idx: (0, 0)), *[any_spec()] * len(kept)],
+        [pl.BlockSpec((cols, half), lambda i, idx: (0, idx[n] if own else 1 - idx[n]))],
+        [jax.ShapeDtypeStruct((cols, CORES * half), F32)],
+        [],
+        [piece, *kept],
+        3e10,
+        6 * half * cols,
+        {2: 0} if kept else None,
+    )[0]
+
+
 def column_pick():
     pick = np.zeros((SPAN, SPAN, WIN_S, LANES // WIN_S, WIN_S), np.float32)
     for b in range(SPAN):
@@ -1072,6 +1128,19 @@
         concat_axis=0,
         tiled=True,
     )
+    return window_back(out, shape)
+
+
+def from_windows_apart(rows, per_dev, shape):
+    groups = lax.axis_size("win")
+    me = lax.axis_index("win")
+    cells = rows.reshape(per_dev, WIN_T, groups, WIN_S // groups, WIN_S, shape[-1])
+    out = jnp.zeros((groups, *cells.shape[:2], *cells.shape[3:]), rows.dtype)
+    for k in range(groups):
+        piece = lax.dynamic_index_in_dim(cells, me ^ k, 2, keepdims=False)
+        if k:
+            piece = lax.ppermute(piece, "win", [(w, w ^ k) for w in range(groups)])
+        out = lax.dynamic_update_slice_in_dim(out, piece[None], me ^ k, 0)
     return window_back(out, shape)
 
 
@@ -1166,9 +1235,8 @@
     )
     group_b.step()
     cot = to_windows(cotangent, groups)
-    norm_t = turned(norm_in)
     half_mixed = attend(valid, triple, table, 0, 2)
-    *half_mixed, norm_t = stage([group_b], *half_mixed, norm_t)
+    half_mixed = stage([group_b], *half_mixed)
     group_b.step()
     gate_two = mod[5:6]
     grad_ffn = (keep * cot.astype(F32) * gate_two).astype(BF16)
@@ -1176,12 +1244,10 @@
     mixed, logs, grad_ffn = stage([group_b], mixed, logs, grad_ffn)
     spare(group_b, 3)
     ffn_t = grad_ffn.T.reshape(CORES, width // CORES, count)
-    mixed_t = turned(mixed)
-    attention, middle, norm_mid, ffn_t, mixed_t = stage(
+    attention, middle, norm_mid, ffn_t = stage(
         [group_b],
         *attention_out(idx, mixed, x, mod, keep, project_w, project_b),
         ffn_t,
-        mixed_t,
     )
     up_w = Weight(up_weight, *group_b.pieces())
 
@@ -1189,15 +1255,15 @@
     group_c.step()
     half_act = stage([group_c], *gelu_up(idx, norm_mid, up_w, up_b, 0, 2))
     group_c.step()
-    mid_t = turned(norm_mid)
-    activated, slope, mid_t = stage(
-        [group_c], *gelu_up(idx, norm_mid, up_w, up_b, 1, 2, half_act), mid_t
-    )
+    activated, slope = stage([group_c], *gelu_up(idx, norm_mid, up_w, up_b, 1, 2, half_act))
     group_c.step()
-    down_keep, down_send = stage([group_c], *down_outer(idx, ffn_t, activated))
+    down_keep, down_send, norm_in, mixed, mid_rows = stage(
+        [group_c], *down_outer(idx, ffn_t, activated), norm_in, mixed, norm_mid
+    )
     down_got = swap(down_send)
     spare(group_c, 3)
-    (down_got,) = stage([group_c], down_got)
+    norm_t, mixed_t, mid_t = turned(norm_in), turned(mixed), turned(mid_rows)
+    down_got, norm_t, mixed_t, mid_t = stage([group_c], down_got, norm_t, mixed_t, mid_t)
     down_w = Weight(down_weight, *group_c.pieces())
 
     sums_d = Scatter(ring, down_keep, down_got, False)
@@ -1223,31 +1289,34 @@
     (*grads, grad_table), idx = stage(
         [sums_d, sums_u], attend_back(valid, triple, table, grad_mixed, logs), idx
     )
-    spare(sums_d, 3)
-    sums_u.step()
+    for _ in range(3, steps):
+        (idx,) = sums_d.step(idx)
+    (idx,) = sums_u.step(idx)
     last = (norm_t, mixed_t, grads, grad_attention, 1024)
     (last_send, last_sums), idx = together(last_outer(idx, *last, True), idx)
     last_got = swap(split_rows(last_send))
     table_grad = gather_table(grad_table)
     last_keep, last_got, idx, table_grad = stage(
-        [sums_d, sums_u], last_outer(idx, *last, False)[0], last_got, idx, table_grad
-    )
+        [sums_d], last_outer(idx, *last, False)[0], last_got, idx, table_grad
+    )
+    inner = activated.shape[-1]
     sums_l = Scatter(ring, split_rows(last_keep), last_got, False)
-    sums_u.step()
-    sums_l.step()
-    (grad_rows, in_sums), idx, down_sum = stage(
+    (idx,) = sums_l.step(idx)
+    (idx,) = sums_u.step(idx)
+    (result, grad_gate_two), idx, down_sum = stage(
         [sums_u, sums_l],
-        input_back(idx, grads, x, grad_middle, mod, triple_w),
+        ffn_down(idx, activated, middle, cot, keep, gate_two, down_w, down_b),
         idx,
         sums_d.start_finish(),
     )
-    spare(sums_u, 3)
-    sums_l.step()
-    input_grad = from_windows(grad_rows, per_dev, tokens.shape)
-    input_grad, (result, grad_gate_two), down_parts = stage(
+    idx, down_sum, result = sums_l.step(idx, down_sum, result)
+    for _ in range(3, steps):
+        (idx,) = sums_u.step(idx)
+    output = from_windows(result, per_dev, tokens.shape)
+    (grad_rows, in_sums), output, down_parts = stage(
         [sums_l, sums_u],
-        input_grad,
-        ffn_down(idx, activated, middle, cot, keep, gate_two, down_w, down_b),
+        input_back(idx, grads, x, grad_middle, mod, triple_w),
+        output,
         sums_d.finish(down_sum),
     )
 
@@ -1270,15 +1339,26 @@
     ends = np.cumsum([0] + [p.shape[0] for p in pieces])
     pad = -int(ends[-1]) % (n * groups * 8)
     packed = jnp.concatenate(pieces + [jnp.zeros((pad, LANES), F32)])
-    sums_l.step()
-    packed = ring.sum_all(packed)
-    output = from_windows(result, per_dev, tokens.shape)
-    up_sum, packed, output = stage([sums_l], sums_u.start_finish(), packed, output)
-    spare(sums_l, 3)
-    up_parts = sums_u.finish(up_sum)
-
-    down_weight_grad = jnp.concatenate([p.T for p in down_parts], axis=1).astype(F32)
-    up_weight_grad = jnp.concatenate(up_parts, axis=0).astype(F32)
+    packed, idx = sums_l.step(packed, idx)
+    packed, down_half, idx, down_other, input_grad = stage(
+        [sums_l],
+        ring.sum_part(packed),
+        turn_half(idx, down_parts[0], True),
+        idx,
+        down_parts[1],
+        from_windows_apart(grad_rows, per_dev, tokens.shape),
+    )
+    for _ in range(3, steps):
+        packed, idx, sums_u.a, sums_u.b = sums_l.step(packed, idx, sums_u.a, sums_u.b)
+    packed, down_weight_grad, up_sum, idx = stage(
+        [sums_l],
+        ring.share_parts(packed),
+        turn_half(idx, down_other, False, down_half),
+        sums_u.start_finish(),
+        idx,
+    )
+    last_sum = sums_l.start_finish()
+    (up_weight_grad,) = join_halves(idx, *sums_u.finish(up_sum), [inner])
     table_grad, *bias_grads, grad_mod = (packed[ends[i] : ends[i + 1]] for i in range(len(pieces)))
     table_grad = table_grad.reshape(-1, wide)[:, :spans]
     bias_grads = [jnp.concatenate(bias_grads[:2]), *bias_grads[2:]]
@@ -1293,10 +1373,11 @@
     )
     back = lax.all_to_all(mm(grad_mod, modulate_weight, NT), "clip", 0, 0, tiled=True)
     condition_grad = back.reshape(1, width) * (sigma * (1.0 + condition * (1.0 - sigma)))
-    halves_l = sums_l.finish(sums_l.start_finish())
-    triple_weight_grad, project_weight_grad = (
-        jnp.concatenate([h[:, cols] for h in halves_l], axis=0).astype(F32)
-        for cols in (slice(0, 3 * width), slice(3 * width, 4 * width))
+    last_sum, condition_grad, up_weight_grad, table_grad, bias_grads = together(
+        last_sum, condition_grad, up_weight_grad, table_grad, bias_grads
+    )
+    triple_weight_grad, project_weight_grad = join_halves(
+        idx, *sums_l.finish(last_sum), [3 * width, width]
     )
     triple_bias_grad, project_bias_grad, up_bias_grad, down_bias_grad = bias_grads
     return (

time: 523 us -> 508 us (0.971)
  Pallas kernels: 194 us -> 206 us
  local copies, waits for them, and re-layouts: 66.4 us -> 56 us
  other arithmetic: 59.4 us -> 49.8 us
  waiting for transfers between devices: 84.8 us -> 75.2 us
    ppermute x3 -> x6, waiting for transfers between devices: 0.01 us -> 15.2 us  [the longest x3 15.2 us: from_windows_apart(): piece = lax.ppermute(piece, 'win', [(w, w ^ k) for w in range(groups)])]
    pallas_call x14 -> x18, Pallas kernels: 193 us -> 205 us  [kernel_call(): pl.pallas_call(body, grid_spec=pltpu.PrefetchScalarGridSpec(num_scalar_pr...]
    all_to_all x2, waiting for transfers between devices: 12.5 us -> 0.01 us  [the longest x1 0.01 us: share_parts(): return lax.all_to_all(part, ('clip', 'win'), 0, 0).reshape(-1, LANES)]
    ppermute x11, waiting for transfers between devices: 20.4 us -> 10.9 us  [step(): self.a = lax.ppermute(self.a, 'clip', ring.up)]
    ppermute x10, waiting for transfers between devices: 0.03 us -> 7.54 us  [step(): self.b = lax.ppermute(self.b, 'clip', self.ring.down)]
    all_to_all x2 -> x1, waiting for transfers between devices: 7.48 us -> 0.01 us  [from_windows(): lax.all_to_all(rows.reshape(1, per_dev, WIN_T, WIN_S, WIN_S, shape[-1]),...]
    convert_element_type x4 -> x0, other arithmetic: 5.28 us -> none  [the longest x2 2.14 us: body(): jnp.concatenate([h[:, cols] for h in halves_l], axis=0).astype(F32)]
    all_to_all x2 -> x1, starting transfers between devices: 10.8 us -> 5.98 us  [from_windows(): lax.all_to_all(rows.reshape(1, per_dev, WIN_T, WIN_S, WIN_S, shape[-1]),...]
  transfers between devices with their start and end apart: 81 -> 83, of which waited for: 13 -> 20; matrix products, arithmetic and copies ran while one was open for 20% -> 15% of each run, Pallas kernels for 36% -> 38%
where the time goes in v3:
time: 508 us; the launch traced here: 499 us
  Pallas kernels  206 us (41%)
  starting transfers between devices  101 us (20%)
  waiting for transfers between devices  75.2 us (15%)
  local copies, waits for them, and re-layouts  56 us (11%)
  other arithmetic  49.8 us (10%)
  matrix products  7.58 us (1%)
    pallas_call x18, Pallas kernels, kernel_call(): pl.pallas_call(body, grid_spec=pltpu.PrefetchScalarGridSpec(num_scalar_pr...  205 us
    convert_element_type x6, other arithmetic, step(): self.b = (self.b.astype(F32) + self.part(s - near)).astype(BF16)  19.6 us
    ppermute x3, waiting for transfers between devices, from_windows_apart(): piece = lax.ppermute(piece, 'win', [(w, w ^ k) for w in range(groups)])  15.2 us
    ppermute x3, waiting for transfers between devices, start_finish(): other = lax.ppermute(total, 'win', perm)  12.1 us
    all_to_all x2, waiting for transfers between devices, to_windows(): lax.all_to_all(window_rows(grid, groups), 'win', split_axis=0, concat_axi...  11.7 us
    all_to_all x2, starting transfers between devices, to_windows(): lax.all_to_all(window_rows(grid, groups), 'win', split_axis=0, concat_axi...  11.1 us
    ppermute x11, waiting for transfers between devices, step(): self.a = lax.ppermute(self.a, 'clip', ring.up)  10.9 us
    ppermute x10, starting transfers between devices, step(): self.b = lax.ppermute(self.b, 'clip', self.ring.down)  10.6 us
  transfers between devices with their start and end apart: 83, of which 20 were waited for; matrix products, arithmetic and copies ran while one was open for 15% of the time, Pallas kernels for 38%

profile of v3, /device:TPU:1, one launch (start us, length us, event | category | flops | bytes accessed | tf_op | source)
XLA Modules:
  0.0 498.6 jit_solution(480730398904168164)
XLA Ops:
  6.3 6.4 %all-to-all-start = ((bf16[8,22,128]{2,1,0:T(8,128)(2,1)}), bf16[8,22,128]{2,1,0:T(8,128)(2,1)S(1)}, u32[]{:S(2)}, u32[]{:S(2)}) async-start(bf16[8,22,128]{2,1,0:T(8,128)(2,1)} %broadcast_in_dim.64), calls=%async_computation | async-start | bytes 98304 | tf_op jit(solution)/shard_map/all_to_all | solution.py:108
  32.2 6.9 %all-to-all-start.2 = ((bf16[4,2,5,2,8,1024]{5,4,3,2,1,0:T(8,128)(2,1)}), bf16[4,2,5,2,8,1024]{5,4,3,2,1,0:T(8,128)(2,1)}, u32[]{:S(2)}, u32[]{:S(2)}) async-start(bf16[4,2,5,2,8,1024]{5,4,3,2,1,0:T(8,128)(2,1)} %bitcast.14), calls=%async_computation.2 | async-start | bytes 2621440 | tf_op jit(solution)/shard_map/all_to_all | solution.py:1117
  44.0 11.7 %all-to-all-done.2 = bf16[4,2,5,2,8,1024]{5,4,3,2,1,0:T(8,128)(2,1)} async-done(((bf16[4,2,5,2,8,1024]{5,4,3,2,1,0:T(8,128)(2,1)}), bf16[4,2,5,2,8,1024]{5,4,3,2,1,0:T(8,128)(2,1)}, u32[]{:S(2)}, u32[]{:S(2)}) %all-to-all-start.2) | async-done | bytes 1310752 | tf_op jit(solution)/shard_map/all_to_all | solution.py:1117
  63.2 7.9 %collective-permute-done.6.rest_4_.rest_19_ = bf16[64,4096]{1,0:T(8,128)(2,1)} collective-permute-done((bf16[64,4096]{1,0:T(8,128)(2,1)}, bf16[64,4096]{1,0:T(8,128)(2,1)}, u32[]{:S(2)}, u32[]{:S(2)}) %collective-permute-start.6) | collective-permute-done | bytes 524320 | tf_op jit(solution)/shard_map/ppermute | solution.py:141
  77.5 11.9 %shard_map.282 = (bf16[640,1024]{1,0:T(8,128)(2,1)}, bf16[640,3072]{1,0:T(8,128)(2,1)}) custom-call(s32[9]{0:T(128)} %fusion.50.idx, bf16[640,1024]{1,0:T(8,128)(2,1)} %bitcast.235, f32[6,1024]{1,0:T(8,128)} %add.250.mod_ref, f32[1,3072]{1,0:T(1,128)} %pad_maximum_fusion.2.bias_ref, bf16[128,3072]{1,0:T(8,128)(2,1)} %rest_0_.15, ...), custom_call_target="tpu_custom_call" | custom-call | flops 4026531840 | bytes 12845056 | tf_op jit(solution)/shard_map/pallas_call | solution.py:252
  96.2 11.0 %shard_map.283 = (bf16[640,1024]{1,0:T(8,128)(2,1)}, f32[2,8,2,320]{3,2,1,0:T(2,128)}) custom-call(s32[2]{0:T(128)} %subtract_clamp_fusion.nv, bf16[640,3072]{1,0:T(8,128)(2,1)} %get-tuple-element.244.q_ref.k_ref.v_ref, bf16[640,3072]{1,0:T(8,128)(2,1)} %get-tuple-element.244.q_ref.k_ref.v_ref, bf16[640,3072]{1,0:T(8,128)(2,1)} %get-tuple-element.244.q_ref.k_ref.v_ref, ...), custom_call_target="tpu_custom_call" | custom-call | flops 1677721600 | bytes 2621440 | tf_op jit(solution)/shard_map/pallas_call | solution.py:252
  111.4 10.9 %shard_map.284 = (bf16[640,1024]{1,0:T(8,128)(2,1)}, f32[2,8,2,320]{3,2,1,0:T(2,128)}) custom-call(s32[2]{0:T(128)} %subtract_clamp_fusion.nv, bf16[640,3072]{1,0:T(8,128)(2,1)} %get-tuple-element.244.q_ref.k_ref.v_ref, bf16[640,3072]{1,0:T(8,128)(2,1)} %get-tuple-element.244.q_ref.k_ref.v_ref, ...), custom_call_target="tpu_custom_call", output_to_operand_aliasing={{0}: (5, {}), {1}: (6, {})} | custom-call | flops 1677721600 | bytes 2621440 | tf_op jit(solution)/shard_map/pallas_call | solution.py:252
  136.0 10.2 %shard_map.285 = (bf16[640,1024]{1,0:T(8,128)(2,1)}, f32[640,1024]{1,0:T(8,128)}, bf16[640,1024]{1,0:T(8,128)(2,1)}) custom-call(s32[9]{0:T(128)} %fusion.50.idx, bf16[640,1024]{1,0:T(8,128)(2,1)} %get-tuple-element.287.mixed_ref, bf16[640,1024]{1,0:T(8,128)(2,1)} %bitcast.236, f32[6,1024]{1,0:T(8,128)} %add.250.mod_ref, f32[640,1]{1,0:T(8,128)} %reshape.497.keep_ref, ...), custom_call_target="tpu_custom_call" | custom-call | flops 1342177280 | bytes 9961472 | tf_op jit(solution)/shard_map/pallas_call | solution.py:252
  151.5 11.3 %shard_map.286 = (bf16[640,4096]{1,0:T(8,128)(2,1)}, bf16[640,4096]{1,0:T(8,128)(2,1)}) custom-call(s32[9]{0:T(128)} %fusion.50.idx, bf16[640,1024]{1,0:T(8,128)(2,1)} %get-tuple-element.288.x_ref, f32[1,4096]{1,0:T(1,128)} %bitcast.272, bf16[128,4096]{1,0:T(8,128)(2,1)} %rest_0_.13, bf16[64,4096]{1,0:T(8,128)(2,1)} %collective-permute-done.8.rest_1_, ...), custom_call_target="tpu_custom_call" | custom-call | flops 2684354560 | bytes 10092544 | tf_op jit(solution)/shard_map/pallas_call | solution.py:252
  164.3 11.4 %shard_map.287 = (bf16[640,4096]{1,0:T(8,128)(2,1)}, bf16[640,4096]{1,0:T(8,128)(2,1)}) custom-call(s32[9]{0:T(128)} %fusion.50.idx, bf16[640,1024]{1,0:T(8,128)(2,1)} %get-tuple-element.288.x_ref, f32[1,4096]{1,0:T(1,128)} %bitcast.273, bf16[128,4096]{1,0:T(8,128)(2,1)} %rest_0_.13, ...), custom_call_target="tpu_custom_call", output_to_operand_aliasing={{0}: (18, {}), {1}: (19, {})} | custom-call | flops 2684354560 | bytes 10092544 | tf_op jit(solution)/shard_map/pallas_call | solution.py:252
  180.8 12.1 %shard_map.288 = (bf16[8,512,512]{2,1,0:T(8,128)(2,1)}, bf16[8,512,512]{2,1,0:T(8,128)(2,1)}) custom-call(s32[9]{0:T(128)} %fusion.50.idx, bf16[2,512,640]{2,1,0:T(8,128)(2,1)} %copy.111.mine_ref.other_ref, bf16[2,512,640]{2,1,0:T(8,128)(2,1)} %copy.111.mine_ref.other_ref, bf16[640,4096]{1,0:T(8,128)(2,1)} %get-tuple-element.278.right_ref.act_ref), custom_call_target="tpu_custom_call" | custom-call | flops 5368709120 | bytes 14942208 | tf_op jit(solution)/shard_map/pallas_call | solution.py:252
  215.9 19.7 %shard_map.289 = (bf16[640,4096]{1,0:T(8,128)(2,1)}, bf16[512,4096]{1,0:T(8,128)(2,1)}, bf16[512,4096]{1,0:T(8,128)(2,1)}, f32[1,4096]{1,0:T(1,128)}) custom-call(s32[9]{0:T(128)} %fusion.50.idx, bf16[640,1024]{1,0:T(8,128)(2,1)} %multiply_convert_fusion.g_ref, bf16[640,4096]{1,0:T(8,128)(2,1)} %get-tuple-element.298.slope_ref, ...), custom_call_target="tpu_custom_call" | custom-call | flops 21474836480 | bytes 28573696 | tf_op jit(solution)/shard_map/pallas_call | solution.py:252
  241.1 21.3 %shard_map.290 = (f32[640,1024]{1,0:T(8,128)}, bf16[640,1024]{1,0:T(8,128)(2,1)}, bf16[640,1024]{1,0:T(8,128)(2,1)}, f32[4,1024]{1,0:T(4,128)}) custom-call(s32[9]{0:T(128)} %fusion.50.idx, bf16[640,4096]{1,0:T(8,128)(2,1)} %get-tuple-element.309.gh_ref, f32[640,1024]{1,0:T(8,128)} %get-tuple-element.310.mid_ref, bf16[640,1024]{1,0:T(8,128)(2,1)} %bitcast.238, ...), custom_call_target="tpu_custom_call" | custom-call | flops 6710886400 | bytes 26214400 | tf_op jit(solution)/shard_map/pallas_call | solution.py:252
  271.2 27.3 %shard_map.291 = (bf16[640,1024]{1,0:T(8,128)(2,1)}, bf16[640,1024]{1,0:T(8,128)(2,1)}, bf16[640,1024]{1,0:T(8,128)(2,1)}, f32[16,8,1152]{2,1,0:T(8,128)}) custom-call(s32[2]{0:T(128)} %subtract_clamp_fusion.nv, bf16[640,3072]{1,0:T(8,128)(2,1)} %get-tuple-element.244.q_ref.k_ref.v_ref, bf16[640,3072]{1,0:T(8,128)(2,1)} %get-tuple-element.244.q_ref.k_ref.v_ref, ...), custom_call_target="tpu_custom_call" | custom-call | flops 8388608000 | bytes 10485760 | tf_op jit(solution)/shard_map/pallas_call | solution.py:252
  303.9 9.0 %shard_map.292 = (bf16[512,4096]{1,0:T(8,128)(2,1)}, f32[1,4096]{1,0:T(1,128)}) custom-call(s32[9]{0:T(128)} %fusion.50.idx, bf16[2,512,640]{2,1,0:T(8,128)(2,1)} %bitcast.244, bf16[2,512,640]{2,1,0:T(8,128)(2,1)} %bitcast.246, bf16[640,1024]{1,0:T(8,128)(2,1)} %get-tuple-element.341.refs_2_.dq_ref, bf16[640,1024]{1,0:T(8,128)(2,1)} %get-tuple-element.342.refs_3_.dk_ref, ...), custom_call_target="tpu_custom_call" | custom-call | flops 2684354560 | bytes 10747904 | tf_op jit(solution)/shard_map/pallas_call | solution.py:252
  318.0 8.8 %shard_map.293 = bf16[512,4096]{1,0:T(8,128)(2,1)} custom-call(s32[9]{0:T(128)} %fusion.50.idx, bf16[2,512,640]{2,1,0:T(8,128)(2,1)} %bitcast.245, bf16[2,512,640]{2,1,0:T(8,128)(2,1)} %bitcast.247, bf16[640,1024]{1,0:T(8,128)(2,1)} %get-tuple-element.341.refs_2_.dq_ref, bf16[640,1024]{1,0:T(8,128)(2,1)} %get-tuple-element.342.refs_3_.dk_ref, ...), custom_call_target="tpu_custom_call" | custom-call | flops 2684354560 | bytes 10747904 | tf_op jit(solution)/shard_map/pallas_call | solution.py:252
  332.5 8.0 %collective-permute-done.54 = bf16[512,512]{1,0:T(8,128)(2,1)S(1)} collective-permute-done((bf16[512,512]{1,0:T(8,128)(2,1)}, bf16[512,512]{1,0:T(8,128)(2,1)S(1)}, u32[]{:S(2)}, u32[]{:S(2)}) %collective-permute-start.54) | collective-permute-done | bytes 524320 | tf_op jit(solution)/shard_map/ppermute | solution.py:179
  349.8 13.1 %shard_map.294 = (bf16[640,1024]{1,0:T(8,128)(2,1)}, f32[1,1024]{1,0:T(1,128)}) custom-call(s32[9]{0:T(128)} %fusion.50.idx, bf16[640,4096]{1,0:T(8,128)(2,1)} %get-tuple-element.278.right_ref.act_ref, f32[640,1024]{1,0:T(8,128)} %get-tuple-element.310.mid_ref, bf16[640,1024]{1,0:T(8,128)(2,1)} %bitcast.239, f32[640,1]{1,0:T(8,128)} %reshape.497.keep_ref, ...), custom_call_target="tpu_custom_call" | custom-call | flops 5368709120 | bytes 18874368 | tf_op jit(solution)/shard_map/pallas_call | solution.py:252
  372.8 6.0 %all-to-all-start.4 = ((bf16[1,2,5,8,8,1024]{5,4,2,1,0,3:T(8,128)(2,1)}), bf16[1,2,5,8,8,1024]{5,4,2,1,0,3:T(8,128)(2,1)S(1)}, u32[]{:S(2)}, u32[]{:S(2)}) async-start(bf16[1,2,5,8,8,1024]{5,4,2,1,0,3:T(8,128)(2,1)} %copy.121), calls=%async_computation.4 | async-start | bytes 2621440 | tf_op jit(solution)/shard_map/all_to_all | solution.py:1124
  384.8 14.8 %shard_map.295 = (bf16[640,1024]{1,0:T(8,128)(2,1)}, f32[2,1024]{1,0:T(2,128)}) custom-call(s32[9]{0:T(128)} %fusion.50.idx, bf16[640,1024]{1,0:T(8,128)(2,1)} %get-tuple-element.341.refs_2_.dq_ref, bf16[640,1024]{1,0:T(8,128)(2,1)} %get-tuple-element.342.refs_3_.dk_ref, bf16[640,1024]{1,0:T(8,128)(2,1)} %get-tuple-element.343.refs_4_.dv_ref, ...), custom_call_target="tpu_custom_call" | custom-call | flops 4026531840 | bytes 18087936 | tf_op jit(solution)/shard_map/pallas_call | solution.py:252
  422.9 7.1 %collective-permute-done.68 = bf16[2,5,2,8,1024]{4,3,2,1,0:T(8,128)(2,1)S(1)} collective-permute-done((bf16[2,5,2,8,1024]{4,3,2,1,0:T(8,128)(2,1)S(1)}, bf16[2,5,2,8,1024]{4,3,2,1,0:T(8,128)(2,1)S(1)}, u32[]{:S(2)}, u32[]{:S(2)}) %collective-permute-start.68) | collective-permute-done | bytes 327712 | tf_op jit(solution)/shard_map/ppermute | solution.py:1142
  430.1 8.1 %collective-permute-done.69 = bf16[2,5,2,8,1024]{4,3,2,1,0:T(8,128)(2,1)S(1)} collective-permute-done((bf16[2,5,2,8,1024]{4,3,2,1,0:T(8,128)(2,1)S(1)}, bf16[2,5,2,8,1024]{4,3,2,1,0:T(8,128)(2,1)S(1)}, u32[]{:S(2)}, u32[]{:S(2)}) %collective-permute-start.69) | collective-permute-done | bytes 327712 | tf_op jit(solution)/shard_map/ppermute | solution.py:1142
  454.2 12.1 %collective-permute-done.71 = bf16[64,4096]{1,0:T(8,128)(2,1)S(1)} collective-permute-done((bf16[64,4096]{1,0:T(8,128)(2,1)S(1)}, bf16[64,4096]{1,0:T(8,128)(2,1)S(1)}, u32[]{:S(2)}, u32[]{:S(2)}) %collective-permute-start.71) | collective-permute-done | bytes 524320 | tf_op jit(solution)/shard_map/ppermute | solution.py:192
  471.0 5.3 %all-to-all-start.7 = ((f32[8,1,128]{2,1,0:T(1,128)}), f32[8,1,128]{2,1,0:T(1,128)S(1)}, u32[]{:S(2)}, u32[]{:S(2)}) async-start(f32[8,1,128]{2,1,0:T(1,128)} %bitcast.95), calls=%async_computation.7 | async-start | bytes 8192 | tf_op jit(solution)/shard_map/all_to_all | solution.py:1374
  (370 shorter events, 223.8 us)
Async XLA Ops:
  32.2 23.4 %all-to-all-start.2 = ((bf16[4,2,5,2,8,1024]{5,4,3,2,1,0:T(8,128)(2,1)}), bf16[4,2,5,2,8,1024]{5,4,3,2,1,0:T(8,128)(2,1)}, u32[]{:S(2)}, u32[]{:S(2)}) async-start(bf16[4,2,5,2,8,1024]{5,4,3,2,1,0:T(8,128)(2,1)} %bitcast.14), calls=%async_computation.2 | async-start | bytes 2621440 | tf_op jit(solution)/shard_map/all_to_all | solution.py:1117
  90.6 31.7 %all-to-all-start.3 = ((bf16[4,2,5,2,8,1024]{5,4,3,2,1,0:T(8,128)(2,1)}), bf16[4,2,5,2,8,1024]{5,4,3,2,1,0:T(8,128)(2,1)S(1)}, u32[]{:S(2)}, u32[]{:S(2)}) async-start(bf16[4,2,5,2,8,1024]{5,4,3,2,1,0:T(8,128)(2,1)} %bitcast.249), calls=%async_computation.3 | async-start | bytes 2621440 | tf_op jit(solution)/shard_map/all_to_all | solution.py:1117
  212.4 23.2 %collective-permute-start.36 = (bf16[512,512]{1,0:T(8,128)(2,1)S(1)}, bf16[512,512]{1,0:T(8,128)(2,1)S(1)}, u32[]{:S(2)}, u32[]{:S(2)}) collective-permute-start(bf16[512,512]{1,0:T(8,128)(2,1)S(1)} %get-tuple-element.294), channel_id=1, source_target_pairs={{4,12},{12,20},{20,28},{28,24},{24,16},{16,8},{8,0},{0,4},{5,13},{... | collective-permute-start | bytes 1572872 | tf_op jit(solution)/shard_map/ppermute | solution.py:179
  212.5 23.1 %collective-permute-start.37 = (bf16[512,512]{1,0:T(8,128)(2,1)S(1)}, bf16[512,512]{1,0:T(8,128)(2,1)S(1)}, u32[]{:S(2)}, u32[]{:S(2)}) collective-permute-start(bf16[512,512]{1,0:T(8,128)(2,1)S(1)} %get-tuple-element.295), channel_id=1, source_target_pairs={{12,4},{20,12},{28,20},{24,28},{16,24},{8,16},{0,8},{4,0},{13,5},{... | collective-permute-start | bytes 1572872 | tf_op jit(solution)/shard_map/ppermute | solution.py:181
  235.6 26.7 %collective-permute-start.47 = (bf16[8,64,4096]{2,1,0:T(8,128)(2,1)}, bf16[8,64,4096]{2,1,0:T(8,128)(2,1)}, u32[]{:S(2)}, u32[]{:S(2)}) collective-permute-start(bf16[8,64,4096]{2,1,0:T(8,128)(2,1)} %bitcast.290), channel_id=1, source_target_pairs={{0,1},{1,0},{2,3},{3,2},{4,5},{5,4},{6,7},{7,6},{8,9},{9,8},{10,11... | collective-permute-start | bytes 12582920 | tf_op jit(solution)/shard_map/ppermute | solution.py:1185
  239.6 25.2 %collective-permute-start.45 = (bf16[512,512]{1,0:T(8,128)(2,1)}, bf16[512,512]{1,0:T(8,128)(2,1)}, u32[]{:S(2)}, u32[]{:S(2)}) collective-permute-start(bf16[512,512]{1,0:T(8,128)(2,1)} %get-tuple-element.443), channel_id=1, source_target_pairs={{4,12},{12,20},{20,28},{28,24},{24,16},{16,8},{8,0},{0,4},{5,13},{... | collective-permute-start | bytes 1572872 | tf_op jit(solution)/shard_map/ppermute | solution.py:179
  239.7 25.1 %collective-permute-start.46 = (bf16[512,512]{1,0:T(8,128)(2,1)}, bf16[512,512]{1,0:T(8,128)(2,1)}, u32[]{:S(2)}, u32[]{:S(2)}) collective-permute-start(bf16[512,512]{1,0:T(8,128)(2,1)} %get-tuple-element.442), channel_id=1, source_target_pairs={{12,4},{20,12},{28,20},{24,28},{16,24},{8,16},{0,8},{4,0},{13,5},{... | collective-permute-start | bytes 1572872 | tf_op jit(solution)/shard_map/ppermute | solution.py:181
  268.1 30.5 %collective-permute-start.48 = (bf16[512,512]{1,0:T(8,128)(2,1)}, bf16[512,512]{1,0:T(8,128)(2,1)}, u32[]{:S(2)}, u32[]{:S(2)}) collective-permute-start(bf16[512,512]{1,0:T(8,128)(2,1)} %get-tuple-element.439), channel_id=1, source_target_pairs={{4,12},{12,20},{20,28},{28,24},{24,16},{16,8},{8,0},{0,4},{5,13},{... | collective-permute-start | bytes 1572872 | tf_op jit(solution)/shard_map/ppermute | solution.py:179
  268.2 30.4 %collective-permute-start.49 = (bf16[512,512]{1,0:T(8,128)(2,1)}, bf16[512,512]{1,0:T(8,128)(2,1)}, u32[]{:S(2)}, u32[]{:S(2)}) collective-permute-start(bf16[512,512]{1,0:T(8,128)(2,1)} %get-tuple-element.438), channel_id=1, source_target_pairs={{12,4},{20,12},{28,20},{24,28},{16,24},{8,16},{0,8},{4,0},{13,5},{... | collective-permute-start | bytes 1572872 | tf_op jit(solution)/shard_map/ppermute | solution.py:181
  269.5 29.0 %collective-permute-start.50 = (bf16[64,4096]{1,0:T(8,128)(2,1)}, bf16[64,4096]{1,0:T(8,128)(2,1)}, u32[]{:S(2)}, u32[]{:S(2)}) collective-permute-start(bf16[64,4096]{1,0:T(8,128)(2,1)} %get-tuple-element.318), channel_id=1, source_target_pairs={{4,12},{12,20},{20,28},{28,24},{24,16},{16,8},{8,0},{0,4},{5,13},{... | collective-permute-start | bytes 1572872 | tf_op jit(solution)/shard_map/ppermute | solution.py:179
  269.6 28.9 %collective-permute-start.51 = (bf16[64,4096]{1,0:T(8,128)(2,1)}, bf16[64,4096]{1,0:T(8,128)(2,1)}, u32[]{:S(2)}, u32[]{:S(2)}) collective-permute-start(bf16[64,4096]{1,0:T(8,128)(2,1)} %get-tuple-element.319), channel_id=1, source_target_pairs={{12,4},{20,12},{28,20},{24,28},{16,24},{8,16},{0,8},{4,0},{13,5},{... | collective-permute-start | bytes 1572872 | tf_op jit(solution)/shard_map/ppermute | solution.py:181
  312.9 27.5 %collective-permute-start.55 = (bf16[8,64,4096]{2,1,0:T(8,128)(2,1)}, bf16[8,64,4096]{2,1,0:T(8,128)(2,1)}, u32[]{:S(2)}, u32[]{:S(2)}) collective-permute-start(bf16[8,64,4096]{2,1,0:T(8,128)(2,1)} %bitcast.289), channel_id=1, source_target_pairs={{0,1},{1,0},{2,3},{3,2},{4,5},{5,4},{6,7},{7,6},{8,9},{9,8},{10,11... | collective-permute-start | bytes 12582920 | tf_op jit(solution)/shard_map/ppermute | solution.py:1185
  316.6 23.9 %collective-permute-start.54 = (bf16[512,512]{1,0:T(8,128)(2,1)}, bf16[512,512]{1,0:T(8,128)(2,1)S(1)}, u32[]{:S(2)}, u32[]{:S(2)}) collective-permute-start(bf16[512,512]{1,0:T(8,128)(2,1)} %fusion.32), channel_id=1, source_target_pairs={{4,12},{12,20},{20,28},{28,24},{24,16},{16,8},{8,0},{0,4},{5,13},{... | collective-permute-start | bytes 1572872 | tf_op jit(solution)/shard_map/ppermute | solution.py:179
  343.4 22.2 %collective-permute-start.56 = (bf16[64,4096]{1,0:T(8,128)(2,1)}, bf16[64,4096]{1,0:T(8,128)(2,1)S(1)}, u32[]{:S(2)}, u32[]{:S(2)}) collective-permute-start(bf16[64,4096]{1,0:T(8,128)(2,1)} %get-tuple-element.354), channel_id=1, source_target_pairs={{4,12},{12,20},{20,28},{28,24},{24,16},{16,8},{8,0},{0,4},{5,13},{... | collective-permute-start | bytes 1572872 | tf_op jit(solution)/shard_map/ppermute | solution.py:179
  344.8 22.4 %collective-permute-start.58 = (bf16[64,4096]{1,0:T(8,128)(2,1)}, bf16[64,4096]{1,0:T(8,128)(2,1)}, u32[]{:S(2)}, u32[]{:S(2)}) collective-permute-start(bf16[64,4096]{1,0:T(8,128)(2,1)} %get-tuple-element.356), channel_id=1, source_target_pairs={{4,12},{12,20},{20,28},{28,24},{24,16},{16,8},{8,0},{0,4},{5,13},{... | collective-permute-start | bytes 1572872 | tf_op jit(solution)/shard_map/ppermute | solution.py:179
  345.6 22.1 %collective-permute-start.59 = (bf16[64,4096]{1,0:T(8,128)(2,1)}, bf16[64,4096]{1,0:T(8,128)(2,1)}, u32[]{:S(2)}, u32[]{:S(2)}) collective-permute-start(bf16[64,4096]{1,0:T(8,128)(2,1)} %get-tuple-element.357), channel_id=1, source_target_pairs={{12,4},{20,12},{28,20},{24,28},{16,24},{8,16},{0,8},{4,0},{13,5},{... | collective-permute-start | bytes 1572872 | tf_op jit(solution)/shard_map/ppermute | solution.py:181
  372.8 26.7 %all-to-all-start.4 = ((bf16[1,2,5,8,8,1024]{5,4,2,1,0,3:T(8,128)(2,1)}), bf16[1,2,5,8,8,1024]{5,4,2,1,0,3:T(8,128)(2,1)S(1)}, u32[]{:S(2)}, u32[]{:S(2)}) async-start(bf16[1,2,5,8,8,1024]{5,4,2,1,0,3:T(8,128)(2,1)} %copy.121), calls=%async_computation.4 | async-start | bytes 2621440 | tf_op jit(solution)/shard_map/all_to_all | solution.py:1124
  382.6 23.3 %collective-permute-start.63 = (bf16[64,4096]{1,0:T(8,128)(2,1)}, bf16[64,4096]{1,0:T(8,128)(2,1)S(1)}, u32[]{:S(2)}, u32[]{:S(2)}) collective-permute-start(bf16[64,4096]{1,0:T(8,128)(2,1)} %get-tuple-element.374), channel_id=1, source_target_pairs={{12,4},{20,12},{28,20},{24,28},{16,24},{8,16},{0,8},{4,0},{13,5},{... | collective-permute-start | bytes 1572872 | tf_op jit(solution)/shard_map/ppermute | solution.py:181
  383.3 22.6 %collective-permute-start.64 = (bf16[512,512]{1,0:T(8,128)(2,1)}, bf16[512,512]{1,0:T(8,128)(2,1)}, u32[]{:S(2)}, u32[]{:S(2)}) collective-permute-start(bf16[512,512]{1,0:T(8,128)(2,1)} %add_convert_fusion.2.ref), channel_id=1, source_target_pairs={{0,1},{1,0},{2,3},{3,2},{4,5},{5,4},{6,7},{7,6},{8,9},{9,8},{10,11... | collective-permute-start | bytes 1572872 | tf_op jit(solution)/shard_map/ppermute | solution.py:197
  410.8 28.6 %collective-permute-start.65 = (bf16[64,4096]{1,0:T(8,128)(2,1)}, bf16[64,4096]{1,0:T(8,128)(2,1)}, u32[]{:S(2)}, u32[]{:S(2)}) collective-permute-start(bf16[64,4096]{1,0:T(8,128)(2,1)} %get-tuple-element.390), channel_id=1, source_target_pairs={{4,12},{12,20},{20,28},{28,24},{24,16},{16,8},{8,0},{0,4},{5,13},{... | collective-permute-start | bytes 1572872 | tf_op jit(solution)/shard_map/ppermute | solution.py:179
  411.8 27.6 %collective-permute-start.66 = (bf16[64,4096]{1,0:T(8,128)(2,1)}, bf16[64,4096]{1,0:T(8,128)(2,1)}, u32[]{:S(2)}, u32[]{:S(2)}) collective-permute-start(bf16[64,4096]{1,0:T(8,128)(2,1)} %get-tuple-element.391), channel_id=1, source_target_pairs={{12,4},{20,12},{28,20},{24,28},{16,24},{8,16},{0,8},{4,0},{13,5},{... | collective-permute-start | bytes 1572872 | tf_op jit(solution)/shard_map/ppermute | solution.py:181
  412.3 27.1 %all-to-all-start.5 = ((f32[32,24,128]{2,1,0:T(8,128)}), f32[32,24,128]{2,1,0:T(8,128)S(1)}, u32[]{:S(2)}, u32[]{:S(2)}) async-start(f32[32,24,128]{2,1,0:T(8,128)} %bitcast.78), calls=%async_computation.5 | async-start | bytes 786432 | tf_op jit(solution)/shard_map/all_to_all | solution.py:122
  441.9 24.6 %collective-permute-start.70 = (bf16[64,4096]{1,0:T(8,128)(2,1)}, bf16[64,4096]{1,0:T(8,128)(2,1)}, u32[]{:S(2)}, u32[]{:S(2)}) collective-permute-start(bf16[64,4096]{1,0:T(8,128)(2,1)} %fusion.4), channel_id=1, source_target_pairs={{4,12},{12,20},{20,28},{28,24},{24,16},{16,8},{8,0},{0,4},{5,13},{... | collective-permute-start | bytes 1572872 | tf_op jit(solution)/shard_map/ppermute | solution.py:179
  443.9 22.7 %all-to-all-start.6 = ((f32[32,24,128]{2,1,0:T(8,128)}), f32[32,24,128]{2,1,0:T(8,128)S(1)}, u32[]{:S(2)}, u32[]{:S(2)}) async-start(f32[32,24,128]{2,1,0:T(8,128)} %broadcast_in_dim.79), calls=%async_computation.6 | async-start | bytes 786432 | tf_op jit(solution)/shard_map/all_to_all | solution.py:127
  (107 other events, 1158.8 us)

commit v4 on v3

--- a/solution.py
+++ b/solution.py
@@ -1297,7 +1297,7 @@
     last_got = swap(split_rows(last_send))
     table_grad = gather_table(grad_table)
     last_keep, last_got, idx, table_grad = stage(
-        [sums_d], last_outer(idx, *last, False)[0], last_got, idx, table_grad
+        [], last_outer(idx, *last, False)[0], last_got, idx, table_grad
     )
     inner = activated.shape[-1]
     sums_l = Scatter(ring, split_rows(last_keep), last_got, False)

time: 508 us -> 522 us (1.028)
  waiting for transfers between devices: 75.2 us -> 90.3 us
    ppermute x11, waiting for transfers between devices: 9.98 us -> 19.4 us  [step(): self.a = lax.ppermute(self.a, 'clip', self.ring.up)]
    ppermute x3, waiting for transfers between devices: 12.1 us -> 19.7 us  [start_finish(): other = lax.ppermute(total, 'win', perm)]
  transfers between devices with their start and end apart: 83 -> 83, of which waited for: 20 -> 19; matrix products, arithmetic and copies ran while one was open for 15% -> 14% of each run, Pallas kernels for 38% -> 37%
where the time goes in v4:
time: 522 us; the launch traced here: 513 us
  Pallas kernels  207 us (40%)
  starting transfers between devices  102 us (20%)
  waiting for transfers between devices  90.3 us (17%)
  local copies, waits for them, and re-layouts  55.9 us (11%)
  other arithmetic  48.1 us (9%)
  matrix products  7.57 us (1%)
    pallas_call x18, Pallas kernels, kernel_call(): pl.pallas_call(body, grid_spec=pltpu.PrefetchScalarGridSpec(num_scalar_pr...  205 us
    ppermute x3, waiting for transfers between devices, start_finish(): other = lax.ppermute(total, 'win', perm)  19.7 us
    convert_element_type x6, other arithmetic, step(): self.b = (self.b.astype(F32) + self.part(s - near)).astype(BF16)  19.7 us
    ppermute x11, waiting for transfers between devices, step(): self.a = lax.ppermute(self.a, 'clip', self.ring.up)  19.4 us
    ppermute x3, waiting for transfers between devices, from_windows_apart(): piece = lax.ppermute(piece, 'win', [(w, w ^ k) for w in range(groups)])  15.2 us
    all_to_all x2, waiting for transfers between devices, to_windows(): lax.all_to_all(window_rows(grid, groups), 'win', split_axis=0, concat_axi...  11.7 us
    all_to_all x2, starting transfers between devices, to_windows(): lax.all_to_all(window_rows(grid, groups), 'win', split_axis=0, concat_axi...  11.1 us
    ppermute x11, waiting for transfers between devices, step(): self.a = lax.ppermute(self.a, 'clip', ring.up)  11 us
  transfers between devices with their start and end apart: 83, of which 19 were waited for; matrix products, arithmetic and copies ran while one was open for 14% of the time, Pallas kernels for 37%

profile of v4, /device:TPU:1, one launch (start us, length us, event | category | flops | bytes accessed | tf_op | source)
XLA Modules:
  0.0 512.8 jit_solution(11051372995319201612)
XLA Ops:
  6.3 6.4 %all-to-all-start = ((bf16[8,22,128]{2,1,0:T(8,128)(2,1)}), bf16[8,22,128]{2,1,0:T(8,128)(2,1)S(1)}, u32[]{:S(2)}, u32[]{:S(2)}) async-start(bf16[8,22,128]{2,1,0:T(8,128)(2,1)} %broadcast_in_dim.64), calls=%async_computation | async-start | bytes 98304 | tf_op jit(solution)/shard_map/all_to_all | solution.py:108
  32.2 6.9 %all-to-all-start.2 = ((bf16[4,2,5,2,8,1024]{5,4,3,2,1,0:T(8,128)(2,1)}), bf16[4,2,5,2,8,1024]{5,4,3,2,1,0:T(8,128)(2,1)}, u32[]{:S(2)}, u32[]{:S(2)}) async-start(bf16[4,2,5,2,8,1024]{5,4,3,2,1,0:T(8,128)(2,1)} %bitcast.14), calls=%async_computation.2 | async-start | bytes 2621440 | tf_op jit(solution)/shard_map/all_to_all | solution.py:1117
  44.0 11.7 %all-to-all-done.2 = bf16[4,2,5,2,8,1024]{5,4,3,2,1,0:T(8,128)(2,1)} async-done(((bf16[4,2,5,2,8,1024]{5,4,3,2,1,0:T(8,128)(2,1)}), bf16[4,2,5,2,8,1024]{5,4,3,2,1,0:T(8,128)(2,1)}, u32[]{:S(2)}, u32[]{:S(2)}) %all-to-all-start.2) | async-done | bytes 1310752 | tf_op jit(solution)/shard_map/all_to_all | solution.py:1117
  63.2 7.9 %collective-permute-done.6.rest_4_.rest_19_ = bf16[64,4096]{1,0:T(8,128)(2,1)} collective-permute-done((bf16[64,4096]{1,0:T(8,128)(2,1)}, bf16[64,4096]{1,0:T(8,128)(2,1)}, u32[]{:S(2)}, u32[]{:S(2)}) %collective-permute-start.6) | collective-permute-done | bytes 524320 | tf_op jit(solution)/shard_map/ppermute | solution.py:141
  77.5 11.8 %shard_map.282 = (bf16[640,1024]{1,0:T(8,128)(2,1)}, bf16[640,3072]{1,0:T(8,128)(2,1)}) custom-call(s32[9]{0:T(128)} %fusion.50.idx, bf16[640,1024]{1,0:T(8,128)(2,1)} %bitcast.235, f32[6,1024]{1,0:T(8,128)} %add.250.mod_ref, f32[1,3072]{1,0:T(1,128)} %pad_maximum_fusion.2.bias_ref, bf16[128,3072]{1,0:T(8,128)(2,1)} %rest_0_.15, ...), custom_call_target="tpu_custom_call" | custom-call | flops 4026531840 | bytes 12845056 | tf_op jit(solution)/shard_map/pallas_call | solution.py:252
  96.1 11.0 %shard_map.283 = (bf16[640,1024]{1,0:T(8,128)(2,1)}, f32[2,8,2,320]{3,2,1,0:T(2,128)}) custom-call(s32[2]{0:T(128)} %subtract_clamp_fusion.nv, bf16[640,3072]{1,0:T(8,128)(2,1)} %get-tuple-element.242.q_ref.k_ref.v_ref, bf16[640,3072]{1,0:T(8,128)(2,1)} %get-tuple-element.242.q_ref.k_ref.v_ref, bf16[640,3072]{1,0:T(8,128)(2,1)} %get-tuple-element.242.q_ref.k_ref.v_ref, ...), custom_call_target="tpu_custom_call" | custom-call | flops 1677721600 | bytes 2621440 | tf_op jit(solution)/shard_map/pallas_call | solution.py:252
  111.4 10.9 %shard_map.284 = (bf16[640,1024]{1,0:T(8,128)(2,1)}, f32[2,8,2,320]{3,2,1,0:T(2,128)}) custom-call(s32[2]{0:T(128)} %subtract_clamp_fusion.nv, bf16[640,3072]{1,0:T(8,128)(2,1)} %get-tuple-element.242.q_ref.k_ref.v_ref, bf16[640,3072]{1,0:T(8,128)(2,1)} %get-tuple-element.242.q_ref.k_ref.v_ref, ...), custom_call_target="tpu_custom_call", output_to_operand_aliasing={{0}: (5, {}), {1}: (6, {})} | custom-call | flops 1677721600 | bytes 2621440 | tf_op jit(solution)/shard_map/pallas_call | solution.py:252
  135.9 10.2 %shard_map.285 = (bf16[640,1024]{1,0:T(8,128)(2,1)}, f32[640,1024]{1,0:T(8,128)}, bf16[640,1024]{1,0:T(8,128)(2,1)}) custom-call(s32[9]{0:T(128)} %fusion.50.idx, bf16[640,1024]{1,0:T(8,128)(2,1)} %get-tuple-element.285.mixed_ref, bf16[640,1024]{1,0:T(8,128)(2,1)} %bitcast.236, f32[6,1024]{1,0:T(8,128)} %add.250.mod_ref, f32[640,1]{1,0:T(8,128)} %reshape.497.keep_ref, ...), custom_call_target="tpu_custom_call" | custom-call | flops 1342177280 | bytes 9961472 | tf_op jit(solution)/shard_map/pallas_call | solution.py:252
  151.4 11.3 %shard_map.286 = (bf16[640,4096]{1,0:T(8,128)(2,1)}, bf16[640,4096]{1,0:T(8,128)(2,1)}) custom-call(s32[9]{0:T(128)} %fusion.50.idx, bf16[640,1024]{1,0:T(8,128)(2,1)} %get-tuple-element.286.x_ref, f32[1,4096]{1,0:T(1,128)} %bitcast.272, bf16[128,4096]{1,0:T(8,128)(2,1)} %rest_0_.13, bf16[64,4096]{1,0:T(8,128)(2,1)} %collective-permute-done.8.rest_1_, ...), custom_call_target="tpu_custom_call" | custom-call | flops 2684354560 | bytes 10092544 | tf_op jit(solution)/shard_map/pallas_call | solution.py:252
  164.3 11.3 %shard_map.287 = (bf16[640,4096]{1,0:T(8,128)(2,1)}, bf16[640,4096]{1,0:T(8,128)(2,1)}) custom-call(s32[9]{0:T(128)} %fusion.50.idx, bf16[640,1024]{1,0:T(8,128)(2,1)} %get-tuple-element.286.x_ref, f32[1,4096]{1,0:T(1,128)} %bitcast.273, bf16[128,4096]{1,0:T(8,128)(2,1)} %rest_0_.13, ...), custom_call_target="tpu_custom_call", output_to_operand_aliasing={{0}: (18, {}), {1}: (19, {})} | custom-call | flops 2684354560 | bytes 10092544 | tf_op jit(solution)/shard_map/pallas_call | solution.py:252
  180.8 12.1 %shard_map.288 = (bf16[8,512,512]{2,1,0:T(8,128)(2,1)}, bf16[8,512,512]{2,1,0:T(8,128)(2,1)}) custom-call(s32[9]{0:T(128)} %fusion.50.idx, bf16[2,512,640]{2,1,0:T(8,128)(2,1)} %copy.111.mine_ref.other_ref, bf16[2,512,640]{2,1,0:T(8,128)(2,1)} %copy.111.mine_ref.other_ref, bf16[640,4096]{1,0:T(8,128)(2,1)} %get-tuple-element.276.right_ref.act_ref), custom_call_target="tpu_custom_call" | custom-call | flops 5368709120 | bytes 14942208 | tf_op jit(solution)/shard_map/pallas_call | solution.py:252
  215.9 19.8 %shard_map.289 = (bf16[640,4096]{1,0:T(8,128)(2,1)}, bf16[512,4096]{1,0:T(8,128)(2,1)}, bf16[512,4096]{1,0:T(8,128)(2,1)}, f32[1,4096]{1,0:T(1,128)}) custom-call(s32[9]{0:T(128)} %fusion.50.idx, bf16[640,1024]{1,0:T(8,128)(2,1)} %multiply_convert_fusion.g_ref, bf16[640,4096]{1,0:T(8,128)(2,1)} %get-tuple-element.296.slope_ref, ...), custom_call_target="tpu_custom_call" | custom-call | flops 21474836480 | bytes 28573696 | tf_op jit(solution)/shard_map/pallas_call | solution.py:252
  241.1 21.2 %shard_map.290 = (f32[640,1024]{1,0:T(8,128)}, bf16[640,1024]{1,0:T(8,128)(2,1)}, bf16[640,1024]{1,0:T(8,128)(2,1)}, f32[4,1024]{1,0:T(4,128)}) custom-call(s32[9]{0:T(128)} %fusion.50.idx, bf16[640,4096]{1,0:T(8,128)(2,1)} %get-tuple-element.307.gh_ref, f32[640,1024]{1,0:T(8,128)} %get-tuple-element.308.mid_ref, bf16[640,1024]{1,0:T(8,128)(2,1)} %bitcast.238, ...), custom_call_target="tpu_custom_call" | custom-call | flops 6710886400 | bytes 26214400 | tf_op jit(solution)/shard_map/pallas_call | solution.py:252
  271.2 27.3 %shard_map.291 = (bf16[640,1024]{1,0:T(8,128)(2,1)}, bf16[640,1024]{1,0:T(8,128)(2,1)}, bf16[640,1024]{1,0:T(8,128)(2,1)}, f32[16,8,1152]{2,1,0:T(8,128)}) custom-call(s32[2]{0:T(128)} %subtract_clamp_fusion.nv, bf16[640,3072]{1,0:T(8,128)(2,1)} %get-tuple-element.242.q_ref.k_ref.v_ref, bf16[640,3072]{1,0:T(8,128)(2,1)} %get-tuple-element.242.q_ref.k_ref.v_ref, ...), custom_call_target="tpu_custom_call" | custom-call | flops 8388608000 | bytes 10485760 | tf_op jit(solution)/shard_map/pallas_call | solution.py:252
  304.0 8.9 %shard_map.292 = (bf16[512,4096]{1,0:T(8,128)(2,1)}, f32[1,4096]{1,0:T(1,128)}) custom-call(s32[9]{0:T(128)} %fusion.50.idx, bf16[2,512,640]{2,1,0:T(8,128)(2,1)} %bitcast.244, bf16[2,512,640]{2,1,0:T(8,128)(2,1)} %bitcast.246, bf16[640,1024]{1,0:T(8,128)(2,1)} %get-tuple-element.337.refs_2_.dq_ref, bf16[640,1024]{1,0:T(8,128)(2,1)} %get-tuple-element.338.refs_3_.dk_ref, ...), custom_call_target="tpu_custom_call" | custom-call | flops 2684354560 | bytes 10747904 | tf_op jit(solution)/shard_map/pallas_call | solution.py:252
  317.8 9.0 %shard_map.293 = bf16[512,4096]{1,0:T(8,128)(2,1)} custom-call(s32[9]{0:T(128)} %fusion.50.idx, bf16[2,512,640]{2,1,0:T(8,128)(2,1)} %bitcast.245, bf16[2,512,640]{2,1,0:T(8,128)(2,1)} %bitcast.247, bf16[640,1024]{1,0:T(8,128)(2,1)} %get-tuple-element.337.refs_2_.dq_ref, bf16[640,1024]{1,0:T(8,128)(2,1)} %get-tuple-element.338.refs_3_.dk_ref, ...), custom_call_target="tpu_custom_call" | custom-call | flops 2684354560 | bytes 10747904 | tf_op jit(solution)/shard_map/pallas_call | solution.py:252
  326.9 13.5 %collective-permute-done.59 = bf16[512,512]{1,0:T(8,128)(2,1)S(1)} collective-permute-done((bf16[512,512]{1,0:T(8,128)(2,1)}, bf16[512,512]{1,0:T(8,128)(2,1)S(1)}, u32[]{:S(2)}, u32[]{:S(2)}) %collective-permute-start.59) | collective-permute-done | bytes 524320 | tf_op jit(solution)/shard_map/ppermute | solution.py:179
  346.7 7.6 %collective-permute-done.60 = bf16[512,512]{1,0:T(8,128)(2,1)S(1)} collective-permute-done((bf16[512,512]{1,0:T(8,128)(2,1)S(1)}, bf16[512,512]{1,0:T(8,128)(2,1)S(1)}, u32[]{:S(2)}, u32[]{:S(2)}) %collective-permute-start.60) | collective-permute-done | bytes 524320 | tf_op jit(solution)/shard_map/ppermute | solution.py:192
  361.3 13.1 %shard_map.294 = (bf16[640,1024]{1,0:T(8,128)(2,1)}, f32[1,1024]{1,0:T(1,128)}) custom-call(s32[9]{0:T(128)} %fusion.50.idx, bf16[640,4096]{1,0:T(8,128)(2,1)} %get-tuple-element.276.right_ref.act_ref, f32[640,1024]{1,0:T(8,128)} %get-tuple-element.308.mid_ref, bf16[640,1024]{1,0:T(8,128)(2,1)} %bitcast.239, f32[640,1]{1,0:T(8,128)} %reshape.497.keep_ref, ...), custom_call_target="tpu_custom_call" | custom-call | flops 5368709120 | bytes 18874368 | tf_op jit(solution)/shard_map/pallas_call | solution.py:252
  386.0 6.9 %all-to-all-start.4 = ((bf16[1,2,5,8,8,1024]{5,4,2,1,0,3:T(8,128)(2,1)}), bf16[1,2,5,8,8,1024]{5,4,2,1,0,3:T(8,128)(2,1)S(1)}, u32[]{:S(2)}, u32[]{:S(2)}) async-start(bf16[1,2,5,8,8,1024]{5,4,2,1,0,3:T(8,128)(2,1)} %copy.121), calls=%async_computation.4 | async-start | bytes 2621440 | tf_op jit(solution)/shard_map/all_to_all | solution.py:1124
  398.8 14.8 %shard_map.295 = (bf16[640,1024]{1,0:T(8,128)(2,1)}, f32[2,1024]{1,0:T(2,128)}) custom-call(s32[9]{0:T(128)} %fusion.50.idx, bf16[640,1024]{1,0:T(8,128)(2,1)} %get-tuple-element.337.refs_2_.dq_ref, bf16[640,1024]{1,0:T(8,128)(2,1)} %get-tuple-element.338.refs_3_.dk_ref, bf16[640,1024]{1,0:T(8,128)(2,1)} %get-tuple-element.339.refs_4_.dv_ref, ...), custom_call_target="tpu_custom_call" | custom-call | flops 4026531840 | bytes 18087936 | tf_op jit(solution)/shard_map/pallas_call | solution.py:252
  437.1 7.2 %collective-permute-done.68 = bf16[2,5,2,8,1024]{4,3,2,1,0:T(8,128)(2,1)S(1)} collective-permute-done((bf16[2,5,2,8,1024]{4,3,2,1,0:T(8,128)(2,1)S(1)}, bf16[2,5,2,8,1024]{4,3,2,1,0:T(8,128)(2,1)S(1)}, u32[]{:S(2)}, u32[]{:S(2)}) %collective-permute-start.68) | collective-permute-done | bytes 327712 | tf_op jit(solution)/shard_map/ppermute | solution.py:1142
  444.3 8.0 %collective-permute-done.69 = bf16[2,5,2,8,1024]{4,3,2,1,0:T(8,128)(2,1)S(1)} collective-permute-done((bf16[2,5,2,8,1024]{4,3,2,1,0:T(8,128)(2,1)S(1)}, bf16[2,5,2,8,1024]{4,3,2,1,0:T(8,128)(2,1)S(1)}, u32[]{:S(2)}, u32[]{:S(2)}) %collective-permute-start.69) | collective-permute-done | bytes 327712 | tf_op jit(solution)/shard_map/ppermute | solution.py:1142
  468.5 12.1 %collective-permute-done.71 = bf16[64,4096]{1,0:T(8,128)(2,1)S(1)} collective-permute-done((bf16[64,4096]{1,0:T(8,128)(2,1)S(1)}, bf16[64,4096]{1,0:T(8,128)(2,1)S(1)}, u32[]{:S(2)}, u32[]{:S(2)}) %collective-permute-start.71) | collective-permute-done | bytes 524320 | tf_op jit(solution)/shard_map/ppermute | solution.py:192
  (366 shorter events, 229.2 us)
Async XLA Ops:
  32.2 23.4 %all-to-all-start.2 = ((bf16[4,2,5,2,8,1024]{5,4,3,2,1,0:T(8,128)(2,1)}), bf16[4,2,5,2,8,1024]{5,4,3,2,1,0:T(8,128)(2,1)}, u32[]{:S(2)}, u32[]{:S(2)}) async-start(bf16[4,2,5,2,8,1024]{5,4,3,2,1,0:T(8,128)(2,1)} %bitcast.14), calls=%async_computation.2 | async-start | bytes 2621440 | tf_op jit(solution)/shard_map/all_to_all | solution.py:1117
  90.5 31.8 %all-to-all-start.3 = ((bf16[4,2,5,2,8,1024]{5,4,3,2,1,0:T(8,128)(2,1)}), bf16[4,2,5,2,8,1024]{5,4,3,2,1,0:T(8,128)(2,1)S(1)}, u32[]{:S(2)}, u32[]{:S(2)}) async-start(bf16[4,2,5,2,8,1024]{5,4,3,2,1,0:T(8,128)(2,1)} %bitcast.249), calls=%async_computation.3 | async-start | bytes 2621440 | tf_op jit(solution)/shard_map/all_to_all | solution.py:1117
  212.4 23.3 %collective-permute-start.36 = (bf16[512,512]{1,0:T(8,128)(2,1)S(1)}, bf16[512,512]{1,0:T(8,128)(2,1)S(1)}, u32[]{:S(2)}, u32[]{:S(2)}) collective-permute-start(bf16[512,512]{1,0:T(8,128)(2,1)S(1)} %get-tuple-element.292), channel_id=1, source_target_pairs={{4,12},{12,20},{20,28},{28,24},{24,16},{16,8},{8,0},{0,4},{5,13},{... | collective-permute-start | bytes 1572872 | tf_op jit(solution)/shard_map/ppermute | solution.py:179
  212.5 23.2 %collective-permute-start.37 = (bf16[512,512]{1,0:T(8,128)(2,1)S(1)}, bf16[512,512]{1,0:T(8,128)(2,1)S(1)}, u32[]{:S(2)}, u32[]{:S(2)}) collective-permute-start(bf16[512,512]{1,0:T(8,128)(2,1)S(1)} %get-tuple-element.293), channel_id=1, source_target_pairs={{12,4},{20,12},{28,20},{24,28},{16,24},{8,16},{0,8},{4,0},{13,5},{... | collective-permute-start | bytes 1572872 | tf_op jit(solution)/shard_map/ppermute | solution.py:181
  235.7 26.7 %collective-permute-start.47 = (bf16[8,64,4096]{2,1,0:T(8,128)(2,1)}, bf16[8,64,4096]{2,1,0:T(8,128)(2,1)}, u32[]{:S(2)}, u32[]{:S(2)}) collective-permute-start(bf16[8,64,4096]{2,1,0:T(8,128)(2,1)} %bitcast.290), channel_id=1, source_target_pairs={{0,1},{1,0},{2,3},{3,2},{4,5},{5,4},{6,7},{7,6},{8,9},{9,8},{10,11... | collective-permute-start | bytes 12582920 | tf_op jit(solution)/shard_map/ppermute | solution.py:1185
  239.7 25.2 %collective-permute-start.45 = (bf16[512,512]{1,0:T(8,128)(2,1)}, bf16[512,512]{1,0:T(8,128)(2,1)}, u32[]{:S(2)}, u32[]{:S(2)}) collective-permute-start(bf16[512,512]{1,0:T(8,128)(2,1)} %get-tuple-element.439), channel_id=1, source_target_pairs={{4,12},{12,20},{20,28},{28,24},{24,16},{16,8},{8,0},{0,4},{5,13},{... | collective-permute-start | bytes 1572872 | tf_op jit(solution)/shard_map/ppermute | solution.py:179
  239.7 25.1 %collective-permute-start.46 = (bf16[512,512]{1,0:T(8,128)(2,1)}, bf16[512,512]{1,0:T(8,128)(2,1)}, u32[]{:S(2)}, u32[]{:S(2)}) collective-permute-start(bf16[512,512]{1,0:T(8,128)(2,1)} %get-tuple-element.438), channel_id=1, source_target_pairs={{12,4},{20,12},{28,20},{24,28},{16,24},{8,16},{0,8},{4,0},{13,5},{... | collective-permute-start | bytes 1572872 | tf_op jit(solution)/shard_map/ppermute | solution.py:181
  268.1 30.5 %collective-permute-start.48 = (bf16[512,512]{1,0:T(8,128)(2,1)}, bf16[512,512]{1,0:T(8,128)(2,1)}, u32[]{:S(2)}, u32[]{:S(2)}) collective-permute-start(bf16[512,512]{1,0:T(8,128)(2,1)} %get-tuple-element.435), channel_id=1, source_target_pairs={{4,12},{12,20},{20,28},{28,24},{24,16},{16,8},{8,0},{0,4},{5,13},{... | collective-permute-start | bytes 1572872 | tf_op jit(solution)/shard_map/ppermute | solution.py:179
  268.2 30.4 %collective-permute-start.49 = (bf16[512,512]{1,0:T(8,128)(2,1)}, bf16[512,512]{1,0:T(8,128)(2,1)}, u32[]{:S(2)}, u32[]{:S(2)}) collective-permute-start(bf16[512,512]{1,0:T(8,128)(2,1)} %get-tuple-element.434), channel_id=1, source_target_pairs={{12,4},{20,12},{28,20},{24,28},{16,24},{8,16},{0,8},{4,0},{13,5},{... | collective-permute-start | bytes 1572872 | tf_op jit(solution)/shard_map/ppermute | solution.py:181
  269.6 29.0 %collective-permute-start.50 = (bf16[64,4096]{1,0:T(8,128)(2,1)}, bf16[64,4096]{1,0:T(8,128)(2,1)}, u32[]{:S(2)}, u32[]{:S(2)}) collective-permute-start(bf16[64,4096]{1,0:T(8,128)(2,1)} %get-tuple-element.316), channel_id=1, source_target_pairs={{4,12},{12,20},{20,28},{28,24},{24,16},{16,8},{8,0},{0,4},{5,13},{... | collective-permute-start | bytes 1572872 | tf_op jit(solution)/shard_map/ppermute | solution.py:179
  269.6 28.9 %collective-permute-start.51 = (bf16[64,4096]{1,0:T(8,128)(2,1)}, bf16[64,4096]{1,0:T(8,128)(2,1)}, u32[]{:S(2)}, u32[]{:S(2)}) collective-permute-start(bf16[64,4096]{1,0:T(8,128)(2,1)} %get-tuple-element.317), channel_id=1, source_target_pairs={{12,4},{20,12},{28,20},{24,28},{16,24},{8,16},{0,8},{4,0},{13,5},{... | collective-permute-start | bytes 1572872 | tf_op jit(solution)/shard_map/ppermute | solution.py:181
  312.9 41.6 %collective-permute-start.54 = (bf16[8,64,4096]{2,1,0:T(8,128)(2,1)}, bf16[8,64,4096]{2,1,0:T(8,128)(2,1)}, u32[]{:S(2)}, u32[]{:S(2)}) collective-permute-start(bf16[8,64,4096]{2,1,0:T(8,128)(2,1)} %bitcast.289), channel_id=1, source_target_pairs={{0,1},{1,0},{2,3},{3,2},{4,5},{5,4},{6,7},{7,6},{8,9},{9,8},{10,11... | collective-permute-start | bytes 12582920 | tf_op jit(solution)/shard_map/ppermute | solution.py:1185
  315.1 28.4 %collective-permute-start.53 = (bf16[64,4096]{1,0:T(8,128)(2,1)}, bf16[64,4096]{1,0:T(8,128)(2,1)}, u32[]{:S(2)}, u32[]{:S(2)}) collective-permute-start(bf16[64,4096]{1,0:T(8,128)(2,1)} %get-tuple-element.333), channel_id=1, source_target_pairs={{12,4},{20,12},{28,20},{24,28},{16,24},{8,16},{0,8},{4,0},{13,5},{... | collective-permute-start | bytes 1572872 | tf_op jit(solution)/shard_map/ppermute | solution.py:181
  315.7 27.7 %collective-permute-start.52 = (bf16[64,4096]{1,0:T(8,128)(2,1)}, bf16[64,4096]{1,0:T(8,128)(2,1)}, u32[]{:S(2)}, u32[]{:S(2)}) collective-permute-start(bf16[64,4096]{1,0:T(8,128)(2,1)} %get-tuple-element.332), channel_id=1, source_target_pairs={{4,12},{12,20},{20,28},{28,24},{24,16},{16,8},{8,0},{0,4},{5,13},{... | collective-permute-start | bytes 1572872 | tf_op jit(solution)/shard_map/ppermute | solution.py:179
  316.6 23.8 %collective-permute-start.59 = (bf16[512,512]{1,0:T(8,128)(2,1)}, bf16[512,512]{1,0:T(8,128)(2,1)S(1)}, u32[]{:S(2)}, u32[]{:S(2)}) collective-permute-start(bf16[512,512]{1,0:T(8,128)(2,1)} %fusion.32), channel_id=1, source_target_pairs={{4,12},{12,20},{20,28},{28,24},{24,16},{16,8},{8,0},{0,4},{5,13},{... | collective-permute-start | bytes 1572872 | tf_op jit(solution)/shard_map/ppermute | solution.py:179
  358.9 21.4 %collective-permute-start.57 = (bf16[64,4096]{1,0:T(8,128)(2,1)}, bf16[64,4096]{1,0:T(8,128)(2,1)}, u32[]{:S(2)}, u32[]{:S(2)}) collective-permute-start(bf16[64,4096]{1,0:T(8,128)(2,1)} %get-tuple-element.352), channel_id=1, source_target_pairs={{4,12},{12,20},{20,28},{28,24},{24,16},{16,8},{8,0},{0,4},{5,13},{... | collective-permute-start | bytes 1572872 | tf_op jit(solution)/shard_map/ppermute | solution.py:179
  386.0 27.6 %all-to-all-start.4 = ((bf16[1,2,5,8,8,1024]{5,4,2,1,0,3:T(8,128)(2,1)}), bf16[1,2,5,8,8,1024]{5,4,2,1,0,3:T(8,128)(2,1)S(1)}, u32[]{:S(2)}, u32[]{:S(2)}) async-start(bf16[1,2,5,8,8,1024]{5,4,2,1,0,3:T(8,128)(2,1)} %copy.121), calls=%async_computation.4 | async-start | bytes 2621440 | tf_op jit(solution)/shard_map/all_to_all | solution.py:1124
  396.7 23.3 %collective-permute-start.63 = (bf16[64,4096]{1,0:T(8,128)(2,1)}, bf16[64,4096]{1,0:T(8,128)(2,1)}, u32[]{:S(2)}, u32[]{:S(2)}) collective-permute-start(bf16[64,4096]{1,0:T(8,128)(2,1)} %get-tuple-element.370), channel_id=1, source_target_pairs={{12,4},{20,12},{28,20},{24,28},{16,24},{8,16},{0,8},{4,0},{13,5},{... | collective-permute-start | bytes 1572872 | tf_op jit(solution)/shard_map/ppermute | solution.py:181
  397.3 22.8 %collective-permute-start.64 = (bf16[512,512]{1,0:T(8,128)(2,1)S(1)}, bf16[512,512]{1,0:T(8,128)(2,1)}, u32[]{:S(2)}, u32[]{:S(2)}) collective-permute-start(bf16[512,512]{1,0:T(8,128)(2,1)S(1)} %add_convert_fusion.2.ref), channel_id=1, source_target_pairs={{0,1},{1,0},{2,3},{3,2},{4,5},{5,4},{6,7},{7,6},{8,9},{9,8},{10,11... | collective-permute-start | bytes 1572872 | tf_op jit(solution)/shard_map/ppermute | solution.py:197
  424.9 28.6 %collective-permute-start.65 = (bf16[64,4096]{1,0:T(8,128)(2,1)}, bf16[64,4096]{1,0:T(8,128)(2,1)}, u32[]{:S(2)}, u32[]{:S(2)}) collective-permute-start(bf16[64,4096]{1,0:T(8,128)(2,1)} %get-tuple-element.386), channel_id=1, source_target_pairs={{4,12},{12,20},{20,28},{28,24},{24,16},{16,8},{8,0},{0,4},{5,13},{... | collective-permute-start | bytes 1572872 | tf_op jit(solution)/shard_map/ppermute | solution.py:179
  426.0 27.5 %collective-permute-start.66 = (bf16[64,4096]{1,0:T(8,128)(2,1)}, bf16[64,4096]{1,0:T(8,128)(2,1)}, u32[]{:S(2)}, u32[]{:S(2)}) collective-permute-start(bf16[64,4096]{1,0:T(8,128)(2,1)} %get-tuple-element.387), channel_id=1, source_target_pairs={{12,4},{20,12},{28,20},{24,28},{16,24},{8,16},{0,8},{4,0},{13,5},{... | collective-permute-start | bytes 1572872 | tf_op jit(solution)/shard_map/ppermute | solution.py:181
  426.4 27.1 %all-to-all-start.5 = ((f32[32,24,128]{2,1,0:T(8,128)}), f32[32,24,128]{2,1,0:T(8,128)S(1)}, u32[]{:S(2)}, u32[]{:S(2)}) async-start(f32[32,24,128]{2,1,0:T(8,128)} %bitcast.78), calls=%async_computation.5 | async-start | bytes 786432 | tf_op jit(solution)/shard_map/all_to_all | solution.py:122
  456.0 24.8 %collective-permute-start.70 = (bf16[64,4096]{1,0:T(8,128)(2,1)}, bf16[64,4096]{1,0:T(8,128)(2,1)}, u32[]{:S(2)}, u32[]{:S(2)}) collective-permute-start(bf16[64,4096]{1,0:T(8,128)(2,1)} %fusion.4), channel_id=1, source_target_pairs={{4,12},{12,20},{20,28},{28,24},{24,16},{16,8},{8,0},{0,4},{5,13},{... | collective-permute-start | bytes 1572872 | tf_op jit(solution)/shard_map/ppermute | solution.py:179
  458.0 22.8 %all-to-all-start.6 = ((f32[32,24,128]{2,1,0:T(8,128)}), f32[32,24,128]{2,1,0:T(8,128)S(1)}, u32[]{:S(2)}, u32[]{:S(2)}) async-start(f32[32,24,128]{2,1,0:T(8,128)} %broadcast_in_dim.79), calls=%async_computation.6 | async-start | bytes 786432 | tf_op jit(solution)/shard_map/all_to_all | solution.py:127
  (105 other events, 1202.2 us)
